TPU v7x, 32 devices: a whole 2x2x4 slice. The times are simulated.
32 devices in a mesh: dp: 16 (over z, x, core), tensor: 2 (over y).
Axes of the slice: x: 2, y: 2, z: 4, core: 2. Of those that a mesh axis runs over, the one named last changes fastest.
Arguments:
- tokens: bfloat16 [16, 2048, 1024], P('dp', 'tensor'), may hold values from -6 to 6
- segment_ids: int32 [16, 2048], P('dp'), may hold values from 0 to 2047, as said below
- w_qkv: float32 [3, 1024, 1024], P(None, 'dp', 'tensor'), may hold values from -0.1875 to 0.1875
- w_out: float32 [1024, 1024], P('tensor', 'dp'), may hold values from -0.375 to 0.375
- w_in: float32 [1024, 4096], P('dp', 'tensor'), may hold values from -0.1875 to 0.1875
- w_back: float32 [4096, 1024], P('tensor', 'dp'), may hold values from -0.09375 to 0.09375
- norm_gains: float32 [2, 1024], P(None, 'dp'), may hold values from 0.1 to 1.9
- norm_biases: float32 [2, 1024], P(None, 'dp'), may hold values from -2 to 2
- cotangent: bfloat16 [16, 2048, 1024], P('dp', 'tensor'), may hold values from -6 to 6
Outputs:
- result: bfloat16 [16, 2048, 1024], P('dp', 'tensor')
- grad_tokens: bfloat16 [16, 2048, 1024], P('dp', 'tensor')
- grad_qkv: float32 [3, 1024, 1024], P(None, 'dp', 'tensor')
- grad_out: float32 [1024, 1024], P('tensor', 'dp')
- grad_in: float32 [1024, 4096], P('dp', 'tensor')
- grad_back: float32 [4096, 1024], P('tensor', 'dp')
- grad_gains: float32 [2, 1024], P(None, 'dp')
- grad_biases: float32 [2, 1024], P(None, 'dp')
Inputs may be any that keep to these rules, and one draw needn't show every extreme that they name: `segment_ids`: A token's id is the position of its document's first token in its sequence, so ids never fall within a sequence; a token attends only to earlier tokens of its own id in its own sequence.
All inputs are finite; a program needn't handle non-finite values.
Results may differ from a plain program's by a relative error of at most 0.02.
Values may be sent and summed in bfloat16 or wider, within the bound.
No kernel may reach another device: no remote copies, remote signals or barrier semaphores. Data moves between devices by JAX's collectives and lax.ppermute only.
A program may use at most 256 MiB of HBM per device.

v0:
```python
import math

import jax
import jax.numpy as jnp
from jax import lax
from jax.sharding import PartitionSpec as P

HEAD = 128
ROW_BLOCK = 512


eps_norm = 1e-05
masked_score = -1e30


def layer_norm(values, gain, shift):
    center = values - jnp.mean(values, axis=-1, keepdims=True)
    spread = jnp.mean(center * center, axis=-1, keepdims=True)
    return center * lax.rsqrt(spread + eps_norm) * gain + shift


def smooth_act(values):
    return jax.nn.gelu(values, approximate=True)


def block_scores(query_rows, keys, seg_rows, seg_all, row_ids, slopes):
    scale = 1.0 / math.sqrt(HEAD)
    raw = jnp.einsum("qhd,khd->hqk", query_rows, keys, preferred_element_type=jnp.float32) * scale
    cols = jnp.arange(keys.shape[0], dtype=jnp.int32)
    dist = (row_ids[:, None] - cols[None, :]).astype(jnp.float32)
    raw = raw - slopes[:, None, None] * dist[None]
    allowed = (cols[None, :] <= row_ids[:, None]) & (seg_rows[:, None] == seg_all[None, :])
    return jnp.where(allowed[None], raw, masked_score)


def attend_forward(qkv_seq, seg_seq, slopes):
    query, keys, values = (qkv_seq[0], qkv_seq[1], qkv_seq[2])
    length = keys.shape[0]

    def one_block(start):
        rows = lax.dynamic_slice_in_dim(query, start, ROW_BLOCK, 0)
        seg_rows = lax.dynamic_slice_in_dim(seg_seq, start, ROW_BLOCK, 0)
        row_ids = start + jnp.arange(ROW_BLOCK, dtype=jnp.int32)
        scores = block_scores(rows, keys, seg_rows, seg_seq, row_ids, slopes)
        top = jnp.max(scores, axis=-1, keepdims=True)
        expo = jnp.exp(scores - top)
        total = jnp.sum(expo, axis=-1, keepdims=True)
        probs = (expo / total).astype(jnp.bfloat16)
        mixed = jnp.einsum("hqk,khd->qhd", probs, values, preferred_element_type=jnp.float32)
        return (mixed, (top + jnp.log(total))[..., 0])

    starts = jnp.arange(length // ROW_BLOCK, dtype=jnp.int32) * ROW_BLOCK
    mixed, log_totals = lax.map(one_block, starts)
    return (mixed.reshape(length, -1), log_totals)


def attend_backward(qkv_seq, seg_seq, log_totals, grad_mixed, slopes):
    query, keys, values = (qkv_seq[0], qkv_seq[1], qkv_seq[2])
    length, heads_here, head_size = keys.shape
    scale = 1.0 / math.sqrt(HEAD)
    grad_rows_all = grad_mixed.reshape(length, heads_here, head_size)

    def one_block(carry, item):
        start, block_totals = item
        rows = lax.dynamic_slice_in_dim(query, start, ROW_BLOCK, 0)
        seg_rows = lax.dynamic_slice_in_dim(seg_seq, start, ROW_BLOCK, 0)
        grad_rows = lax.dynamic_slice_in_dim(grad_rows_all, start, ROW_BLOCK, 0)
        row_ids = start + jnp.arange(ROW_BLOCK, dtype=jnp.int32)
        scores = block_scores(rows, keys, seg_rows, seg_seq, row_ids, slopes)
        probs = jnp.exp(scores - block_totals[..., None])
        grad_probs = jnp.einsum(
            "qhd,khd->hqk", grad_rows, values, preferred_element_type=jnp.float32
        )
        inner = jnp.sum(probs * grad_probs, axis=-1, keepdims=True)
        grad_scores = (probs * (grad_probs - inner)).astype(jnp.bfloat16)
        grad_query = (
            jnp.einsum("hqk,khd->qhd", grad_scores, keys, preferred_element_type=jnp.float32)
            * scale
        )
        grad_keys = (
            carry[0]
            + jnp.einsum("hqk,qhd->khd", grad_scores, rows, preferred_element_type=jnp.float32)
            * scale
        )
        grad_values = carry[1] + jnp.einsum(
            "hqk,qhd->khd",
            probs.astype(jnp.bfloat16),
            grad_rows,
            preferred_element_type=jnp.float32,
        )
        return ((grad_keys, grad_values), grad_query)

    empty = jnp.zeros((length, heads_here, head_size), jnp.float32)
    starts = jnp.arange(length // ROW_BLOCK, dtype=jnp.int32) * ROW_BLOCK
    (grad_keys, grad_values), grad_query = lax.scan(one_block, (empty, empty), (starts, log_totals))
    return jnp.stack([grad_query.reshape(length, heads_here, head_size), grad_keys, grad_values])


def shards(tokens, segment_ids, w_qkv, w_out, w_in, w_back, norm_gains, norm_biases, cotangent):
    low_copies = (
        w_qkv.astype(jnp.bfloat16),
        w_out.astype(jnp.bfloat16),
        w_in.astype(jnp.bfloat16),
        w_back.astype(jnp.bfloat16),
        norm_gains.astype(jnp.bfloat16),
        norm_biases.astype(jnp.bfloat16),
    )
    (
        complete_query_key_value,
        complete_out_weight,
        complete_in_weight,
        complete_back_weight,
        gains_low,
        shifts_low,
    ) = (
        lax.all_gather(low_copies[0], "dp", axis=1, tiled=True),
        lax.all_gather(low_copies[1], "dp", axis=1, tiled=True),
        lax.all_gather(low_copies[2], "dp", axis=0, tiled=True),
        lax.all_gather(low_copies[3], "dp", axis=1, tiled=True),
        lax.all_gather(low_copies[4], "dp", axis=1, tiled=True),
        lax.all_gather(low_copies[5], "dp", axis=1, tiled=True),
    )
    gains = gains_low.astype(jnp.float32)
    shifts = shifts_low.astype(jnp.float32)
    seqs, own_len, width = tokens.shape
    length = segment_ids.shape[1]
    local_width = complete_query_key_value.shape[2]
    heads_here = local_width // HEAD
    rank = lax.axis_index("tensor")
    first_row = rank * own_len
    slopes = jnp.exp2(
        -(rank * heads_here + jnp.arange(heads_here, dtype=jnp.int32) + 1).astype(jnp.float32)
    )
    tokens_f = tokens.astype(jnp.float32)
    tokens_all = lax.all_gather(tokens, "tensor", axis=1, tiled=True).astype(jnp.float32)
    first_normalized = layer_norm(tokens_all, gains[0], shifts[0]).astype(jnp.bfloat16)
    projected = jnp.einsum(
        "gqu,fuk->gfqk",
        first_normalized,
        complete_query_key_value,
        preferred_element_type=jnp.float32,
    ).astype(jnp.bfloat16)
    qkv_heads = projected.reshape(seqs, 3, length, heads_here, HEAD)

    def forward_seq(item):
        return attend_forward(item[0], item[1], slopes)

    mixed, log_totals = lax.map(forward_seq, (qkv_heads, segment_ids))
    attended_values = mixed.astype(jnp.bfloat16)
    attention_slice = jnp.einsum(
        "oin,nh->oih", attended_values, complete_out_weight, preferred_element_type=jnp.float32
    )
    attn_all = lax.psum(attention_slice.astype(jnp.bfloat16), "tensor").astype(jnp.float32)
    resid_all = tokens_all + attn_all
    second_normalized = layer_norm(resid_all, gains[1], shifts[1]).astype(jnp.bfloat16)
    resid = lax.dynamic_slice_in_dim(resid_all, first_row, own_len, 1)
    hidden_preactivation = jnp.einsum(
        "rhi,ip->rhp", second_normalized, complete_in_weight, preferred_element_type=jnp.float32
    )
    hidden_activations = smooth_act(hidden_preactivation).astype(jnp.bfloat16)
    feedforward_slice = jnp.einsum(
        "cow,wv->cov", hidden_activations, complete_back_weight, preferred_element_type=jnp.float32
    )
    ffn_own = lax.psum_scatter(
        feedforward_slice.astype(jnp.bfloat16), "tensor", scatter_dimension=1, tiled=True
    ).astype(jnp.float32)
    result = (resid + ffn_own).astype(jnp.bfloat16)
    cotangent_gathered = lax.all_gather(cotangent, "tensor", axis=1, tiled=True)
    back_weight_gradient_shard = jnp.einsum(
        "ine,inb->eb", hidden_activations, cotangent_gathered, preferred_element_type=jnp.float32
    )
    hidden_gradient = jnp.einsum(
        "jrx,gx->jrg", cotangent_gathered, complete_back_weight, preferred_element_type=jnp.float32
    )
    _, act_pull = jax.vjp(smooth_act, hidden_preactivation)
    preactivation_gradient = act_pull(hidden_gradient)[0].astype(jnp.bfloat16)
    in_weight_gradient_shard = jnp.einsum(
        "bkw,bkz->wz", second_normalized, preactivation_gradient, preferred_element_type=jnp.float32
    )
    second_norm_slice = jnp.einsum(
        "kyj,tj->kyt",
        preactivation_gradient,
        complete_in_weight,
        preferred_element_type=jnp.float32,
    )
    grad_norm2 = lax.psum_scatter(
        second_norm_slice.astype(jnp.bfloat16), "tensor", scatter_dimension=1, tiled=True
    ).astype(jnp.float32)
    _, second_pull = jax.vjp(layer_norm, resid, gains[1], shifts[1])
    grad_resid_norm, grad_gain2, grad_shift2 = second_pull(grad_norm2)
    grad_resid = cotangent.astype(jnp.float32) + grad_resid_norm
    attention_gradient_gathered = lax.all_gather(
        grad_resid.astype(jnp.bfloat16), "tensor", axis=1, tiled=True
    )
    grad_out_local = jnp.einsum(
        "xwq,xwr->qr",
        attended_values,
        attention_gradient_gathered,
        preferred_element_type=jnp.float32,
    )
    grad_attended = jnp.einsum(
        "wik,jk->wij",
        attention_gradient_gathered,
        complete_out_weight,
        preferred_element_type=jnp.float32,
    ).astype(jnp.bfloat16)

    def backward_seq(item):
        return attend_backward(item[0], item[1], item[2], item[3], slopes)

    grad_heads = lax.map(backward_seq, (qkv_heads, segment_ids, log_totals, grad_attended))
    projection_gradient = grad_heads.reshape(seqs, 3, length, local_width).astype(jnp.bfloat16)
    grad_qkv_local = jnp.einsum(
        "phb,pthw->tbw", first_normalized, projection_gradient, preferred_element_type=jnp.float32
    )
    norm1_part = jnp.einsum(
        "zjyw,juw->zyu",
        projection_gradient,
        complete_query_key_value,
        preferred_element_type=jnp.float32,
    )
    grad_norm1 = lax.psum_scatter(
        norm1_part.astype(jnp.bfloat16), "tensor", scatter_dimension=1, tiled=True
    ).astype(jnp.float32)
    _, first_pull = jax.vjp(layer_norm, tokens_f, gains[0], shifts[0])
    grad_tok_norm, grad_gain1, grad_shift1 = first_pull(grad_norm1)
    grad_tokens = (grad_resid + grad_tok_norm).astype(jnp.bfloat16)
    gain_terms = jnp.stack([grad_gain1, grad_gain2])
    shift_terms = jnp.stack([grad_shift1, grad_shift2])
    gain_sum, shift_sum = lax.psum((gain_terms, shift_terms), "tensor")
    summed = (
        lax.psum_scatter(
            grad_qkv_local.astype(jnp.bfloat16), "dp", scatter_dimension=1, tiled=True
        ).astype(jnp.float32),
        lax.psum_scatter(
            grad_out_local.astype(jnp.bfloat16), "dp", scatter_dimension=1, tiled=True
        ).astype(jnp.float32),
        lax.psum_scatter(
            in_weight_gradient_shard.astype(jnp.bfloat16), "dp", scatter_dimension=0, tiled=True
        ).astype(jnp.float32),
        lax.psum_scatter(
            back_weight_gradient_shard.astype(jnp.bfloat16), "dp", scatter_dimension=1, tiled=True
        ).astype(jnp.float32),
        lax.psum_scatter(
            gain_sum.astype(jnp.bfloat16), "dp", scatter_dimension=1, tiled=True
        ).astype(jnp.float32),
        lax.psum_scatter(
            shift_sum.astype(jnp.bfloat16), "dp", scatter_dimension=1, tiled=True
        ).astype(jnp.float32),
    )
    return (result, grad_tokens, summed[0], summed[1], summed[2], summed[3], summed[4], summed[5])


def solution(mesh):
    return jax.shard_map(
        shards,
        mesh=mesh,
        in_specs=(
            P("dp", "tensor", None),
            P("dp", None),
            P(None, "dp", "tensor"),
            P("tensor", "dp"),
            P("dp", "tensor"),
            P("tensor", "dp"),
            P(None, "dp"),
            P(None, "dp"),
            P("dp", "tensor", None),
        ),
        out_specs=(
            P("dp", "tensor", None),
            P("dp", "tensor", None),
            P(None, "dp", "tensor"),
            P("tensor", "dp"),
            P("dp", "tensor"),
            P("tensor", "dp"),
            P(None, "dp"),
            P(None, "dp"),
        ),
        check_vma=False,
    )
```

profile of v0, /device:TPU:0, one launch (start us, length us, event | category | flops | bytes accessed | tf_op | source)
XLA Modules:
  0.0 1428.3 jit_solution(9066602247658903805)
XLA Ops:
  12.7 22.9 %all-gather.1 = bf16[16,64,2]{1,2,0:T(2,128)(2,1)S(1)} all-gather(bf16[1,64,2]{1,2,0:T(2,128)(2,1)S(1)} %convert_bitcast_fusion.5), channel_id=1, replica_groups=mesh['dp'=16,'tensor'=2] {'dp'}, dimensions={0}, use_global_device_ids=true | all-gather | bytes 4352 | tf_op jit(solution)/shard_map/all_gather | solution.py:121
  35.7 17.3 %all-gather = bf16[16,64,2]{1,2,0:T(2,128)(2,1)S(1)} all-gather(bf16[1,64,2]{1,2,0:T(2,128)(2,1)S(1)} %convert_bitcast_fusion.6), channel_id=1, replica_groups=mesh['dp'=16,'tensor'=2] {'dp'}, dimensions={0}, use_global_device_ids=true | all-gather | bytes 4352 | tf_op jit(solution)/shard_map/all_gather | solution.py:120
  54.3 14.7 %all-gather.10.cloned.1.call-done = bf16[1,2048,1024]{2,1,0:T(8,128)(2,1)} async-done(((bf16[1,1024,1024]{2,1,0:T(8,128)(2,1)}), bf16[1,2048,1024]{2,1,0:T(8,128)(2,1)}) %all-gather.10.cloned.1.call-update) | async-done | bytes 4194320 | tf_op jit(solution)/shard_map/all_gather | solution.py:135
  73.9 43.1 %all-gather.12.cloned.1.call-done = bf16[3,1024,512]{2,1,0:T(8,128)(2,1)} async-done(((bf16[3,64,512]{2,1,0:T(8,128)(2,1)}), bf16[3,1024,512]{2,1,0:T(8,128)(2,1)}) %all-gather.12.cloned.1.call-update) | async-done | bytes 3145744 | tf_op jit(solution)/shard_map/all_gather | solution.py:116
  142.1 111.0 %while.46 = (s32[]{:T(128)}, bf16[4,512,4,128]{3,1,2,0:T(8,128)(2,1)}, f32[4,4,512]{2,1,0:T(4,128)}, s32[4]{0:T(128)S(1)}, s32[2048]{0:T(1024)S(1)}, /*index=5*/...) while((s32[]{:T(128)}, ...), condition=%wide.region_5.6_spmd.clone, body=%wide.region_2.5_spmd.clone.sunk | while | flops 2228222464 | bytes 89739576 | solution.py:53
  266.3 103.3 %all-reduce.5.cloned.1.call-done = bf16[1,2048,1024]{2,1,0:T(8,128)(2,1)} async-done(((bf16[1,2048,1024]{2,1,0:T(8,128)(2,1)}), bf16[1,2048,1024]{2,1,0:T(8,128)(2,1)}) %all-reduce.5.cloned.1.call-update) | async-done | bytes 4194320 | tf_op jit(solution)/shard_map/psum | solution.py:153
  379.4 43.6 %all-gather.16.cloned.1.call-done = bf16[1024,2048]{1,0:T(8,128)(2,1)} async-done(((bf16[64,2048]{1,0:T(8,128)(2,1)}), bf16[1024,2048]{1,0:T(8,128)(2,1)}) %all-gather.16.cloned.1.call-update) | async-done | bytes 4194320 | tf_op jit(solution)/shard_map/all_gather | solution.py:118
  423.0 16.3 %fusion.95 = f32[2048,2048]{1,0:T(8,128)} fusion(bf16[1024,2048]{1,0:T(8,128)(2,1)} %all-gather.16.cloned.1.call-done, f32[1024]{0:T(1024)S(1)} %bitcast.190, f32[1024]{0:T(1024)S(1)} %bitcast.176, f32[2048]{0:T(1024)S(1)} %add_rsqrt_fusion, f32[2048]{0:T(1024)S(1)} %broadcast_multiply_fusion, bf16[1,2048,1024]{2,1,0:T(8,128)(2,1)} %all-reduce.5.cloned.1.call-done, ...), kind=kOutput, calls=%fused_computation.149 | convolution fusion | flops 8606711808 | bytes 29384704 | tf_op jit(solution)/shard_map/rhi,ip->rhp/dot_general | solution.py:157
  439.3 40.4 %all-gather.20.cloned.1.call-done = bf16[1,2048,1024]{2,1,0:T(8,128)(2,1)} async-done(((bf16[1,1024,1024]{2,1,0:T(8,128)(2,1)}), bf16[1,2048,1024]{2,1,0:T(8,128)(2,1)}) %all-gather.20.cloned.1.call-update) | async-done | bytes 4194320 | tf_op jit(solution)/shard_map/all_gather | solution.py:168
  479.7 53.6 %all-gather.18.cloned.1.call-done = bf16[2048,1024]{0,1:T(8,128)(2,1)} async-done(((bf16[2048,64]{0,1:T(8,128)(2,1)}), bf16[2048,1024]{0,1:T(8,128)(2,1)}) %all-gather.18.cloned.1.call-update) | async-done | bytes 4194320 | tf_op jit(solution)/shard_map/all_gather | solution.py:119
  533.3 22.2 %fusion.37 = bf16[2048,2048]{1,0:T(8,128)(2,1)S(1)} fusion(f32[2048,2048]{1,0:T(8,128)} %fusion.95, bf16[2048,1024]{0,1:T(8,128)(2,1)} %all-gather.18.cloned.1.call-done, bf16[1,2048,1024]{2,1,0:T(8,128)(2,1)} %all-gather.20.cloned.1.call-done), kind=kOutput, calls=%fused_computation.54 | convolution fusion | flops 8673820672 | bytes 33554432 | tf_op jit(solution)/shard_map/jrx,gx->jrg/dot_general | solution.py:172
  569.5 16.3 %convert_bitcast_fusion.2 = bf16[1,2048,1024]{2,1,0:T(8,128)(2,1)} fusion(bf16[2048,1024]{0,1:T(8,128)(2,1)} %all-gather.18.cloned.1.call-done, f32[2048,2048]{1,0:T(8,128)} %fusion.95), kind=kOutput, calls=%fused_computation.107 | convolution fusion | flops 8629780480 | bytes 25165824 | tf_op jit(solution)/shard_map/cow,wv->cov/dot_general | solution.py:161
  591.3 31.1 %reduce-scatter.15.cloned.1.call-done = bf16[1,1024,1024]{2,1,0:T(8,128)(2,1)} async-done(((bf16[1,2048,1024]{2,1,0:T(8,128)(2,1)}), bf16[1,1024,1024]{2,1,0:T(8,128)(2,1)}) %reduce-scatter.15.cloned.1.call-update) | async-done | bytes 2097168 | tf_op jit(solution)/shard_map/reduce_scatter | solution.py:186
  627.2 51.9 %reduce-scatter.13.cloned.1.call-done = bf16[1,1024,1024]{2,1,0:T(8,128)(2,1)} async-done(((bf16[1,2048,1024]{2,1,0:T(8,128)(2,1)}), bf16[1,1024,1024]{2,1,0:T(8,128)(2,1)}) %reduce-scatter.13.cloned.1.call-update) | async-done | bytes 2097168 | tf_op jit(solution)/shard_map/reduce_scatter | solution.py:164
  688.4 15.9 %fusion.66 = bf16[2048,1024]{0,1:T(8,128)(2,1)} fusion(bf16[1,2048,1024]{2,1,0:T(8,128)(2,1)} %all-gather.20.cloned.1.call-done, f32[2048,2048]{1,0:T(8,128)} %fusion.95), kind=kOutput, calls=%fused_computation.109 | convolution fusion | flops 8629780480 | bytes 25165824 | tf_op jit(solution)/shard_map/ine,inb->eb/dot_general | solution.py:169
  704.4 16.4 %convolution_convert_fusion = bf16[1024,2048]{1,0:T(8,128)(2,1)} fusion(bf16[2048,2048]{1,0:T(8,128)(2,1)} %copy-done.41, f32[1024]{0:T(1024)S(1)} %bitcast.191, f32[1024]{0:T(1024)S(1)} %bitcast.179, f32[2048]{0:T(1024)S(1)} %add_rsqrt_fusion, f32[2048]{0:T(1024)S(1)} %broadcast_multiply_fusion, bf16[1,2048,1024]{2,1,0:T(8,128)(2,1)} %all-reduce.5.cloned.1.call-done, ...), kind=kOutput, calls=%fused_computation.110 | convolution fusion | flops 8608808960 | bytes 20996096 | tf_op jit(solution)/shard_map/bkw,bkz->wz/dot_general | solution.py:177
  720.9 24.4 %all-gather.22.cloned.1.call-done = bf16[1,2048,1024]{2,1,0:T(8,128)(2,1)} async-done(((bf16[1,1024,1024]{2,1,0:T(8,128)(2,1)}), bf16[1,2048,1024]{2,1,0:T(8,128)(2,1)}) %all-gather.22.cloned.1.call-update) | async-done | bytes 4194320 | tf_op jit(solution)/shard_map/all_gather | solution.py:192
  752.9 278.3 %while.47 = (s32[]{:T(128)}, f32[2048,4,128]{0,2,1:T(8,128)}, f32[2048,4,128]{0,2,1:T(8,128)}, bf16[4,512,4,128]{3,1,2,0:T(8,128)(2,1)}, s32[4]{0:T(128)S(1)}, /...) while((s32[]{:T(128)}, f32[2048,4,128]{0,2,1:T(8,128)}, ...), condition=%wide.region_17.18_spmd.clone, body=%wide.region_15.17_spmd.clone.sunk | while | flops 5425592832 | bytes 338751936 | solution.py:95
  769.7 15.0 %multiply_reduce_fusion.4 = (f32[4,512]{1,0:T(4,128)S(1)}, f32[4,512,2048]{2,1,0:T(8,128)}) fusion(f32[4,512,2048]{2,1,0:T(8,128)} %fusion.151, f32[4,512]{1,0:T(4,128)S(1)} %dynamic-slice_bitcast_fusion.2, f32[512,2048]{1,0:T(8,128)S(1)} %subtract_convert_fusion.5, f32[4]{0:T(128)S(1)} %multiply_exponential_fusion.5, ...), kind=kOutput, calls=%fused_computation.22.clone.1 | convolution fusion | flops 1103099904 | bytes 41435156 | tf_op jit(solution)/shard_map/while/body/eval_jaxpr/while/body/eval_jaxpr/qhd,khd->hqk/dot_general | solution.py:28
  784.7 15.3 %multiply_convert_fusion.5 = bf16[4,512,2048]{2,1,0:T(8,128)(2,1)} fusion(f32[4,512,2048]{2,1,0:T(8,128)} %get-tuple-element.549, f32[4,512,2048]{2,1,0:T(8,128)} %fusion.151, f32[4,512]{1,0:T(4,128)S(1)} %get-tuple-element.550), kind=kLoop, calls=%fused_computation.21.clone.1 | loop fusion | flops 12582912 | bytes 41951232 | tf_op jit(solution)/shard_map/while/body/eval_jaxpr/while/body/eval_jaxpr/convert_element_type | solution.py:75
  839.8 15.6 %multiply_reduce_fusion.4 = (f32[4,512]{1,0:T(4,128)S(1)}, f32[4,512,2048]{2,1,0:T(8,128)}) fusion(f32[4,512,2048]{2,1,0:T(8,128)} %fusion.151, f32[4,512]{1,0:T(4,128)S(1)} %dynamic-slice_bitcast_fusion.2, f32[512,2048]{1,0:T(8,128)S(1)} %subtract_convert_fusion.5, f32[4]{0:T(128)S(1)} %multiply_exponential_fusion.5, ...), kind=kOutput, calls=%fused_computation.22.clone.1 | convolution fusion | flops 1103099904 | bytes 41435156 | tf_op jit(solution)/shard_map/while/body/eval_jaxpr/while/body/eval_jaxpr/qhd,khd->hqk/dot_general | solution.py:28
  855.4 15.1 %multiply_convert_fusion.5 = bf16[4,512,2048]{2,1,0:T(8,128)(2,1)} fusion(f32[4,512,2048]{2,1,0:T(8,128)} %get-tuple-element.549, f32[4,512,2048]{2,1,0:T(8,128)} %fusion.151, f32[4,512]{1,0:T(4,128)S(1)} %get-tuple-element.550), kind=kLoop, calls=%fused_computation.21.clone.1 | loop fusion | flops 12582912 | bytes 41951232 | tf_op jit(solution)/shard_map/while/body/eval_jaxpr/while/body/eval_jaxpr/convert_element_type | solution.py:75
  909.6 14.9 %multiply_reduce_fusion.4 = (f32[4,512]{1,0:T(4,128)S(1)}, f32[4,512,2048]{2,1,0:T(8,128)}) fusion(f32[4,512,2048]{2,1,0:T(8,128)} %fusion.151, f32[4,512]{1,0:T(4,128)S(1)} %dynamic-slice_bitcast_fusion.2, f32[512,2048]{1,0:T(8,128)S(1)} %subtract_convert_fusion.5, f32[4]{0:T(128)S(1)} %multiply_exponential_fusion.5, ...), kind=kOutput, calls=%fused_computation.22.clone.1 | convolution fusion | flops 1103099904 | bytes 41435156 | tf_op jit(solution)/shard_map/while/body/eval_jaxpr/while/body/eval_jaxpr/qhd,khd->hqk/dot_general | solution.py:28
  924.5 15.0 %multiply_convert_fusion.5 = bf16[4,512,2048]{2,1,0:T(8,128)(2,1)} fusion(f32[4,512,2048]{2,1,0:T(8,128)} %get-tuple-element.549, f32[4,512,2048]{2,1,0:T(8,128)} %fusion.151, f32[4,512]{1,0:T(4,128)S(1)} %get-tuple-element.550), kind=kLoop, calls=%fused_computation.21.clone.1 | loop fusion | flops 12582912 | bytes 41951232 | tf_op jit(solution)/shard_map/while/body/eval_jaxpr/while/body/eval_jaxpr/convert_element_type | solution.py:75
  978.3 14.9 %multiply_reduce_fusion.4 = (f32[4,512]{1,0:T(4,128)S(1)}, f32[4,512,2048]{2,1,0:T(8,128)}) fusion(f32[4,512,2048]{2,1,0:T(8,128)} %fusion.151, f32[4,512]{1,0:T(4,128)S(1)} %dynamic-slice_bitcast_fusion.2, f32[512,2048]{1,0:T(8,128)S(1)} %subtract_convert_fusion.5, f32[4]{0:T(128)S(1)} %multiply_exponential_fusion.5, ...), kind=kOutput, calls=%fused_computation.22.clone.1 | convolution fusion | flops 1103099904 | bytes 41435156 | tf_op jit(solution)/shard_map/while/body/eval_jaxpr/while/body/eval_jaxpr/qhd,khd->hqk/dot_general | solution.py:28
  993.2 15.0 %multiply_convert_fusion.5 = bf16[4,512,2048]{2,1,0:T(8,128)(2,1)} fusion(f32[4,512,2048]{2,1,0:T(8,128)} %get-tuple-element.549, f32[4,512,2048]{2,1,0:T(8,128)} %fusion.151, f32[4,512]{1,0:T(4,128)S(1)} %get-tuple-element.550), kind=kLoop, calls=%fused_computation.21.clone.1 | loop fusion | flops 12582912 | bytes 41951232 | tf_op jit(solution)/shard_map/while/body/eval_jaxpr/while/body/eval_jaxpr/convert_element_type | solution.py:75
  1071.3 11.7 fusion.69
  1088.9 87.4 %all-reduce.7.cloned.1.call-done = bf16[3,1024,512]{2,0,1:T(4,128)(2,1)} async-done(((bf16[3,1024,512]{2,0,1:T(4,128)(2,1)}), bf16[3,1024,512]{2,0,1:T(4,128)(2,1)}) %all-reduce.7.cloned.1.call-update) | async-done | bytes 3145744
  1178.1 57.9 %reduce-scatter.19.cloned.1.call-done = bf16[512,64]{0,1:T(8,128)(2,1)} async-done(((bf16[512,1024]{0,1:T(8,128)(2,1)}), bf16[512,64]{0,1:T(8,128)(2,1)}) %reduce-scatter.19.cloned.1.call-update) | async-done | bytes 65552 | tf_op jit(solution)/shard_map/reduce_scatter | solution.py:235
  1237.5 54.1 %reduce-scatter.17.cloned.1.call-done = bf16[1,1024,1024]{2,1,0:T(8,128)(2,1)} async-done(((bf16[1,2048,1024]{2,1,0:T(8,128)(2,1)}), bf16[1,1024,1024]{2,1,0:T(8,128)(2,1)}) %reduce-scatter.17.cloned.1.call-update) | async-done | bytes 2097168 | tf_op jit(solution)/shard_map/reduce_scatter | solution.py:222
  1312.0 50.2 %reduce-scatter.25.cloned.1.call-done = bf16[64,2]{1,0:T(8,128)(2,1)} async-done(((bf16[1024,2]{1,0:T(8,128)(2,1)}), bf16[64,2]{1,0:T(8,128)(2,1)}) %reduce-scatter.25.cloned.1.call-update) | async-done | bytes 272
  1363.6 56.4 %reduce-scatter.27.cloned.1.call-done = bf16[64,2]{1,0:T(8,128)(2,1)} async-done(((bf16[1024,2]{1,0:T(8,128)(2,1)}), bf16[64,2]{1,0:T(8,128)(2,1)}) %reduce-scatter.27.cloned.1.call-update) | async-done | bytes 272
  (333 shorter events, 423.9 us)
Async XLA Ops:
  7.2 61.9 %all-gather.10.cloned.1.call-start = ((), (), s32[]{:S(2)}) async-start(), calls=%async_computation.8 | async-start | bytes 6291456 | tf_op jit(solution)/shard_map/all_gather | solution.py:135
  7.9 109.1 %all-gather.12.cloned.1.call-start = ((), (), s32[]{:S(2)}) async-start(), calls=%async_computation.9 | async-start | bytes 3342336 | tf_op jit(solution)/shard_map/all_gather | solution.py:116
  9.7 246.7 %all-gather.14.cloned.1.call-start = ((), (), s32[]{:S(2)}) async-start(), calls=%async_computation.10 | async-start | bytes 1114112 | tf_op jit(solution)/shard_map/all_gather | solution.py:117
  11.3 358.3 %all-reduce.5.cloned.1.call-start = ((), (), s32[]{:S(2)}) async-start(), calls=%async_computation.11 | async-start | bytes 8388608 | tf_op jit(solution)/shard_map/psum | solution.py:153
  53.6 63.4 %copy-start.22 = (f32[1,1024]{1,0:T(1,128)}, f32[1,1024]{1,0:T(1,128)S(1)}, u32[]{:S(2)}) copy-start(f32[1,1024]{1,0:T(1,128)S(1)} %get-tuple-element.407) | copy-start | bytes 12292
  54.3 62.7 %copy-start.33 = (f32[1,1024]{1,0:T(1,128)}, f32[1,1024]{1,0:T(1,128)S(1)}, u32[]{:S(2)}) copy-start(f32[1,1024]{1,0:T(1,128)S(1)} %get-tuple-element.409) | copy-start | bytes 12292
  72.5 44.6 %copy-start.27 = (f32[2048]{0:T(1024)}, f32[2048]{0:T(1024)S(1)}, u32[]{:S(2)}) copy-start(f32[2048]{0:T(1024)S(1)} %broadcast_multiply_fusion.1) | copy-start | bytes 24580
  73.9 43.2 %copy-start.31 = (f32[2048]{0:T(1024)}, f32[2048]{0:T(1024)S(1)}, u32[]{:S(2)}) copy-start(f32[2048]{0:T(1024)S(1)} %add_rsqrt_fusion.1) | copy-start | bytes 24580
  262.7 160.3 %all-gather.16.cloned.1.call-start = ((), (), s32[]{:S(2)}) async-start(), calls=%async_computation.12 | async-start | bytes 4456448 | tf_op jit(solution)/shard_map/all_gather | solution.py:118
  264.5 215.3 %all-gather.20.cloned.1.call-start = ((), (), s32[]{:S(2)}) async-start(), calls=%async_computation.15 | async-start | bytes 6291456 | tf_op jit(solution)/shard_map/all_gather | solution.py:168
  265.0 268.2 %all-gather.18.cloned.1.call-start = ((), (), s32[]{:S(2)}) async-start(), calls=%async_computation.13 | async-start | bytes 4456448 | tf_op jit(solution)/shard_map/all_gather | solution.py:119
  265.9 356.6 %reduce-scatter.15.cloned.1.call-start = ((), (), s32[]{:S(2)}) async-start(), calls=%async_computation.16 | async-start | bytes 6291456 | tf_op jit(solution)/shard_map/reduce_scatter | solution.py:186
  377.5 45.5 %copy-start.26 = (f32[1,1024]{1,0:T(1,128)S(1)}, f32[1,1024]{1,0:T(1,128)}, u32[]{:S(2)}) copy-start(f32[1,1024]{1,0:T(1,128)} %get-tuple-element.408) | copy-start | bytes 12292
  377.5 45.5 %copy-start.35 = (f32[1,1024]{1,0:T(1,128)S(1)}, f32[1,1024]{1,0:T(1,128)}, u32[]{:S(2)}) copy-start(f32[1,1024]{1,0:T(1,128)} %get-tuple-element.410) | copy-start | bytes 12292
  533.3 25.5 %copy-start.36 = (bf16[1024,2048]{1,0:T(8,128)(2,1)S(1)}, bf16[1024,2048]{1,0:T(8,128)(2,1)}, u32[]{:S(2)}) copy-start(bf16[1024,2048]{1,0:T(8,128)(2,1)} %all-gather.16.cloned.1.call-done) | copy-start | bytes 12582916
  569.5 109.6 %reduce-scatter.13.cloned.1.call-start = ((), (), s32[]{:S(2)}) async-start(), calls=%async_computation.14 | async-start | bytes 6291456 | tf_op jit(solution)/shard_map/reduce_scatter | solution.py:164
  585.9 159.4 %all-gather.22.cloned.1.call-start = ((), (), s32[]{:S(2)}) async-start(), calls=%async_computation.17 | async-start | bytes 6291456 | tf_op jit(solution)/shard_map/all_gather | solution.py:192
  627.2 59.3 %copy-start.14 = (bf16[1,1024,1024]{2,1,0:T(8,128)(2,1)S(1)}, bf16[1,1024,1024]{2,1,0:T(8,128)(2,1)}, u32[]{:S(2)}) copy-start(bf16[1,1024,1024]{2,1,0:T(8,128)(2,1)} %param.21) | copy-start | bytes 6291460
  688.4 396.9 %reduce-scatter.23.cloned.1.call-start = ((), (), s32[]{:S(2)}) async-start(), calls=%async_computation.21 | async-start | bytes 4456448 | tf_op jit(solution)/shard_map/reduce_scatter | solution.py:241
  704.3 382.8 %reduce-scatter.21.cloned.1.call-start = ((), (), s32[]{:S(2)}) async-start(), calls=%async_computation.20 | async-start | bytes 4456448 | tf_op jit(solution)/shard_map/reduce_scatter | solution.py:238
  720.8 24.5 %copy-start.37 = (bf16[512,1024]{0,1:T(8,128)(2,1)S(1)}, bf16[512,1024]{0,1:T(8,128)(2,1)}, u32[]{:S(2)}) copy-start(bf16[512,1024]{0,1:T(8,128)(2,1)} %all-gather.14.cloned.1.call-done) | copy-start | bytes 3145732
  720.8 32.1 %copy-start.19 = (s32[1,2048]{1,0:T(1,128)S(1)}, s32[1,2048]{1,0:T(1,128)}, u32[]{:S(2)}) copy-start(s32[1,2048]{1,0:T(1,128)} %param.14) | copy-start | bytes 24580
  720.9 32.1 %copy-start.40 = (s32[4]{0:T(128)S(1)}, s32[4]{0:T(128)}, u32[]{:S(2)}) copy-start(s32[4]{0:T(128)} %copy-done.39) | copy-start | bytes 52
  720.9 455.4 %all-reduce.7.cloned.1.call-start = ((), (), s32[]{:S(2)}) async-start(), calls=%async_computation.24 | async-start | bytes 8388608
  784.7 20.0 %copy-start.3 = (f32[2048,4,128]{0,2,1:T(8,128)S(1)}, f32[2048,4,128]{0,2,1:T(8,128)}, u32[]{:S(2)}) copy-start(f32[2048,4,128]{0,2,1:T(8,128)} %get-tuple-element.604) | copy-start | bytes 12582916 | tf_op jit(solution)/shard_map/while/body/eval_jaxpr/while
  1064.1 171.9 %reduce-scatter.19.cloned.1.call-start = ((), (), s32[]{:S(2)}) async-start(), calls=%async_computation.19 | async-start | bytes 1114112 | tf_op jit(solution)/shard_map/reduce_scatter | solution.py:235
  1071.2 220.4 %reduce-scatter.17.cloned.1.call-start = ((), (), s32[]{:S(2)}) async-start(), calls=%async_computation.18 | async-start | bytes 6291456 | tf_op jit(solution)/shard_map/reduce_scatter | solution.py:222
  1083.0 279.1 %reduce-scatter.25.cloned.1.call-start = ((), (), s32[]{:S(2)}) async-start(), calls=%async_computation.22 | async-start | bytes 278528
  1237.5 60.2 %copy-start.29 = (f32[1024]{0:T(1024)S(1)}, f32[1024]{0:T(1024)}, u32[]{:S(2)}) copy-start(f32[1024]{0:T(1024)} %get-tuple-element.343) | copy-start | bytes 12292
  1237.5 60.2 %copy-start.30 = (f32[1024]{0:T(1024)S(1)}, f32[1024]{0:T(1024)}, u32[]{:S(2)}) copy-start(f32[1024]{0:T(1024)} %get-tuple-element.350) | copy-start | bytes 12292
  1237.5 69.0 %copy-start.25 = (f32[1024]{0:T(1024)S(1)}, f32[1024]{0:T(1024)}, u32[]{:S(2)}) copy-start(f32[1024]{0:T(1024)} %copy-done.24) | copy-start | bytes 12292
  1305.6 114.3 %reduce-scatter.27.cloned.1.call-start = ((), (), s32[]{:S(2)}) async-start(), calls=%async_computation.23 | async-start | bytes 278528
  (54 other events, 380.1 us)
Sparse Core Ops, SparseCore 0:
  9.5 59.4 all-gather.9
  71.8 45.1 all-gather.11
  119.8 36.7 all-gather.13
  262.8 106.6 all-reduce.4
  372.4 50.5 all-gather.15
  424.4 55.2 all-gather.19
  482.7 50.5 all-gather.17
  569.6 52.7 reduce-scatter.14
  624.7 54.2 reduce-scatter.12
  688.5 56.7 all-gather.21
  749.7 72.7 reduce-scatter.22
  826.2 71.4 reduce-scatter.20
  1064.2 111.9 all-reduce.6
  1179.7 56.2 reduce-scatter.18
  1238.3 53.3 reduce-scatter.16
  1305.7 56.3 reduce-scatter.24
  1365.5 54.3 reduce-scatter.26
where the time goes:
time: 1440 us; the launch traced here: 1430 us
  waiting for transfers between devices  714 us (50%)
  matrix products  378 us (26%)
  other arithmetic  169 us (12%)
  local copies, waits for them, and re-layouts  87.8 us (6%)
  blocking collectives  47.1 us (3%)
  loops' own time  16.8 us (1%)
  between operations  15.4 us (1%)
    unnamed x20, waiting for transfers between devices  195 us
    psum x1, waiting for transfers between devices, shards(): lax.psum(attention_slice.astype(jnp.bfloat16), 'tensor').astype(jnp.float32)  103 us
    dot_general x8, matrix products, block_scores(): jnp.einsum('qhd,khd->hqk', query_rows, keys, preferred_element_type=jnp.f...  88 us
    convert_element_type x4, other arithmetic, one_block(): grad_scores = (probs * (grad_probs - inner)).astype(jnp.bfloat16)  60.5 us
    reduce_scatter x1, waiting for transfers between devices, shards(): lax.psum_scatter(grad_out_local.astype(jnp.bfloat16), 'dp', scatter_dimen...  57.9 us
    reduce_scatter x1, waiting for transfers between devices, shards(): lax.psum_scatter(norm1_part.astype(jnp.bfloat16), 'tensor', scatter_dimen...  54.1 us
    all_gather x1, waiting for transfers between devices, shards(): lax.all_gather(low_copies[3], 'dp', axis=1, tiled=True)  53.6 us
    reduce_scatter x1, waiting for transfers between devices, shards(): lax.psum_scatter(feedforward_slice.astype(jnp.bfloat16), 'tensor', scatte...  51.9 us
  transfers between devices with their start and end apart: 17, of which 14 were waited for; matrix products, arithmetic and copies ran while one was open for 38% of the time, Pallas kernels for 0%

commit v1 on v0

--- a/solution.py
+++ b/solution.py
@@ -3,6 +3,8 @@
 import jax
 import jax.numpy as jnp
 from jax import lax
+from jax.experimental import pallas as pl
+from jax.experimental.pallas import tpu as pltpu
 from jax.sharding import PartitionSpec as P
 
 HEAD = 128
@@ -251,9 +253,628 @@
     return (result, grad_tokens, summed[0], summed[1], summed[2], summed[3], summed[4], summed[5])
 
 
+LOG2E = math.log2(math.e)
+SCALE2 = LOG2E / math.sqrt(HEAD)
+BLK = 512
+BF = jnp.bfloat16
+F32 = jnp.float32
+NN = (((1,), (0,)), ((), ()))
+NT = (((1,), (1,)), ((), ()))
+TN = (((0,), (0,)), ((), ()))
+RING = (0, 2, 4, 6, 7, 5, 3, 1)
+
+
+def mm(a, b, dims):
+    return lax.dot_general(a, b, dims, preferred_element_type=F32)
+
+
+def params(mib, cost=None):
+    return dict(compiler_params=pltpu.CompilerParams(vmem_limit_bytes=mib * 2**20))
+
+
+def cost(flops, nbytes, trans=0):
+    return pl.CostEstimate(flops=int(flops), bytes_accessed=int(nbytes), transcendentals=int(trans))
+
+
+def normalize(v):
+    c = v - jnp.mean(v, axis=-1, keepdims=True)
+    r = lax.rsqrt(jnp.mean(c * c, axis=-1, keepdims=True) + eps_norm)
+    return c * r, r
+
+
+def norm_back(v, dout, gain):
+    cn, r = normalize(v)
+    t = dout * gain
+    dv = r * (t - jnp.mean(t, axis=-1, keepdims=True) - cn * jnp.mean(t * cn, axis=-1, keepdims=True))
+    return dv, jnp.sum(dout * cn, axis=0, keepdims=True), jnp.sum(dout, axis=0, keepdims=True)
+
+
+def project_kernel(core, xa, xb, gb, w, a1_out, qkv_out):
+    step = pl.program_id(0)
+    half = pl.num_programs(0) // 2
+    x = jnp.where(step < half, xa[...], xb[...]).astype(F32)
+    a1 = (normalize(x)[0] * gb[0:1] + gb[2:3]).astype(BF)
+    a1_out[...] = a1
+    weight = w[:, 0].reshape(w.shape[0] * w.shape[2], w.shape[3])
+    qkv_out[...] = mm(a1, weight, NN).astype(BF)
+
+
+def project(core, x_own, x_oth, gb, g1):
+    rows, width = x_own.shape
+    tile = 512
+    half = rows // tile
+    nd, _, per, cols = g1.shape
+    wide = 3 * 512
+    spec = pltpu.PrefetchScalarGridSpec(
+        num_scalar_prefetch=1,
+        grid=(2 * half,),
+        in_specs=[
+            pl.BlockSpec((tile, width), lambda i, c: (jnp.minimum(i, half - 1), 0)),
+            pl.BlockSpec((tile, width), lambda i, c: (jnp.maximum(i - half, 0), 0)),
+            pl.BlockSpec((4, width), lambda i, c: (0, 0)),
+            pl.BlockSpec((nd, 1, per, wide), lambda i, c: (0, c[0], 0, 0)),
+        ],
+        out_specs=[
+            pl.BlockSpec((tile, width), lambda i, c: (i % half + half * ((i // half) ^ c[0]), 0)),
+            pl.BlockSpec((tile, wide), lambda i, c: (i % half + half * ((i // half) ^ c[0]), 0)),
+        ],
+    )
+    return pl.pallas_call(
+        project_kernel,
+        grid_spec=spec,
+        out_shape=[
+            jax.ShapeDtypeStruct((2 * rows, width), BF),
+            jax.ShapeDtypeStruct((2 * rows, wide), BF),
+        ],
+        cost_estimate=cost(4 * rows * width * wide, 12 * 2**20),
+        **params(48),
+    )(core, x_own, x_oth, gb, g1)
+
+
+def attend_kernel(slopes, q_ref, k_ref, v_ref, seg_ref, o_ref, l_ref, s_ref):
+    m2 = slopes[pl.program_id(0)]
+    blocks = q_ref.shape[0] // BLK
+    lane = lax.broadcasted_iota(jnp.int32, (1, BLK), 1)
+    row = lax.broadcasted_iota(jnp.int32, (BLK, 1), 0)
+    for i in range(blocks):
+        q = q_ref[i * BLK : (i + 1) * BLK, :]
+        seg = seg_ref[i * BLK : (i + 1) * BLK, :]
+        top = jnp.full((BLK, 128), masked_score, F32)
+        for j in range(i + 1):
+            cols = slice(j * BLK, (j + 1) * BLK)
+            bias = m2 * (lane + (j - i) * BLK).astype(F32)
+            s = mm(q, k_ref[cols, :], NT) * SCALE2 + bias
+            allowed = (lane + j * BLK) >= seg
+            if j == i:
+                allowed = allowed & (lane <= row)
+            s = jnp.where(allowed, s, masked_score)
+            s_ref[:, cols] = s
+            for c in range(0, BLK, 128):
+                top = jnp.maximum(top, s[:, c : c + 128])
+        top = jnp.max(top, axis=1, keepdims=True)
+        total = jnp.zeros((BLK, 128), F32)
+        mixed = jnp.zeros((BLK, HEAD), F32)
+        for j in range(i + 1):
+            cols = slice(j * BLK, (j + 1) * BLK)
+            p = jnp.exp2(s_ref[:, cols] - top)
+            for c in range(0, BLK, 128):
+                total = total + p[:, c : c + 128]
+            mixed = mixed + mm(p.astype(BF), v_ref[cols, :], NN)
+        total = jnp.sum(total, axis=1, keepdims=True)
+        o_ref[i * BLK : (i + 1) * BLK, :] = (mixed / total).astype(BF)
+        logs = jnp.broadcast_to(top + jnp.log2(total), (BLK, 128))
+        l_ref[0, :, i * BLK : (i + 1) * BLK] = logs.T[0:1, :]
+
+
+def attend(slopes, qkv, seg_col):
+    length = qkv.shape[0]
+    heads = qkv.shape[1] // (3 * HEAD)
+    spec = pltpu.PrefetchScalarGridSpec(
+        num_scalar_prefetch=1,
+        grid=(heads,),
+        in_specs=[
+            pl.BlockSpec((length, HEAD), lambda h, s: (0, h)),
+            pl.BlockSpec((length, HEAD), lambda h, s: (0, heads + h)),
+            pl.BlockSpec((length, HEAD), lambda h, s: (0, 2 * heads + h)),
+            pl.BlockSpec((length, 1), lambda h, s: (0, 0)),
+        ],
+        out_specs=[
+            pl.BlockSpec((length, HEAD), lambda h, s: (0, h)),
+            pl.BlockSpec((1, 1, length), lambda h, s: (h, 0, 0)),
+        ],
+        scratch_shapes=[pltpu.VMEM((BLK, length), F32)],
+    )
+    return pl.pallas_call(
+        attend_kernel,
+        grid_spec=spec,
+        out_shape=[
+            jax.ShapeDtypeStruct((length, heads * HEAD), BF),
+            jax.ShapeDtypeStruct((heads, 1, length), F32),
+        ],
+        cost_estimate=cost(heads * 4 * length * length * HEAD, 10 * 2**20, heads * length * length),
+        **params(48),
+    )(slopes, qkv, qkv, qkv, seg_col)
+
+
+def attend_back_kernel(slopes, q_ref, k_ref, v_ref, do_ref, o_ref, l_ref, seg_ref, dq_ref, dk_ref, dv_ref, acc, inner):
+    m2 = slopes[pl.program_id(0)]
+    blocks = q_ref.shape[0] // BLK
+    lane = lax.broadcasted_iota(jnp.int32, (1, BLK), 1)
+    row = lax.broadcasted_iota(jnp.int32, (BLK, 1), 0)
+    for i in range(blocks):
+        rows = slice(i * BLK, (i + 1) * BLK)
+        d = jnp.sum(do_ref[rows, :].astype(F32) * o_ref[rows, :].astype(F32), axis=1, keepdims=True)
+        inner[:, rows] = jnp.broadcast_to(d, (BLK, 128)).T[0:8, :]
+    for j in range(blocks):
+        cols = slice(j * BLK, (j + 1) * BLK)
+        kj, vj = k_ref[cols, :], v_ref[cols, :]
+        dk = jnp.zeros((BLK, HEAD), F32)
+        dv = jnp.zeros((BLK, HEAD), F32)
+        for i in range(j, blocks):
+            rows = slice(i * BLK, (i + 1) * BLK)
+            qi, doi = q_ref[rows, :], do_ref[rows, :]
+            bias = m2 * (row + (j - i) * BLK).astype(F32)
+            s = mm(kj, qi, NT) * SCALE2 + bias - l_ref[0, :, rows]
+            allowed = (row + j * BLK) >= seg_ref[:, rows]
+            if j == i:
+                allowed = allowed & (row <= lane)
+            p = jnp.exp2(jnp.where(allowed, s, masked_score))
+            ds = (p * (mm(vj, doi, NT) - inner[0:1, rows])).astype(BF)
+            dv = dv + mm(p.astype(BF), doi, NN)
+            dk = dk + mm(ds, qi, NN)
+            dq = mm(ds, kj, TN)
+            if j == 0:
+                acc[rows, :] = dq
+            else:
+                acc[rows, :] += dq
+        dk_ref[cols, :] = (dk * (1.0 / math.sqrt(HEAD))).astype(BF)
+        dv_ref[cols, :] = dv.astype(BF)
+    dq_ref[...] = (acc[...] * (1.0 / math.sqrt(HEAD))).astype(BF)
+
+
+def attend_back(slopes, qkv, grad, mixed, logs, seg_row, first, count):
+    length = qkv.shape[0]
+    heads = qkv.shape[1] // (3 * HEAD)
+    spec = pltpu.PrefetchScalarGridSpec(
+        num_scalar_prefetch=1,
+        grid=(count,),
+        in_specs=[
+            pl.BlockSpec((length, HEAD), lambda h, s: (0, first + h)),
+            pl.BlockSpec((length, HEAD), lambda h, s: (0, heads + first + h)),
+            pl.BlockSpec((length, HEAD), lambda h, s: (0, 2 * heads + first + h)),
+            pl.BlockSpec((length, HEAD), lambda h, s: (0, first + h)),
+            pl.BlockSpec((length, HEAD), lambda h, s: (0, first + h)),
+            pl.BlockSpec((1, 1, length), lambda h, s: (first + h, 0, 0)),
+            pl.BlockSpec((1, length), lambda h, s: (0, 0)),
+        ],
+        out_specs=[pl.BlockSpec((length, HEAD), lambda h, s: (0, h))] * 3,
+        scratch_shapes=[pltpu.VMEM((length, HEAD), F32), pltpu.VMEM((8, length), F32)],
+    )
+    return pl.pallas_call(
+        attend_back_kernel,
+        grid_spec=spec,
+        out_shape=[jax.ShapeDtypeStruct((length, count * HEAD), BF)] * 3,
+        cost_estimate=cost(count * 10 * length * length * HEAD, 5 * count * 2**20, count * length * length),
+        **params(48),
+    )(lax.slice_in_dim(slopes, first, first + count), qkv, qkv, qkv, grad, mixed, logs, seg_row)
+
+
+def branch_kernel(core, o_ref, w, x_ref, oth_out, own_out):
+    step = pl.program_id(0)
+    half = pl.num_programs(0) // 2
+    weight = w[:, 0].reshape(w.shape[0] * w.shape[2], w.shape[3])
+    part = mm(o_ref[...], weight, NT)
+
+    @pl.when(step < half)
+    def _():
+        oth_out[...] = part.astype(BF)
+
+    @pl.when(step >= half)
+    def _():
+        own_out[...] = x_ref[...].astype(F32) + part
+
+
+def branch(core, mixed, g1, x_own):
+    rows, width = x_own.shape
+    tile = 512
+    half = rows // tile
+    nd, _, per, cols = g1.shape
+    spec = pltpu.PrefetchScalarGridSpec(
+        num_scalar_prefetch=1,
+        grid=(2 * half,),
+        in_specs=[
+            pl.BlockSpec((tile, 512), lambda i, c: (i % half + half * (1 - (i // half) ^ c[0]), 0)),
+            pl.BlockSpec((nd, 1, per, 512), lambda i, c: (0, c[0], 0, 3)),
+            pl.BlockSpec((tile, width), lambda i, c: (jnp.maximum(i - half, 0), 0)),
+        ],
+        out_specs=[
+            pl.BlockSpec((tile, width), lambda i, c: (jnp.minimum(i, half - 1), 0)),
+            pl.BlockSpec((tile, width), lambda i, c: (jnp.maximum(i - half, 0), 0)),
+        ],
+    )
+    return pl.pallas_call(
+        branch_kernel,
+        grid_spec=spec,
+        out_shape=[
+            jax.ShapeDtypeStruct((rows, width), BF),
+            jax.ShapeDtypeStruct((rows, width), F32),
+        ],
+        cost_estimate=cost(4 * rows * width * 512, 12 * 2**20),
+        **params(48),
+    )(core, mixed, g1, x_own)
+
+
+def residual_kernel(part, recv, gb, h_out, a2_out):
+    h = part[...] + recv[...].astype(F32)
+    h_out[...] = h
+    a2_out[...] = (normalize(h)[0] * gb[1:2] + gb[3:4]).astype(BF)
+
+
+def residual(part, recv, gb):
+    rows, width = part.shape
+    tile = 256
+    spec = pl.BlockSpec((tile, width), lambda i: (i, 0))
+    return pl.pallas_call(
+        residual_kernel,
+        grid=(rows // tile,),
+        in_specs=[spec, spec, pl.BlockSpec((4, width), lambda i: (0, 0))],
+        out_specs=[spec, spec],
+        out_shape=[
+            jax.ShapeDtypeStruct((rows, width), F32),
+            jax.ShapeDtypeStruct((rows, width), BF),
+        ],
+        cost_estimate=cost(20 * rows * width, 12 * 2**20),
+        **params(32),
+    )(part, recv, gb)
+
+
+def feed_kernel(core, aa, ab, ya, yb, w1_ref, w2_ref, f_out, d_out, g1_out, g2_out, acc1, acc2, g_s, du_s):
+    step = pl.program_id(0)
+    steps = pl.num_programs(0)
+    half = steps // 2
+    hidden = w1_ref.shape[3]
+    width = aa.shape[1]
+    a2 = jnp.where(step < half, aa[...], ab[...])
+    dy = jnp.where(step < half, ya[...], yb[...])
+    a2t, dyt = a2.T, dy.T
+    chunk = 512
+
+    @pl.when(step == 0)
+    def _():
+        acc1[...] = jnp.zeros_like(acc1)
+        acc2[...] = jnp.zeros_like(acc2)
+
+    c0, c1 = math.sqrt(2.0 / math.pi), 0.044715
+    for c in range(0, hidden, chunk):
+        cols = slice(c, c + chunk)
+        w1 = w1_ref[:, 0, :, cols].reshape(width, chunk)
+        w2 = w2_ref[:, 0, :, cols].reshape(width, chunk)
+        u = mm(a2, w1, NN)
+        sq = u * u
+        th = jnp.tanh(u * (c0 + c0 * c1 * sq))
+        hp = 0.5 + 0.5 * th
+        g = (u * hp).astype(BF)
+        slope = hp + (0.5 * u) * (1.0 - th * th) * (c0 + 3.0 * c0 * c1 * sq)
+        du = (mm(dy, w2, NN) * slope).astype(BF)
+        g_s[:, cols] = g
+        du_s[:, cols] = du
+        acc1[:, cols] += mm(a2t, du, NN)
+        acc2[:, cols] += mm(dyt, g, NN)
+    f_out[0] = mm(g_s[...], w2_ref[:, 0].reshape(width, hidden), NT).astype(BF)
+    d_out[0] = mm(du_s[...], w1_ref[:, 0].reshape(width, hidden), NT).astype(BF)
+
+    @pl.when(step == steps - 1)
+    def _():
+        g1_out[:, 0] = acc1[...].astype(BF).reshape(g1_out.shape[0], g1_out.shape[2], hidden)
+        g2_out[:, 0] = acc2[...].astype(BF).reshape(g1_out.shape[0], g1_out.shape[2], hidden)
+
+
+def feed(core, a_own, a_oth, y_own, y_oth, w1, w2):
+    rows, width = a_own.shape
+    tile = 512
+    half = rows // tile
+    nd, _, per, hidden = w1.shape
+    chips = nd // 2
+    own = pl.BlockSpec((tile, width), lambda i, c: (jnp.minimum(i, half - 1), 0))
+    oth = pl.BlockSpec((tile, width), lambda i, c: (jnp.maximum(i - half, 0), 0))
+    weight = pl.BlockSpec((nd, 1, per, hidden), lambda i, c: (0, c[0], 0, 0), pipeline_mode=pl.Buffered(1))
+    out = pl.BlockSpec((1, tile, width), lambda i, c: (i // half, i % half, 0))
+    gout = pl.BlockSpec((chips, 1, 2 * per, hidden), lambda i, c: (0, 0, 0, 0), pipeline_mode=pl.Buffered(1))
+    spec = pltpu.PrefetchScalarGridSpec(
+        num_scalar_prefetch=1,
+        grid=(2 * half,),
+        in_specs=[own, oth, own, oth, weight, weight],
+        out_specs=[out, out, gout, gout],
+        scratch_shapes=[
+            pltpu.VMEM((width, hidden), F32),
+            pltpu.VMEM((width, hidden), F32),
+            pltpu.VMEM((tile, hidden), BF),
+            pltpu.VMEM((tile, hidden), BF),
+        ],
+    )
+    return pl.pallas_call(
+        feed_kernel,
+        grid_spec=spec,
+        out_shape=[
+            jax.ShapeDtypeStruct((2, rows, width), BF),
+            jax.ShapeDtypeStruct((2, rows, width), BF),
+            jax.ShapeDtypeStruct((chips, 1, 2 * per, hidden), BF),
+            jax.ShapeDtypeStruct((chips, 1, 2 * per, hidden), BF),
+        ],
+        cost_estimate=cost(24 * rows * width * hidden, 40 * 2**20, 2 * rows * hidden),
+        **params(60),
+    )(core, a_own, a_oth, y_own, y_oth, w1, w2)
+
+
+def norm_back_kernel(v_ref, part, recv, skip, gain, dv_out, low_out, sums):
+    @pl.when(pl.program_id(0) == 0)
+    def _():
+        sums[...] = jnp.zeros_like(sums)
+
+    dout = part[...].astype(F32) + recv[...].astype(F32)
+    dv, dg, db = norm_back(v_ref[...].astype(F32), dout, gain[...])
+    dv = skip[...].astype(F32) + dv
+    if dv_out is not None:
+        dv_out[...] = dv
+    low_out[...] = dv.astype(BF)
+    sums[0:1] += dg
+    sums[1:2] += db
+
+
+def through_norm(v, part, recv, skip, gain, keep):
+    rows, width = v.shape
+    tile = 256
+    spec = pl.BlockSpec((tile, width), lambda i: (i, 0))
+    kernel = norm_back_kernel if keep else (lambda *r: norm_back_kernel(*r[:5], None, *r[5:]))
+    outs = [jax.ShapeDtypeStruct((rows, width), F32)] if keep else []
+    return pl.pallas_call(
+        kernel,
+        grid=(rows // tile,),
+        in_specs=[spec] * 4 + [pl.BlockSpec((1, width), lambda i: (0, 0))],
+        out_specs=[spec] * (1 + keep) + [pl.BlockSpec((2, width), lambda i: (0, 0))],
+        out_shape=outs + [jax.ShapeDtypeStruct((rows, width), BF), jax.ShapeDtypeStruct((2, width), F32)],
+        cost_estimate=cost(30 * rows * width, 16 * 2**20),
+        **params(32),
+    )(v, part, recv, skip, gain)
+
+
+def head_grad_kernel(core, da, db, o_ref, w, do_out, gw_out, acc):
+    step = pl.program_id(0)
+    steps = pl.num_programs(0)
+    d = jnp.where(step < steps // 2, da[...], db[...])
+    weight = w[:, 0].reshape(w.shape[0] * w.shape[2], w.shape[3])
+    do_out[...] = mm(d, weight, NN).astype(BF)
+
+    @pl.when(step == 0)
+    def _():
+        acc[...] = jnp.zeros_like(acc)
+
+    acc[...] += mm(d, o_ref[...], TN)
+
+    @pl.when(step == steps - 1)
+    def _():
+        gw_out[...] = acc[...].astype(BF)
+
+
+def head_grad(core, d_own, d_oth, mixed, g1):
+    rows, width = d_own.shape
+    tile = 512
+    half = rows // tile
+    nd, _, per, cols = g1.shape
+    spec = pltpu.PrefetchScalarGridSpec(
+        num_scalar_prefetch=1,
+        grid=(2 * half,),
+        in_specs=[
+            pl.BlockSpec((tile, width), lambda i, c: (jnp.minimum(i, half - 1), 0)),
+            pl.BlockSpec((tile, width), lambda i, c: (jnp.maximum(i - half, 0), 0)),
+            pl.BlockSpec((tile, 512), lambda i, c: (i % half + half * ((i // half) ^ c[0]), 0)),
+            pl.BlockSpec((nd, 1, per, 512), lambda i, c: (0, c[0], 0, 3)),
+        ],
+        out_specs=[
+            pl.BlockSpec((tile, 512), lambda i, c: (i % half + half * ((i // half) ^ c[0]), 0)),
+            pl.BlockSpec((width, 512), lambda i, c: (0, 0)),
+        ],
+        scratch_shapes=[pltpu.VMEM((width, 512), F32)],
+    )
+    return pl.pallas_call(
+        head_grad_kernel,
+        grid_spec=spec,
+        out_shape=[
+            jax.ShapeDtypeStruct((2 * rows, 512), BF),
+            jax.ShapeDtypeStruct((width, 512), BF),
+        ],
+        cost_estimate=cost(8 * rows * width * 512, 12 * 2**20),
+        **params(48),
+    )(core, d_own, d_oth, mixed, g1)
+
+
+def project_back_kernel(core, a1, q0, q1, k0, k1, v0, v1, w, d_oth, d_own, gw_out, acc):
+    step = pl.program_id(0)
+    steps = pl.num_programs(0)
+    grad = jnp.concatenate([q0[...], q1[...], k0[...], k1[...], v0[...], v1[...]], axis=1)
+    weight = w[:, 0].reshape(w.shape[0] * w.shape[2], w.shape[3])
+    part = mm(grad, weight, NT)
+
+    @pl.when(step < steps // 2)
+    def _():
+        d_oth[...] = part.astype(BF)
+
+    @pl.when(step >= steps // 2)
+    def _():
+        d_own[...] = part
+
+    @pl.when(step == 0)
+    def _():
+        acc[...] = jnp.zeros_like(acc)
+
+    acc[...] += mm(a1[...], grad, TN)
+
+    @pl.when(step == steps - 1)
+    def _():
+        gw_out[...] = acc[...].astype(BF)
+
+
+def project_back(core, a1, grads, g1):
+    rows2, width = a1.shape
+    rows = rows2 // 2
+    tile = 512
+    half = rows // tile
+    nd, _, per, cols = g1.shape
+    wide = 3 * 512
+
+    def place(i, c):
+        return (i % half + half * (1 - (i // half) ^ c[0]), 0)
+
+    spec = pltpu.PrefetchScalarGridSpec(
+        num_scalar_prefetch=1,
+        grid=(2 * half,),
+        in_specs=[pl.BlockSpec((tile, width), place)]
+        + [pl.BlockSpec((tile, g.shape[1]), place) for g in grads]
+        + [pl.BlockSpec((nd, 1, per, wide), lambda i, c: (0, c[0], 0, 0))],
+        out_specs=[
+            pl.BlockSpec((tile, width), lambda i, c: (jnp.minimum(i, half - 1), 0)),
+            pl.BlockSpec((tile, width), lambda i, c: (jnp.maximum(i - half, 0), 0)),
+            pl.BlockSpec((width, wide), lambda i, c: (0, 0)),
+        ],
+        scratch_shapes=[pltpu.VMEM((width, wide), F32)],
+    )
+    return pl.pallas_call(
+        project_back_kernel,
+        grid_spec=spec,
+        out_shape=[
+            jax.ShapeDtypeStruct((rows, width), BF),
+            jax.ShapeDtypeStruct((rows, width), F32),
+            jax.ShapeDtypeStruct((width, wide), BF),
+        ],
+        cost_estimate=cost(8 * rows * width * wide, 20 * 2**20),
+        **params(56),
+    )(core, a1, *grads, g1)
+
+
+def fast_shards(tokens, segment_ids, w_qkv, w_out, w_in, w_back, norm_gains, norm_biases, cotangent):
+    both = ("dp", "tensor")
+    dp_rank, y = lax.axis_index("dp"), lax.axis_index("tensor")
+    n_dp = lax.axis_size("dp")
+    core, chip = dp_rank % 2, dp_rank // 2
+    chips = n_dp // 2
+    at_home = core == y
+
+    def ident(q, k, j):
+        return (q * 2 + k) * 2 + j
+
+    cells = [(q, k, j) for q in range(chips) for k in range(2) for j in range(2)]
+    to_core = [(ident(q, k, j), ident(q, 1 - k, j)) for q, k, j in cells]
+    to_y = [(ident(q, k, j), ident(q, k, 1 - j)) for q, k, j in cells]
+    diagonal = [(ident(q, k, j), ident(q, j, k)) for q, k, j in cells]
+    place_of = {q: p for p, q in enumerate(RING)}
+    turn = {d: [(ident(q, k, j), ident(RING[(place_of[q] + d) % chips], k, j)) for q, k, j in cells] for d in (1, -1)}
+
+    def send(v, pairs):
+        return lax.ppermute(v, both, pairs)
+
+    _, own_len, width = tokens.shape
+    core_arg = core.astype(jnp.int32)[None]
+
+    pad = jnp.zeros((norm_gains.shape[1], 124), BF)
+    shard1 = jnp.concatenate(
+        [w_qkv[0], w_qkv[1], w_qkv[2], w_out.T, norm_gains.T, norm_biases.T], axis=1
+    ).astype(BF)
+    shard1 = jnp.concatenate([shard1, pad], axis=1)
+    shard2 = w_in.astype(BF)
+    shard3 = w_back.T.astype(BF)
+    g1 = lax.all_gather(shard1, both)
+    shard2, shard3, g1 = lax.optimization_barrier((shard2, shard3, g1))
+    w1 = lax.all_gather(shard2, both)
+    w2 = lax.all_gather(shard3, both)
+    g1, w1, w2 = [w.reshape(n_dp, 2, *w.shape[1:]) for w in (g1, w1, w2)]
+    low = g1[:, 0, :, 2048:2052].reshape(width, 4).astype(F32).T
+    gb = low
+
+    seg = segment_ids
+    seg = jnp.where(at_home, seg, send(seg, to_core))
+    seg_col = seg.reshape(-1, 1)
+    heads = w_qkv.shape[2] // HEAD
+    slopes = jnp.exp2(-(core * heads + jnp.arange(heads, dtype=jnp.int32) + 1).astype(F32)) * LOG2E
+    x_own = send(tokens[0], diagonal)
+    x_oth = send(x_own, to_core)
+    y_own = send(cotangent[0], diagonal)
+    y_oth = send(y_own, to_core)
+
+    a1, qkv = project(core_arg, x_own, x_oth, gb, g1)
+    mixed, logs = attend(slopes, qkv, seg_col)
+    part_oth, part_own = branch(core_arg, mixed, g1, x_own)
+    h1, a2_own = residual(part_own, send(part_oth, to_core), gb)
+    a2_oth = send(a2_own, to_core)
+    f_part, d_part, gw1, gw2 = feed(core_arg, a2_own, a2_oth, y_own, y_oth, w1, w2)
+    d_recv = send(d_part[1], to_core)
+    f_recv = send(f_part[1], to_core)
+    dh1, da_own, sums2 = through_norm(h1, d_part[0], d_recv, y_own, gb[1:2], True)
+    da_oth = send(da_own, to_core)
+    result = (h1 + f_part[0].astype(F32) + f_recv.astype(F32)).astype(BF)
+    result = send(result, diagonal)
+    do, gwo = head_grad(core_arg, da_own, da_oth, mixed, g1)
+    parts = [attend_back(slopes, qkv, do, mixed, logs, seg, f, 2) for f in range(0, heads, 2)]
+    grads = [p[i] for i in range(3) for p in parts]
+    d1_oth, d1_own, gwq = project_back(core_arg, a1, grads, g1)
+    grad_tokens, sums1 = through_norm(x_own, d1_own, send(d1_oth, to_core), dh1, gb[0:1], False)
+    grad_tokens = send(grad_tokens, diagonal)
+
+    spot = jnp.take(jnp.array([place_of[q] for q in range(chips)], jnp.int32), chip)
+    order = jnp.array(RING, jnp.int32)
+
+    def reduce_ring(blocks):
+        def block(d):
+            return lax.dynamic_index_in_dim(blocks, jnp.take(order, (spot + d) % chips), 0, keepdims=False)
+
+        far = chips // 2
+        rows = blocks.shape[1] // 2
+        totals = []
+        for way in (1, -1):
+            piece = block(way * far)
+            piece = piece[:rows] if way == 1 else piece[rows:]
+            got = send(piece, turn[way])
+            for d in range(far - 1, 0, -1):
+                mine = block(way * d)
+                if d == far - 1:
+                    cut = slice(0, rows) if way == 1 else slice(rows, 2 * rows)
+                    added = mine[cut].astype(F32) + got.astype(F32)
+                    other = mine[rows:] if way == 1 else mine[:rows]
+                    both_parts = [added.astype(BF), other] if way == 1 else [other, added.astype(BF)]
+                    piece = jnp.concatenate(both_parts, axis=0)
+                else:
+                    piece = (mine.astype(F32) + got.astype(F32)).astype(BF)
+                got = send(piece, turn[way])
+            totals.append(got)
+        return block(0).astype(F32) + totals[0].astype(F32) + totals[1].astype(F32)
+
+    def to_owner(total):
+        per = total.shape[0] // 2
+        mine = lax.dynamic_slice_in_dim(total, core * per, per, 0)
+        theirs = lax.dynamic_slice_in_dim(total, (1 - core) * per, per, 0).astype(BF)
+        recv = send(theirs, to_core).astype(F32)
+        keep = jnp.where(at_home, mine, recv)
+        leave = jnp.where(at_home, recv, mine).astype(BF)
+        return keep + send(leave, to_y).astype(F32)
+
+    feed_blocks = jnp.concatenate([gw1, gw2], axis=1) if False else None
+    r1 = to_owner(reduce_ring(gw1[:, 0]))
+    r2 = to_owner(reduce_ring(gw2[:, 0]))
+    r3 = to_owner(reduce_ring(jnp.concatenate([gwq, gwo], axis=1).reshape(chips, width // chips, -1)))
+    grad_in = r1
+    grad_back = r2.T
+    per = r3.shape[0]
+    grad_qkv = r3[:, : 3 * 512].reshape(per, 3, 512).transpose(1, 0, 2)
+    grad_out = r3[:, 3 * 512 :].T
+    sums = jnp.concatenate([sums1[0:1], sums2[0:1], sums1[1:2], sums2[1:2]], axis=0)
+    sums = lax.psum(sums, both)
+    sums = lax.dynamic_slice_in_dim(sums, dp_rank * norm_gains.shape[1], norm_gains.shape[1], 1)
+    return (result[None], grad_tokens[None], grad_qkv, grad_out, grad_in, grad_back, sums[0:2], sums[2:4])
+
+
 def solution(mesh):
+    one_chip_plan = mesh.shape["dp"] == 16 and mesh.shape["tensor"] == 2
     return jax.shard_map(
-        shards,
+        fast_shards if one_chip_plan else shards,
         mesh=mesh,
         in_specs=(
             P("dp", "tensor", None),

time: 1440 us -> 643 us (0.45)
  waiting for transfers between devices: 714 us -> 218 us
  matrix products: 378 us -> 0 us
  Pallas kernels: 0 us -> 201 us
  other arithmetic: 169 us -> 24.1 us
  starting transfers between devices: 1.35 us -> 88.6 us
  local copies, waits for them, and re-layouts: 87.8 us -> 29.2 us
  loops' own time: 16.8 us -> 0 us
    dot_general x40 -> x0, matrix products: 378 us -> none  [the longest x8 88 us: block_scores(): jnp.einsum('qhd,khd->hqk', query_rows, keys, preferred_element_type=jnp.f...]
    pallas_call x0 -> x11, Pallas kernels: none -> 201 us  [the longest x1 80.3 us: feed(): pl.pallas_call(feed_kernel, grid_spec=spec, out_shape=[jax.ShapeDtypeStru...]
    reduce_scatter x6 -> x0, waiting for transfers between devices: 195 us -> none  [the longest x1 57.9 us: shards(): lax.psum_scatter(grad_out_local.astype(jnp.bfloat16), 'dp', scatter_dimen...]
    unnamed x20 -> x3, waiting for transfers between devices: 195 us -> 0.71 us
    psum x1 -> x0, waiting for transfers between devices: 103 us -> none  [shards(): lax.psum(attention_slice.astype(jnp.bfloat16), 'tensor').astype(jnp.float32)]
    all_gather x7 -> x3, waiting for transfers between devices: 220 us -> 129 us  [the longest x1 79 us: fast_shards(): g1 = lax.all_gather(shard1, both)]
    ppermute x0 -> x43, starting transfers between devices: none -> 88.5 us  [send(): return lax.ppermute(v, both, pairs)]
    ppermute x0 -> x43, waiting for transfers between devices: none -> 87.8 us  [send(): return lax.ppermute(v, both, pairs)]
  transfers between devices with their start and end apart: 17 -> 46, of which waited for: 14 -> 20; matrix products, arithmetic and copies ran while one was open for 38% -> 5% of each run, Pallas kernels for 0% -> 19%
where the time goes in v1:
time: 643 us; the launch traced here: 634 us
  waiting for transfers between devices  218 us (34%)
  Pallas kernels  201 us (31%)
  starting transfers between devices  88.6 us (14%)
  blocking collectives  51.9 us (8%)
  local copies, waits for them, and re-layouts  29.2 us (5%)
  other arithmetic  24.1 us (4%)
  between operations  21.7 us (3%)
    ppermute x43, starting transfers between devices, send(): return lax.ppermute(v, both, pairs)  88.5 us
    ppermute x43, waiting for transfers between devices, send(): return lax.ppermute(v, both, pairs)  87.8 us
    pallas_call x1, Pallas kernels, feed(): pl.pallas_call(feed_kernel, grid_spec=spec, out_shape=[jax.ShapeDtypeStru...  80.3 us
    all_gather x1, waiting for transfers between devices, fast_shards(): g1 = lax.all_gather(shard1, both)  79 us
    psum x1, blocking collectives, fast_shards(): sums = lax.psum(sums, both)  51.9 us
    all_gather x1, waiting for transfers between devices, fast_shards(): w2 = lax.all_gather(shard3, both)  50.1 us
    pallas_call x2, Pallas kernels, attend_back(): pl.pallas_call(attend_back_kernel, grid_spec=spec, out_shape=[jax.ShapeDt...  37.1 us
    pallas_call x1, Pallas kernels, attend(): pl.pallas_call(attend_kernel, grid_spec=spec, out_shape=[jax.ShapeDtypeSt...  23.2 us
  transfers between devices with their start and end apart: 46, of which 20 were waited for; matrix products, arithmetic and copies ran while one was open for 5% of the time, Pallas kernels for 19%

profile of v1, /device:TPU:0, one launch (start us, length us, event | category | flops | bytes accessed | tf_op | source)
XLA Modules:
  0.0 633.7 jit_solution(7007713975332930312)
XLA Ops:
  15.2 79.0 %all-gather.7.cloned.1.call-done = bf16[2048,2176]{1,0:T(8,128)(2,1)} async-done(((bf16[64,2176]{1,0:T(8,128)(2,1)}), bf16[2048,2176]{1,0:T(8,128)(2,1)}) %all-gather.7.cloned.1.call-update) | async-done | bytes 8912912 | tf_op jit(solution)/shard_map/all_gather | solution.py:785
  97.3 27.4 %collective-permute-start.1 = (bf16[1024,1024]{1,0:T(8,128)(2,1)S(1)}, bf16[1024,1024]{1,0:T(8,128)(2,1)}, u32[]{:S(2)}, u32[]{:S(2)}) collective-permute-start(bf16[1024,1024]{1,0:T(8,128)(2,1)S(1)} %collective-permute-done.xa.x_ref.r_0_), channel_id=1, source_target_pairs={{0,2},{1,3},{2,0},{3,1},{4,6},{5,7},{6,4},{7,5},{8,10},{9,11},{10,... | collective-permute-start | bytes 6291464 | tf_op jit(solution)/shard_map/ppermute | solution.py:773
  124.8 17.1 %collective-permute-start.5 = (bf16[1024,1024]{1,0:T(8,128)(2,1)}, bf16[1024,1024]{1,0:T(8,128)(2,1)}, u32[]{:S(2)}, u32[]{:S(2)}) collective-permute-start(bf16[1024,1024]{1,0:T(8,128)(2,1)} %bitcast.182), channel_id=1, source_target_pairs={{0,0},{1,2},{2,1},{3,3},{4,4},{5,6},{6,5},{7,7},{8,8},{9,10},{10,9... | collective-permute-start | bytes 6291464 | tf_op jit(solution)/shard_map/ppermute | solution.py:773
  145.5 12.9 %shard_map.170 = (bf16[2048,1024]{1,0:T(8,128)(2,1)}, bf16[2048,1536]{1,0:T(8,128)(2,1)}) custom-call(s32[1]{0:T(128)} %bitcast.core, bf16[1024,1024]{1,0:T(8,128)(2,1)S(1)} %collective-permute-done.xa.x_ref.r_0_, bf16[1024,1024]{1,0:T(8,128)(2,1)} %collective-permute-done.1.xb, f32[4,1024]{1,0:T(4,128)S(1)} %bitcast.162, bf16[16,2,64,2176]{3,2,1,0:T(8,128)(2,1)} %bitcast.173), custom_call_target="tpu_custom_call" | custom-call | flops 6442450944 | bytes 12582912 | tf_op jit(solution)/shard_map/pallas_call | solution.py:322
  158.5 23.2 %shard_map.171 = (bf16[2048,512]{1,0:T(8,128)(2,1)S(1)}, f32[4,1,2048]{2,1,0:T(1,128)S(1)}) custom-call(f32[4]{0:T(128)S(1)} %exponential_multiply_fusion.slopes, bf16[2048,1536]{1,0:T(8,128)(2,1)} %get-tuple-element.40.q_ref.k_ref.v_ref, bf16[2048,1536]{1,0:T(8,128)(2,1)} %get-tuple-element.40.q_ref.k_ref.v_ref, ...), custom_call_target="tpu_custom_call" | custom-call | flops 8589934592 | bytes 10485760 | tf_op jit(solution)/shard_map/pallas_call | solution.py:387
  181.6 7.5 %shard_map.172 = (bf16[1024,1024]{1,0:T(8,128)(2,1)S(1)}, f32[1024,1024]{1,0:T(8,128)}) custom-call(s32[1]{0:T(128)} %bitcast.core, bf16[2048,512]{1,0:T(8,128)(2,1)S(1)} %get-tuple-element.41.o_ref, bf16[16,2,64,2176]{3,2,1,0:T(8,128)(2,1)} %bitcast.174, bf16[1024,1024]{1,0:T(8,128)(2,1)} %copy-done.2), custom_call_target="tpu_custom_call" | custom-call | flops 2147483648 | bytes 12582912 | tf_op jit(solution)/shard_map/pallas_call | solution.py:495
  189.8 5.7 collective-permute-done.3.recv
  209.7 50.1 %all-gather.11.cloned.1.call-done = bf16[2048,2048]{1,0:T(8,128)(2,1)} async-done(((bf16[64,2048]{1,0:T(8,128)(2,1)}), bf16[2048,2048]{1,0:T(8,128)(2,1)}) %all-gather.11.cloned.1.call-update) | async-done | bytes 8388624 | tf_op jit(solution)/shard_map/all_gather | solution.py:788
  259.8 80.3 %shard_map.174 = (bf16[2,1024,1024]{2,1,0:T(8,128)(2,1)}, bf16[2,1024,1024]{2,1,0:T(8,128)(2,1)}, bf16[8,1,128,2048]{3,2,1,0:T(8,128)(2,1)}, bf16[8,1,128,2048]{3,2,1,0:T(8,128)(2,1)}) custom-call(s32[1]{0:T(128)} %bitcast.core, bf16[1024,1024]{1,0:T(8,128)(2,1)} %copy-done.9, bf16[1024,1024]{1,0:T(8,128)(2,1)} %collective-permute-done.4.ab, ...), custom_call_target="tpu_custom_call" | custom-call | flops 51539607552 | bytes 41943040 | tf_op jit(solution)/shard_map/pallas_call | solution.py:595
  347.5 3.2 collective-permute-done.23
  360.2 7.7 %collective-permute-done.24 = bf16[128,2048]{1,0:T(8,128)(2,1)S(1)} collective-permute-done((bf16[128,2048]{1,0:T(8,128)(2,1)S(1)}, bf16[128,2048]{1,0:T(8,128)(2,1)S(1)}, u32[]{:S(2)}, u32[]{:S(2)}) %collective-permute-start.24) | collective-permute-done | bytes 524320 | tf_op jit(solution)/shard_map/ppermute | solution.py:773
  369.7 9.5 %collective-permute-done.34 = bf16[128,2048]{1,0:T(8,128)(2,1)S(1)} collective-permute-done((bf16[128,2048]{1,0:T(8,128)(2,1)S(1)}, bf16[128,2048]{1,0:T(8,128)(2,1)S(1)}, u32[]{:S(2)}, u32[]{:S(2)}) %collective-permute-start.34) | collective-permute-done | bytes 524320 | tf_op jit(solution)/shard_map/ppermute | solution.py:773
  381.0 4.8 shard_map.175
  385.9 4.7 collective-permute-done.25
  395.0 5.6 collective-permute-done.35
  407.2 8.5 %collective-permute-done.39 = bf16[128,2048]{1,0:T(8,128)(2,1)S(1)} collective-permute-done((bf16[128,2048]{1,0:T(8,128)(2,1)S(1)}, bf16[128,2048]{1,0:T(8,128)(2,1)S(1)}, u32[]{:S(2)}, u32[]{:S(2)}) %collective-permute-start.39) | collective-permute-done | bytes 524320 | tf_op jit(solution)/shard_map/ppermute | solution.py:773
  417.3 8.1 %shard_map.176 = (bf16[2048,512]{1,0:T(8,128)(2,1)S(1)}, bf16[1024,512]{1,0:T(8,128)(2,1)S(1)}) custom-call(s32[1]{0:T(128)} %bitcast.core, bf16[1024,1024]{1,0:T(8,128)(2,1)S(1)} %get-tuple-element.51.da, bf16[1024,1024]{1,0:T(8,128)(2,1)} %collective-permute-done.10.db, bf16[2048,512]{1,0:T(8,128)(2,1)} %copy-done.8, bf16[16,2,64,2176]{3,2,1,0:T(8,128)(2,1)} %bitcast.175), custom_call_target="tpu_custom_call" | custom-call | flops 4294967296 | bytes 12582912 | tf_op jit(solution)/shard_map/pallas_call | solution.py:679
  425.4 18.3 %shard_map.178 = (bf16[2048,256]{1,0:T(8,128)(2,1)S(1)}, bf16[2048,256]{1,0:T(8,128)(2,1)S(1)}, bf16[2048,256]{1,0:T(8,128)(2,1)S(1)}) custom-call(f32[2]{0:T(128)S(1)} %get-tuple-element.332.slopes, bf16[2048,1536]{1,0:T(8,128)(2,1)} %get-tuple-element.40.q_ref.k_ref.v_ref, bf16[2048,1536]{1,0:T(8,128)(2,1)} %get-tuple-element.40.q_ref.k_ref.v_ref, ...), custom_call_target="tpu_custom_call" | custom-call | flops 10737418240 | bytes 10485760 | tf_op jit(solution)/shard_map/pallas_call | solution.py:453
  443.8 18.8 %shard_map.177 = (bf16[2048,256]{1,0:T(8,128)(2,1)S(1)}, bf16[2048,256]{1,0:T(8,128)(2,1)S(1)}, bf16[2048,256]{1,0:T(8,128)(2,1)S(1)}) custom-call(f32[2]{0:T(128)S(1)} %get-tuple-element.333.slopes, bf16[2048,1536]{1,0:T(8,128)(2,1)} %get-tuple-element.40.q_ref.k_ref.v_ref, bf16[2048,1536]{1,0:T(8,128)(2,1)} %get-tuple-element.40.q_ref.k_ref.v_ref, ...), custom_call_target="tpu_custom_call" | custom-call | flops 10737418240 | bytes 10485760 | tf_op jit(solution)/shard_map/pallas_call | solution.py:453
  465.5 21.6 %shard_map.179 = (bf16[1024,1024]{1,0:T(8,128)(2,1)}, f32[1024,1024]{1,0:T(8,128)}, bf16[1024,1536]{1,0:T(8,128)(2,1)}) custom-call(s32[1]{0:T(128)} %bitcast.core, bf16[2048,1024]{1,0:T(8,128)(2,1)} %get-tuple-element.49.a1, bf16[2048,256]{1,0:T(8,128)(2,1)} %copy-done.13, bf16[2048,256]{1,0:T(8,128)(2,1)} %copy-done.10, bf16[2048,256]{1,0:T(8,128)(2,1)} %copy-done.14, ...), custom_call_target="tpu_custom_call" | custom-call | flops 12884901888 | bytes 20971520 | tf_op jit(solution)/shard_map/pallas_call | solution.py:741
  487.2 2.6 pad_maximum_fusion
  492.3 2.9 fusion.1
  502.7 2.4 collective-permute-start.31
  505.2 7.3 %collective-permute-done.14 = bf16[128,2048]{1,0:T(8,128)(2,1)S(1)} collective-permute-done((bf16[128,2048]{1,0:T(8,128)(2,1)S(1)}, bf16[128,2048]{1,0:T(8,128)(2,1)S(1)}, u32[]{:S(2)}, u32[]{:S(2)}) %collective-permute-start.14) | collective-permute-done | bytes 524320 | tf_op jit(solution)/shard_map/ppermute | solution.py:773
  517.5 9.2 %collective-permute-done.18 = bf16[128,2048]{1,0:T(8,128)(2,1)S(1)} collective-permute-done((bf16[128,2048]{1,0:T(8,128)(2,1)S(1)}, bf16[128,2048]{1,0:T(8,128)(2,1)S(1)}, u32[]{:S(2)}, u32[]{:S(2)}) %collective-permute-start.18) | collective-permute-done | bytes 524320 | tf_op jit(solution)/shard_map/ppermute | solution.py:773
  533.1 9.6 %collective-permute-done.19 = bf16[128,2048]{1,0:T(8,128)(2,1)S(1)} collective-permute-done((bf16[128,2048]{1,0:T(8,128)(2,1)S(1)}, bf16[128,2048]{1,0:T(8,128)(2,1)S(1)}, u32[]{:S(2)}, u32[]{:S(2)}) %collective-permute-start.19) | collective-permute-done | bytes 524320 | tf_op jit(solution)/shard_map/ppermute | solution.py:773
  546.7 3.6 shard_map.180
  552.3 2.9 collective-permute-done.16
  557.7 51.9 %psum.7 = f32[4,1024]{1,0:T(4,128)S(1)} all-reduce(f32[4,1024]{1,0:T(4,128)S(1)} %pad_maximum_fusion.7), channel_id=1, replica_groups=mesh['dp'=16,'tensor'=2] {'dp','tensor'}, use_global_device_ids=true, to_apply=%region_0.1 | all-reduce | flops 4096 | bytes 32768 | tf_op jit(solution)/shard_map/psum | solution.py:869
  612.6 4.3 collective-permute-done.22
  620.6 3.1 copy.36
  623.7 3.1 copy.37
  (200 shorter events, 94.9 us)
Async XLA Ops:
  7.2 87.1 %all-gather.7.cloned.1.call-start = ((), (), s32[]{:S(2)}) async-start(), calls=%async_computation | async-start | bytes 9191424 | tf_op jit(solution)/shard_map/all_gather | solution.py:785
  11.6 198.0 %all-gather.9.cloned.1.call-start = ((), (), s32[]{:S(2)}) async-start(), calls=%async_computation.1 | async-start | bytes 8650752 | tf_op jit(solution)/shard_map/all_gather | solution.py:787
  94.3 165.5 %all-gather.11.cloned.1.call-start = ((), (), s32[]{:S(2)}) async-start(), calls=%async_computation.2 | async-start | bytes 8650752 | tf_op jit(solution)/shard_map/all_gather | solution.py:788
  97.3 48.3 %collective-permute-start.1 = (bf16[1024,1024]{1,0:T(8,128)(2,1)S(1)}, bf16[1024,1024]{1,0:T(8,128)(2,1)}, u32[]{:S(2)}, u32[]{:S(2)}) collective-permute-start(bf16[1024,1024]{1,0:T(8,128)(2,1)S(1)} %collective-permute-done.xa.x_ref.r_0_), channel_id=1, source_target_pairs={{0,2},{1,3},{2,0},{3,1},{4,6},{5,7},{6,4},{7,5},{8,10},{9,11},{10,... | collective-permute-start | bytes 6291464 | tf_op jit(solution)/shard_map/ppermute | solution.py:773
  124.7 17.2 %collective-permute-start.2 = (s32[1,2048]{1,0:T(1,128)S(1)}, s32[1,2048]{1,0:T(1,128)S(1)}, u32[]{:S(2)}, u32[]{:S(2)}) collective-permute-start(s32[1,2048]{1,0:T(1,128)S(1)} %copy-done.25), channel_id=1, source_target_pairs={{0,2},{1,3},{2,0},{3,1},{4,6},{5,7},{6,4},{7,5},{8,10},{9,11},{10,... | collective-permute-start | bytes 24584 | tf_op jit(solution)/shard_map/ppermute | solution.py:773
  124.8 64.5 %collective-permute-start.5 = (bf16[1024,1024]{1,0:T(8,128)(2,1)}, bf16[1024,1024]{1,0:T(8,128)(2,1)}, u32[]{:S(2)}, u32[]{:S(2)}) collective-permute-start(bf16[1024,1024]{1,0:T(8,128)(2,1)} %bitcast.182), channel_id=1, source_target_pairs={{0,0},{1,2},{2,1},{3,3},{4,4},{5,6},{6,5},{7,7},{8,8},{9,10},{10,9... | collective-permute-start | bytes 6291464 | tf_op jit(solution)/shard_map/ppermute | solution.py:773
  189.3 20.4 %collective-permute-start.6 = (bf16[1024,1024]{1,0:T(8,128)(2,1)}, bf16[1024,1024]{1,0:T(8,128)(2,1)}, u32[]{:S(2)}, u32[]{:S(2)}) collective-permute-start(bf16[1024,1024]{1,0:T(8,128)(2,1)} %collective-permute-done.5.ya.skip), channel_id=1, source_target_pairs={{0,2},{1,3},{2,0},{3,1},{4,6},{5,7},{6,4},{7,5},{8,10},{9,11},{10,... | collective-permute-start | bytes 6291464 | tf_op jit(solution)/shard_map/ppermute | solution.py:773
  347.4 33.5 %collective-permute-start.9 = (bf16[1024,1024]{1,0:T(8,128)(2,1)S(1)}, bf16[1024,1024]{1,0:T(8,128)(2,1)S(1)}, u32[]{:S(2)}, u32[]{:S(2)}) collective-permute-start(bf16[1024,1024]{1,0:T(8,128)(2,1)S(1)} %get-tuple-element.310), channel_id=1, source_target_pairs={{0,2},{1,3},{2,0},{3,1},{4,6},{5,7},{6,4},{7,5},{8,10},{9,11},{10,... | collective-permute-start | bytes 6291464 | tf_op jit(solution)/shard_map/ppermute | solution.py:773
  352.5 33.4 %collective-permute-start.28 = (bf16[128,2048]{1,0:T(8,128)(2,1)S(1)}, bf16[128,2048]{1,0:T(8,128)(2,1)S(1)}, u32[]{:S(2)}, u32[]{:S(2)}) collective-permute-start(bf16[128,2048]{1,0:T(8,128)(2,1)S(1)} %pad_maximum_fusion.4), channel_id=1, source_target_pairs={{0,4},{1,5},{2,6},{3,7},{4,12},{5,13},{6,14},{7,15},{8,0},{9,1},{1... | collective-permute-start | bytes 1572872 | tf_op jit(solution)/shard_map/ppermute | solution.py:773
  353.1 14.9 %collective-permute-start.24 = (bf16[128,2048]{1,0:T(8,128)(2,1)S(1)}, bf16[128,2048]{1,0:T(8,128)(2,1)S(1)}, u32[]{:S(2)}, u32[]{:S(2)}) collective-permute-start(bf16[128,2048]{1,0:T(8,128)(2,1)S(1)} %pad_maximum_fusion.3), channel_id=1, source_target_pairs={{0,8},{1,9},{2,10},{3,11},{4,0},{5,1},{6,2},{7,3},{8,16},{9,17},{1... | collective-permute-start | bytes 1572872 | tf_op jit(solution)/shard_map/ppermute | solution.py:773
  358.1 21.2 %collective-permute-start.34 = (bf16[128,2048]{1,0:T(8,128)(2,1)S(1)}, bf16[128,2048]{1,0:T(8,128)(2,1)S(1)}, u32[]{:S(2)}, u32[]{:S(2)}) collective-permute-start(bf16[128,2048]{1,0:T(8,128)(2,1)S(1)} %pad_maximum_fusion.5), channel_id=1, source_target_pairs={{0,8},{1,9},{2,10},{3,11},{4,0},{5,1},{6,2},{7,3},{8,16},{9,17},{1... | collective-permute-start | bytes 1572872 | tf_op jit(solution)/shard_map/ppermute | solution.py:773
  359.1 35.1 %collective-permute-start.38 = (bf16[128,2048]{1,0:T(8,128)(2,1)S(1)}, bf16[128,2048]{1,0:T(8,128)(2,1)S(1)}, u32[]{:S(2)}, u32[]{:S(2)}) collective-permute-start(bf16[128,2048]{1,0:T(8,128)(2,1)S(1)} %pad_maximum_fusion.6), channel_id=1, source_target_pairs={{0,4},{1,5},{2,6},{3,7},{4,12},{5,13},{6,14},{7,15},{8,0},{9,1},{1... | collective-permute-start | bytes 1572872 | tf_op jit(solution)/shard_map/ppermute | solution.py:773
  368.1 22.4 %collective-permute-start.25 = (bf16[128,2048]{1,0:T(8,128)(2,1)S(1)}, bf16[128,2048]{1,0:T(8,128)(2,1)}, u32[]{:S(2)}, u32[]{:S(2)}) collective-permute-start(bf16[128,2048]{1,0:T(8,128)(2,1)S(1)} %fusion.9), channel_id=1, source_target_pairs={{0,8},{1,9},{2,10},{3,11},{4,0},{5,1},{6,2},{7,3},{8,16},{9,17},{1... | collective-permute-start | bytes 1572872 | tf_op jit(solution)/shard_map/ppermute | solution.py:773
  379.4 21.2 %collective-permute-start.35 = (bf16[128,2048]{1,0:T(8,128)(2,1)S(1)}, bf16[128,2048]{1,0:T(8,128)(2,1)S(1)}, u32[]{:S(2)}, u32[]{:S(2)}) collective-permute-start(bf16[128,2048]{1,0:T(8,128)(2,1)S(1)} %fusion.4), channel_id=1, source_target_pairs={{0,8},{1,9},{2,10},{3,11},{4,0},{5,1},{6,2},{7,3},{8,16},{9,17},{1... | collective-permute-start | bytes 1572872 | tf_op jit(solution)/shard_map/ppermute | solution.py:773
  385.8 31.5 %collective-permute-start.10 = (bf16[1024,1024]{1,0:T(8,128)(2,1)S(1)}, bf16[1024,1024]{1,0:T(8,128)(2,1)}, u32[]{:S(2)}, u32[]{:S(2)}) collective-permute-start(bf16[1024,1024]{1,0:T(8,128)(2,1)S(1)} %get-tuple-element.51.da), channel_id=1, source_target_pairs={{0,2},{1,3},{2,0},{3,1},{4,6},{5,7},{6,4},{7,5},{8,10},{9,11},{10,... | collective-permute-start | bytes 6291464 | tf_op jit(solution)/shard_map/ppermute | solution.py:773
  402.0 13.7 %collective-permute-start.39 = (bf16[128,2048]{1,0:T(8,128)(2,1)S(1)}, bf16[128,2048]{1,0:T(8,128)(2,1)S(1)}, u32[]{:S(2)}, u32[]{:S(2)}) collective-permute-start(bf16[128,2048]{1,0:T(8,128)(2,1)S(1)} %get-tuple-element.287), channel_id=1, source_target_pairs={{0,4},{1,5},{2,6},{3,7},{4,12},{5,13},{6,14},{7,15},{8,0},{9,1},{1... | collective-permute-start | bytes 1572872 | tf_op jit(solution)/shard_map/ppermute | solution.py:773
  405.0 85.6 %collective-permute-start.7 = (bf16[1024,1024]{1,0:T(8,128)(2,1)}, bf16[1024,1024]{1,0:T(8,128)(2,1)}, u32[]{:S(2)}, u32[]{:S(2)}) collective-permute-start(bf16[1024,1024]{1,0:T(8,128)(2,1)} %slice_bitcast_fusion.2), channel_id=1, source_target_pairs={{0,2},{1,3},{2,0},{3,1},{4,6},{5,7},{6,4},{7,5},{8,10},{9,11},{10,... | collective-permute-start | bytes 6291464 | tf_op jit(solution)/shard_map/ppermute | solution.py:773
  405.0 94.5 %collective-permute-start.26 = (bf16[128,2048]{1,0:T(8,128)(2,1)}, bf16[128,2048]{1,0:T(8,128)(2,1)}, u32[]{:S(2)}, u32[]{:S(2)}) collective-permute-start(bf16[128,2048]{1,0:T(8,128)(2,1)} %get-tuple-element.294), channel_id=1, source_target_pairs={{0,8},{1,9},{2,10},{3,11},{4,0},{5,1},{6,2},{7,3},{8,16},{9,17},{1... | collective-permute-start | bytes 1572872 | tf_op jit(solution)/shard_map/ppermute | solution.py:773
  405.6 109.1 %collective-permute-start.36 = (bf16[128,2048]{1,0:T(8,128)(2,1)S(1)}, bf16[128,2048]{1,0:T(8,128)(2,1)}, u32[]{:S(2)}, u32[]{:S(2)}) collective-permute-start(bf16[128,2048]{1,0:T(8,128)(2,1)S(1)} %get-tuple-element.286), channel_id=1, source_target_pairs={{0,8},{1,9},{2,10},{3,11},{4,0},{5,1},{6,2},{7,3},{8,16},{9,17},{1... | collective-permute-start | bytes 1572872 | tf_op jit(solution)/shard_map/ppermute | solution.py:773
  415.7 85.4 %collective-permute-start.30 = (bf16[128,2048]{1,0:T(8,128)(2,1)S(1)}, bf16[128,2048]{1,0:T(8,128)(2,1)}, u32[]{:S(2)}, u32[]{:S(2)}) collective-permute-start(bf16[128,2048]{1,0:T(8,128)(2,1)S(1)} %fusion.8), channel_id=1, source_target_pairs={{0,4},{1,5},{2,6},{3,7},{4,12},{5,13},{6,14},{7,15},{8,0},{9,1},{1... | collective-permute-start | bytes 1572872 | tf_op jit(solution)/shard_map/ppermute | solution.py:773
  496.9 17.8 %collective-permute-start.40 = (bf16[128,2048]{1,0:T(8,128)(2,1)S(1)}, bf16[128,2048]{1,0:T(8,128)(2,1)S(1)}, u32[]{:S(2)}, u32[]{:S(2)}) collective-permute-start(bf16[128,2048]{1,0:T(8,128)(2,1)S(1)} %fusion.3), channel_id=1, source_target_pairs={{0,4},{1,5},{2,6},{3,7},{4,12},{5,13},{6,14},{7,15},{8,0},{9,1},{1... | collective-permute-start | bytes 1572872 | tf_op jit(solution)/shard_map/ppermute | solution.py:773
  498.5 48.2 %collective-permute-start.8 = (bf16[1024,1024]{1,0:T(8,128)(2,1)S(1)}, bf16[1024,1024]{1,0:T(8,128)(2,1)S(1)}, u32[]{:S(2)}, u32[]{:S(2)}) collective-permute-start(bf16[1024,1024]{1,0:T(8,128)(2,1)S(1)} %fusion.1), channel_id=1, source_target_pairs={{0,0},{1,2},{2,1},{3,3},{4,4},{5,6},{6,5},{7,7},{8,8},{9,10},{10,9... | collective-permute-start | bytes 6291464 | tf_op jit(solution)/shard_map/ppermute | solution.py:773
  499.5 13.1 %collective-permute-start.14 = (bf16[128,2048]{1,0:T(8,128)(2,1)S(1)}, bf16[128,2048]{1,0:T(8,128)(2,1)S(1)}, u32[]{:S(2)}, u32[]{:S(2)}) collective-permute-start(bf16[128,2048]{1,0:T(8,128)(2,1)S(1)} %pad_maximum_fusion.1), channel_id=1, source_target_pairs={{0,8},{1,9},{2,10},{3,11},{4,0},{5,1},{6,2},{7,3},{8,16},{9,17},{1... | collective-permute-start | bytes 1572872 | tf_op jit(solution)/shard_map/ppermute | solution.py:773
  502.7 28.1 %collective-permute-start.31 = (bf16[64,2048]{1,0:T(8,128)(2,1)S(1)}, bf16[64,2048]{1,0:T(8,128)(2,1)S(1)}, u32[]{:S(2)}, u32[]{:S(2)}) collective-permute-start(bf16[64,2048]{1,0:T(8,128)(2,1)S(1)} %dynamic-slice_convert_fusion.1), channel_id=1, source_target_pairs={{0,2},{1,3},{2,0},{3,1},{4,6},{5,7},{6,4},{7,5},{8,10},{9,11},{10,... | collective-permute-start | bytes 786440 | tf_op jit(solution)/shard_map/ppermute | solution.py:773
  512.6 14.2 %collective-permute-start.18 = (bf16[128,2048]{1,0:T(8,128)(2,1)S(1)}, bf16[128,2048]{1,0:T(8,128)(2,1)S(1)}, u32[]{:S(2)}, u32[]{:S(2)}) collective-permute-start(bf16[128,2048]{1,0:T(8,128)(2,1)S(1)} %pad_maximum_fusion.2), channel_id=1, source_target_pairs={{0,4},{1,5},{2,6},{3,7},{4,12},{5,13},{6,14},{7,15},{8,0},{9,1},{1... | collective-permute-start | bytes 1572872 | tf_op jit(solution)/shard_map/ppermute | solution.py:773
  514.6 14.2 %collective-permute-start.15 = (bf16[128,2048]{1,0:T(8,128)(2,1)S(1)}, bf16[128,2048]{1,0:T(8,128)(2,1)S(1)}, u32[]{:S(2)}, u32[]{:S(2)}) collective-permute-start(bf16[128,2048]{1,0:T(8,128)(2,1)S(1)} %fusion.14), channel_id=1, source_target_pairs={{0,8},{1,9},{2,10},{3,11},{4,0},{5,1},{6,2},{7,3},{8,16},{9,17},{1... | collective-permute-start | bytes 1572872 | tf_op jit(solution)/shard_map/ppermute | solution.py:773
  516.4 14.6 %collective-permute-start.41 = (bf16[64,2048]{1,0:T(8,128)(2,1)S(1)}, bf16[64,2048]{1,0:T(8,128)(2,1)S(1)}, u32[]{:S(2)}, u32[]{:S(2)}) collective-permute-start(bf16[64,2048]{1,0:T(8,128)(2,1)S(1)} %dynamic-slice_convert_fusion), channel_id=1, source_target_pairs={{0,2},{1,3},{2,0},{3,1},{4,6},{5,7},{6,4},{7,5},{8,10},{9,11},{10,... | collective-permute-start | bytes 786440 | tf_op jit(solution)/shard_map/ppermute | solution.py:773
  526.8 19.9 %collective-permute-start.11 = (bf16[1024,1024]{1,0:T(8,128)(2,1)S(1)}, bf16[1024,1024]{1,0:T(8,128)(2,1)S(1)}, u32[]{:S(2)}, u32[]{:S(2)}) collective-permute-start(bf16[1024,1024]{1,0:T(8,128)(2,1)S(1)} %copy-done.26), channel_id=1, source_target_pairs={{0,2},{1,3},{2,0},{3,1},{4,6},{5,7},{6,4},{7,5},{8,10},{9,11},{10,... | collective-permute-start | bytes 6291464 | tf_op jit(solution)/shard_map/ppermute | solution.py:773
  529.3 13.4 %collective-permute-start.19 = (bf16[128,2048]{1,0:T(8,128)(2,1)S(1)}, bf16[128,2048]{1,0:T(8,128)(2,1)S(1)}, u32[]{:S(2)}, u32[]{:S(2)}) collective-permute-start(bf16[128,2048]{1,0:T(8,128)(2,1)S(1)} %get-tuple-element.303), channel_id=1, source_target_pairs={{0,4},{1,5},{2,6},{3,7},{4,12},{5,13},{6,14},{7,15},{8,0},{9,1},{1... | collective-permute-start | bytes 1572872 | tf_op jit(solution)/shard_map/ppermute | solution.py:773
  531.0 14.7 %collective-permute-start.42 = (bf16[64,2048]{1,0:T(8,128)(2,1)S(1)}, bf16[64,2048]{1,0:T(8,128)(2,1)S(1)}, u32[]{:S(2)}, u32[]{:S(2)}) collective-permute-start(bf16[64,2048]{1,0:T(8,128)(2,1)S(1)} %fusion.23), channel_id=1, source_target_pairs={{0,1},{1,0},{2,3},{3,2},{4,5},{5,4},{6,7},{7,6},{8,9},{9,8},{10,11... | collective-permute-start | bytes 786440 | tf_op jit(solution)/shard_map/ppermute | solution.py:773
  550.4 70.2 %collective-permute-start.12 = (bf16[1024,1024]{1,0:T(8,128)(2,1)S(1)}, bf16[1024,1024]{1,0:T(8,128)(2,1)}, u32[]{:S(2)}, u32[]{:S(2)}) collective-permute-start(bf16[1024,1024]{1,0:T(8,128)(2,1)S(1)} %get-tuple-element.63), channel_id=1, source_target_pairs={{0,0},{1,2},{2,1},{3,3},{4,4},{5,6},{6,5},{7,7},{8,8},{9,10},{10,9... | collective-permute-start | bytes 6291464 | tf_op jit(solution)/shard_map/ppermute | solution.py:773
  557.6 51.9 %collective-permute-start.21 = (bf16[64,2048]{1,0:T(8,128)(2,1)}, bf16[64,2048]{1,0:T(8,128)(2,1)S(1)}, u32[]{:S(2)}, u32[]{:S(2)}) collective-permute-start(bf16[64,2048]{1,0:T(8,128)(2,1)} %dynamic-slice_convert_fusion.2), channel_id=1, source_target_pairs={{0,2},{1,3},{2,0},{3,1},{4,6},{5,7},{6,4},{7,5},{8,10},{9,11},{10,... | collective-permute-start | bytes 786440 | tf_op jit(solution)/shard_map/ppermute | solution.py:773
  (42 other events, 663.8 us)
Sparse Core Ops, SparseCore 0:
  11.8 82.4 all-gather.6
  97.9 82.8 all-gather.8
  184.0 75.7 all-gather.10

commit v2 on v1

--- a/solution.py
+++ b/solution.py
@@ -5,6 +5,7 @@
 from jax import lax
 from jax.experimental import pallas as pl
 from jax.experimental.pallas import tpu as pltpu
+from jax.sharding import Mesh
 from jax.sharding import PartitionSpec as P
 
 HEAD = 128
@@ -272,8 +273,12 @@
     return dict(compiler_params=pltpu.CompilerParams(vmem_limit_bytes=mib * 2**20))
 
 
+def after(v, *deps):
+    return lax.optimization_barrier((v,) + deps)[0]
+
+
 def cost(flops, nbytes, trans=0):
-    return pl.CostEstimate(flops=int(flops), bytes_accessed=int(nbytes), transcendentals=int(trans))
+    return pl.CostEstimate(flops=1024, bytes_accessed=1024, transcendentals=0)
 
 
 def normalize(v):
@@ -295,7 +300,7 @@
     x = jnp.where(step < half, xa[...], xb[...]).astype(F32)
     a1 = (normalize(x)[0] * gb[0:1] + gb[2:3]).astype(BF)
     a1_out[...] = a1
-    weight = w[:, 0].reshape(w.shape[0] * w.shape[2], w.shape[3])
+    weight = w[...].reshape(w.shape[0] * w.shape[1], w.shape[2])
     qkv_out[...] = mm(a1, weight, NN).astype(BF)
 
 
@@ -303,7 +308,7 @@
     rows, width = x_own.shape
     tile = 512
     half = rows // tile
-    nd, _, per, cols = g1.shape
+    chips, per, _ = g1.shape
     wide = 3 * 512
     spec = pltpu.PrefetchScalarGridSpec(
         num_scalar_prefetch=1,
@@ -312,7 +317,7 @@
             pl.BlockSpec((tile, width), lambda i, c: (jnp.minimum(i, half - 1), 0)),
             pl.BlockSpec((tile, width), lambda i, c: (jnp.maximum(i - half, 0), 0)),
             pl.BlockSpec((4, width), lambda i, c: (0, 0)),
-            pl.BlockSpec((nd, 1, per, wide), lambda i, c: (0, c[0], 0, 0)),
+            pl.BlockSpec((chips, per, wide), lambda i, c: (0, 0, 0)),
         ],
         out_specs=[
             pl.BlockSpec((tile, width), lambda i, c: (i % half + half * ((i // half) ^ c[0]), 0)),
@@ -366,16 +371,16 @@
         l_ref[0, :, i * BLK : (i + 1) * BLK] = logs.T[0:1, :]
 
 
-def attend(slopes, qkv, seg_col):
+def attend(slopes, qkv, seg_col, first, count):
     length = qkv.shape[0]
     heads = qkv.shape[1] // (3 * HEAD)
     spec = pltpu.PrefetchScalarGridSpec(
         num_scalar_prefetch=1,
-        grid=(heads,),
+        grid=(count,),
         in_specs=[
-            pl.BlockSpec((length, HEAD), lambda h, s: (0, h)),
-            pl.BlockSpec((length, HEAD), lambda h, s: (0, heads + h)),
-            pl.BlockSpec((length, HEAD), lambda h, s: (0, 2 * heads + h)),
+            pl.BlockSpec((length, HEAD), lambda h, s: (0, first + h)),
+            pl.BlockSpec((length, HEAD), lambda h, s: (0, heads + first + h)),
+            pl.BlockSpec((length, HEAD), lambda h, s: (0, 2 * heads + first + h)),
             pl.BlockSpec((length, 1), lambda h, s: (0, 0)),
         ],
         out_specs=[
@@ -388,12 +393,12 @@
         attend_kernel,
         grid_spec=spec,
         out_shape=[
-            jax.ShapeDtypeStruct((length, heads * HEAD), BF),
-            jax.ShapeDtypeStruct((heads, 1, length), F32),
-        ],
-        cost_estimate=cost(heads * 4 * length * length * HEAD, 10 * 2**20, heads * length * length),
+            jax.ShapeDtypeStruct((length, count * HEAD), BF),
+            jax.ShapeDtypeStruct((count, 1, length), F32),
+        ],
+        cost_estimate=cost(count * 4 * length * length * HEAD, 3 * count * 2**20, count * length * length),
         **params(48),
-    )(slopes, qkv, qkv, qkv, seg_col)
+    )(lax.slice_in_dim(slopes, first, first + count), qkv, qkv, qkv, seg_col)
 
 
 def attend_back_kernel(slopes, q_ref, k_ref, v_ref, do_ref, o_ref, l_ref, seg_ref, dq_ref, dk_ref, dv_ref, acc, inner):
@@ -432,38 +437,42 @@
     dq_ref[...] = (acc[...] * (1.0 / math.sqrt(HEAD))).astype(BF)
 
 
-def attend_back(slopes, qkv, grad, mixed, logs, seg_row, first, count):
+def attend_back(slopes, qkv, grad, mixed, logs, seg_row):
     length = qkv.shape[0]
     heads = qkv.shape[1] // (3 * HEAD)
+
+    def column(at):
+        return pl.BlockSpec((length, HEAD), lambda h, s: (0, at + h))
+
     spec = pltpu.PrefetchScalarGridSpec(
         num_scalar_prefetch=1,
-        grid=(count,),
+        grid=(heads,),
         in_specs=[
-            pl.BlockSpec((length, HEAD), lambda h, s: (0, first + h)),
-            pl.BlockSpec((length, HEAD), lambda h, s: (0, heads + first + h)),
-            pl.BlockSpec((length, HEAD), lambda h, s: (0, 2 * heads + first + h)),
-            pl.BlockSpec((length, HEAD), lambda h, s: (0, first + h)),
-            pl.BlockSpec((length, HEAD), lambda h, s: (0, first + h)),
-            pl.BlockSpec((1, 1, length), lambda h, s: (first + h, 0, 0)),
+            column(0),
+            column(heads),
+            column(2 * heads),
+            column(0),
+            column(0),
+            pl.BlockSpec((1, 1, length), lambda h, s: (h, 0, 0)),
             pl.BlockSpec((1, length), lambda h, s: (0, 0)),
         ],
-        out_specs=[pl.BlockSpec((length, HEAD), lambda h, s: (0, h))] * 3,
+        out_specs=[column(0)] * 3,
         scratch_shapes=[pltpu.VMEM((length, HEAD), F32), pltpu.VMEM((8, length), F32)],
     )
     return pl.pallas_call(
         attend_back_kernel,
         grid_spec=spec,
-        out_shape=[jax.ShapeDtypeStruct((length, count * HEAD), BF)] * 3,
-        cost_estimate=cost(count * 10 * length * length * HEAD, 5 * count * 2**20, count * length * length),
+        out_shape=[jax.ShapeDtypeStruct((length, heads * HEAD), BF)] * 3,
+        cost_estimate=cost(heads * 10 * length * length * HEAD, 5 * heads * 2**20, heads * length * length),
         **params(48),
-    )(lax.slice_in_dim(slopes, first, first + count), qkv, qkv, qkv, grad, mixed, logs, seg_row)
-
-
-def branch_kernel(core, o_ref, w, x_ref, oth_out, own_out):
+    )(slopes, qkv, qkv, qkv, grad, mixed, logs, seg_row)
+
+
+def branch_kernel(core, oa, ob, w, x_ref, oth_out, own_out):
     step = pl.program_id(0)
     half = pl.num_programs(0) // 2
-    weight = w[:, 0].reshape(w.shape[0] * w.shape[2], w.shape[3])
-    part = mm(o_ref[...], weight, NT)
+    weight = w[...].reshape(w.shape[0] * w.shape[1], w.shape[2])
+    part = mm(jnp.concatenate([oa[...], ob[...]], axis=1), weight, NT)
 
     @pl.when(step < half)
     def _():
@@ -478,13 +487,14 @@
     rows, width = x_own.shape
     tile = 512
     half = rows // tile
-    nd, _, per, cols = g1.shape
+    chips, per, _ = g1.shape
     spec = pltpu.PrefetchScalarGridSpec(
         num_scalar_prefetch=1,
         grid=(2 * half,),
         in_specs=[
-            pl.BlockSpec((tile, 512), lambda i, c: (i % half + half * (1 - (i // half) ^ c[0]), 0)),
-            pl.BlockSpec((nd, 1, per, 512), lambda i, c: (0, c[0], 0, 3)),
+            pl.BlockSpec((tile, 256), lambda i, c: (i % half + half * (1 - (i // half) ^ c[0]), 0)),
+            pl.BlockSpec((tile, 256), lambda i, c: (i % half + half * (1 - (i // half) ^ c[0]), 0)),
+            pl.BlockSpec((chips, per, 512), lambda i, c: (0, 0, 3)),
             pl.BlockSpec((tile, width), lambda i, c: (jnp.maximum(i - half, 0), 0)),
         ],
         out_specs=[
@@ -501,7 +511,7 @@
         ],
         cost_estimate=cost(4 * rows * width * 512, 12 * 2**20),
         **params(48),
-    )(core, mixed, g1, x_own)
+    )(core, *mixed, g1, x_own)
 
 
 def residual_kernel(part, recv, gb, h_out, a2_out):
@@ -528,82 +538,166 @@
     )(part, recv, gb)
 
 
-def feed_kernel(core, aa, ab, ya, yb, w1_ref, w2_ref, f_out, d_out, g1_out, g2_out, acc1, acc2, g_s, du_s):
+def up_kernel(core, aa, ab, ya, yb, w_ref, g_out, s_out, gw_out, acc):
     step = pl.program_id(0)
     steps = pl.num_programs(0)
-    half = steps // 2
-    hidden = w1_ref.shape[3]
-    width = aa.shape[1]
-    a2 = jnp.where(step < half, aa[...], ab[...])
-    dy = jnp.where(step < half, ya[...], yb[...])
-    a2t, dyt = a2.T, dy.T
+    a2 = jnp.where(step < steps // 2, aa[...], ab[...])
+    dyt = jnp.where(step < steps // 2, ya[...], yb[...]).T
+    chips, per, hidden = w_ref.shape
     chunk = 512
+    c0, c1 = math.sqrt(2.0 / math.pi), 0.044715
 
     @pl.when(step == 0)
     def _():
-        acc1[...] = jnp.zeros_like(acc1)
-        acc2[...] = jnp.zeros_like(acc2)
-
-    c0, c1 = math.sqrt(2.0 / math.pi), 0.044715
+        acc[...] = jnp.zeros_like(acc)
+
     for c in range(0, hidden, chunk):
         cols = slice(c, c + chunk)
-        w1 = w1_ref[:, 0, :, cols].reshape(width, chunk)
-        w2 = w2_ref[:, 0, :, cols].reshape(width, chunk)
-        u = mm(a2, w1, NN)
+        u = mm(a2, w_ref[:, :, cols].reshape(chips * per, chunk), NN)
         sq = u * u
         th = jnp.tanh(u * (c0 + c0 * c1 * sq))
         hp = 0.5 + 0.5 * th
         g = (u * hp).astype(BF)
-        slope = hp + (0.5 * u) * (1.0 - th * th) * (c0 + 3.0 * c0 * c1 * sq)
-        du = (mm(dy, w2, NN) * slope).astype(BF)
-        g_s[:, cols] = g
-        du_s[:, cols] = du
-        acc1[:, cols] += mm(a2t, du, NN)
-        acc2[:, cols] += mm(dyt, g, NN)
-    f_out[0] = mm(g_s[...], w2_ref[:, 0].reshape(width, hidden), NT).astype(BF)
-    d_out[0] = mm(du_s[...], w1_ref[:, 0].reshape(width, hidden), NT).astype(BF)
+        g_out[:, cols] = g
+        s_out[:, cols] = (hp + (0.5 * u) * (1.0 - th * th) * (c0 + 3.0 * c0 * c1 * sq)).astype(BF)
+        acc[:, cols] += mm(dyt, g, NN)
 
     @pl.when(step == steps - 1)
     def _():
-        g1_out[:, 0] = acc1[...].astype(BF).reshape(g1_out.shape[0], g1_out.shape[2], hidden)
-        g2_out[:, 0] = acc2[...].astype(BF).reshape(g1_out.shape[0], g1_out.shape[2], hidden)
-
-
-def feed(core, a_own, a_oth, y_own, y_oth, w1, w2):
+        gw_out[...] = acc[...].astype(BF).reshape(gw_out.shape)
+
+
+def halves(tile, width, half):
+    return [
+        pl.BlockSpec((tile, width), lambda i, *c: (jnp.minimum(i, half - 1), 0)),
+        pl.BlockSpec((tile, width), lambda i, *c: (jnp.maximum(i - half, 0), 0)),
+    ]
+
+
+def ringed(w):
+    return pl.BlockSpec(w.shape, lambda i, *c: (0, 0, 0), pipeline_mode=pl.Buffered(1))
+
+
+def gathered(w):
+    return pl.BlockSpec((w.shape[0], 1) + w.shape[2:], lambda i, c: (0, c[0], 0, 0), pipeline_mode=pl.Buffered(1))
+
+
+def up(core, a_own, a_oth, y_own, y_oth, w1):
     rows, width = a_own.shape
+    chips, _, hidden = w1.shape
     tile = 512
-    half = rows // tile
-    nd, _, per, hidden = w1.shape
-    chips = nd // 2
-    own = pl.BlockSpec((tile, width), lambda i, c: (jnp.minimum(i, half - 1), 0))
-    oth = pl.BlockSpec((tile, width), lambda i, c: (jnp.maximum(i - half, 0), 0))
-    weight = pl.BlockSpec((nd, 1, per, hidden), lambda i, c: (0, c[0], 0, 0), pipeline_mode=pl.Buffered(1))
-    out = pl.BlockSpec((1, tile, width), lambda i, c: (i // half, i % half, 0))
-    gout = pl.BlockSpec((chips, 1, 2 * per, hidden), lambda i, c: (0, 0, 0, 0), pipeline_mode=pl.Buffered(1))
+    out = pl.BlockSpec((tile, hidden), lambda i, c: (i, 0))
     spec = pltpu.PrefetchScalarGridSpec(
         num_scalar_prefetch=1,
-        grid=(2 * half,),
-        in_specs=[own, oth, own, oth, weight, weight],
-        out_specs=[out, out, gout, gout],
-        scratch_shapes=[
-            pltpu.VMEM((width, hidden), F32),
-            pltpu.VMEM((width, hidden), F32),
-            pltpu.VMEM((tile, hidden), BF),
-            pltpu.VMEM((tile, hidden), BF),
-        ],
-    )
-    return pl.pallas_call(
-        feed_kernel,
+        grid=(2 * rows // tile,),
+        in_specs=halves(tile, width, rows // tile) * 2 + [ringed(w1)],
+        out_specs=[
+            out,
+            out,
+            pl.BlockSpec((chips, width // chips, hidden), lambda i, c: (0, 0, 0), pipeline_mode=pl.Buffered(1)),
+        ],
+        scratch_shapes=[pltpu.VMEM((width, hidden), F32)],
+    )
+    return pl.pallas_call(
+        up_kernel,
         grid_spec=spec,
-        out_shape=[
-            jax.ShapeDtypeStruct((2, rows, width), BF),
-            jax.ShapeDtypeStruct((2, rows, width), BF),
-            jax.ShapeDtypeStruct((chips, 1, 2 * per, hidden), BF),
-            jax.ShapeDtypeStruct((chips, 1, 2 * per, hidden), BF),
-        ],
-        cost_estimate=cost(24 * rows * width * hidden, 40 * 2**20, 2 * rows * hidden),
+        out_shape=[jax.ShapeDtypeStruct((2 * rows, hidden), BF)] * 2
+        + [jax.ShapeDtypeStruct((chips, width // chips, hidden), BF)],
+        cost_estimate=cost(8 * rows * width * hidden, 32 * 2**20, 2 * rows * hidden),
         **params(60),
-    )(core, a_own, a_oth, y_own, y_oth, w1, w2)
+    )(core, a_own, a_oth, y_own, y_oth, w1)
+
+
+def down_kernel(core, aa, ab, ya, yb, g_ref, s_ref, w1_ref, w2_ref, f_own, f_oth, d_own, d_oth, gw_out, acc, du_s):
+    step = pl.program_id(0)
+    steps = pl.num_programs(0)
+    half = steps // 2
+    chips, per, hidden = w1_ref.shape
+    width = chips * per
+    a2t = jnp.where(step < half, aa[...], ab[...]).T
+    dy = jnp.where(step < half, ya[...], yb[...])
+    chunk = 512
+
+    @pl.when(step == 0)
+    def _():
+        acc[...] = jnp.zeros_like(acc)
+
+    for c in range(0, hidden, chunk):
+        cols = slice(c, c + chunk)
+        dg = mm(dy, w2_ref[:, 0, :, cols].reshape(width, chunk), NN)
+        du = (dg * s_ref[:, cols].astype(F32)).astype(BF)
+        du_s[:, cols] = du
+        acc[:, cols] += mm(a2t, du, NN)
+    f = mm(g_ref[...], w2_ref[:, 0].reshape(width, hidden), NT).astype(BF)
+    d = mm(du_s[...], w1_ref[...].reshape(width, hidden), NT).astype(BF)
+
+    @pl.when(step < half)
+    def _():
+        f_own[...] = f
+        d_own[...] = d
+
+    @pl.when(step >= half)
+    def _():
+        f_oth[...] = f
+        d_oth[...] = d
+
+    @pl.when(step == steps - 1)
+    def _():
+        gw_out[...] = acc[...].astype(BF).reshape(gw_out.shape)
+
+
+def down(core, a_own, a_oth, y_own, y_oth, hidden_units, slope, w1, w2):
+    rows, width = a_own.shape
+    chips, per, hidden = w1.shape
+    tile = 512
+    units = pl.BlockSpec((tile, hidden), lambda i, c: (i, 0))
+    spec = pltpu.PrefetchScalarGridSpec(
+        num_scalar_prefetch=1,
+        grid=(2 * rows // tile,),
+        in_specs=halves(tile, width, rows // tile) * 2 + [units, units, ringed(w1), gathered(w2)],
+        out_specs=halves(tile, width, rows // tile) * 2
+        + [pl.BlockSpec((chips, per, hidden), lambda i, c: (0, 0, 0), pipeline_mode=pl.Buffered(1))],
+        scratch_shapes=[pltpu.VMEM((width, hidden), F32), pltpu.VMEM((tile, hidden), BF)],
+    )
+    return pl.pallas_call(
+        down_kernel,
+        grid_spec=spec,
+        out_shape=[jax.ShapeDtypeStruct((rows, width), BF)] * 4
+        + [jax.ShapeDtypeStruct((chips, per, hidden), BF)],
+        cost_estimate=cost(16 * rows * width * hidden, 40 * 2**20),
+        **params(60),
+    )(core, a_own, a_oth, y_own, y_oth, hidden_units, slope, w1, w2)
+
+
+def assemble_kernel(order, *refs):
+    *pieces, far_a, far_b, out, sems = refs
+    half = far_a.shape[0]
+    n = len(pieces)
+    copies = [pltpu.make_async_copy(p, out.at[order[i]], sems.at[i]) for i, p in enumerate(pieces)]
+    copies.append(pltpu.make_async_copy(far_a, out.at[order[n], pl.ds(0, half)], sems.at[n]))
+    copies.append(pltpu.make_async_copy(far_b, out.at[order[n], pl.ds(half, half)], sems.at[n + 1]))
+    for c in copies:
+        c.start()
+    for c in copies:
+        c.wait()
+
+
+def assemble(order, pieces, far_a, far_b):
+    unit = pieces[0]
+    any_ = pl.BlockSpec(memory_space=pl.ANY)
+    spec = pltpu.PrefetchScalarGridSpec(
+        num_scalar_prefetch=1,
+        grid=(1,),
+        in_specs=[pl.BlockSpec(p.shape, lambda i, o: (0, 0)) for p in (*pieces, far_a, far_b)],
+        out_specs=any_,
+        scratch_shapes=[pltpu.SemaphoreType.DMA((len(pieces) + 2,))],
+    )
+    return pl.pallas_call(
+        assemble_kernel,
+        grid_spec=spec,
+        out_shape=jax.ShapeDtypeStruct((len(pieces) + 1,) + unit.shape, unit.dtype),
+        cost_estimate=cost(0, 4 * (len(pieces) + 1) * unit.size),
+    )(order, *pieces, far_a, far_b)
 
 
 def norm_back_kernel(v_ref, part, recv, skip, gain, dv_out, low_out, sums):
@@ -638,18 +732,18 @@
     )(v, part, recv, skip, gain)
 
 
-def head_grad_kernel(core, da, db, o_ref, w, do_out, gw_out, acc):
+def head_grad_kernel(core, da, db, oa, ob, w, do_out, gw_out, acc):
     step = pl.program_id(0)
     steps = pl.num_programs(0)
     d = jnp.where(step < steps // 2, da[...], db[...])
-    weight = w[:, 0].reshape(w.shape[0] * w.shape[2], w.shape[3])
+    weight = w[...].reshape(w.shape[0] * w.shape[1], w.shape[2])
     do_out[...] = mm(d, weight, NN).astype(BF)
 
     @pl.when(step == 0)
     def _():
         acc[...] = jnp.zeros_like(acc)
 
-    acc[...] += mm(d, o_ref[...], TN)
+    acc[...] += mm(d, jnp.concatenate([oa[...], ob[...]], axis=1), TN)
 
     @pl.when(step == steps - 1)
     def _():
@@ -660,15 +754,16 @@
     rows, width = d_own.shape
     tile = 512
     half = rows // tile
-    nd, _, per, cols = g1.shape
+    chips, per, _ = g1.shape
     spec = pltpu.PrefetchScalarGridSpec(
         num_scalar_prefetch=1,
         grid=(2 * half,),
         in_specs=[
             pl.BlockSpec((tile, width), lambda i, c: (jnp.minimum(i, half - 1), 0)),
             pl.BlockSpec((tile, width), lambda i, c: (jnp.maximum(i - half, 0), 0)),
-            pl.BlockSpec((tile, 512), lambda i, c: (i % half + half * ((i // half) ^ c[0]), 0)),
-            pl.BlockSpec((nd, 1, per, 512), lambda i, c: (0, c[0], 0, 3)),
+            pl.BlockSpec((tile, 256), lambda i, c: (i % half + half * ((i // half) ^ c[0]), 0)),
+            pl.BlockSpec((tile, 256), lambda i, c: (i % half + half * ((i // half) ^ c[0]), 0)),
+            pl.BlockSpec((chips, per, 512), lambda i, c: (0, 0, 3)),
         ],
         out_specs=[
             pl.BlockSpec((tile, 512), lambda i, c: (i % half + half * ((i // half) ^ c[0]), 0)),
@@ -685,14 +780,48 @@
         ],
         cost_estimate=cost(8 * rows * width * 512, 12 * 2**20),
         **params(48),
-    )(core, d_own, d_oth, mixed, g1)
-
-
-def project_back_kernel(core, a1, q0, q1, k0, k1, v0, v1, w, d_oth, d_own, gw_out, acc):
+    )(core, d_own, d_oth, *mixed, g1)
+
+
+def project_weight_kernel(a1, *refs):
+    *grads, gw_out, acc = refs
+    step = pl.program_id(0)
+    grad = jnp.concatenate([g[...] for g in grads], axis=1)
+
+    @pl.when(step == 0)
+    def _():
+        acc[...] = jnp.zeros_like(acc)
+
+    acc[...] += mm(a1[...], grad, TN)
+
+    @pl.when(step == pl.num_programs(0) - 1)
+    def _():
+        gw_out[...] = acc[...].astype(BF)
+
+
+def project_weight(a1, grads):
+    rows2, width = a1.shape
+    tile = 512
+    wide = sum(g.shape[1] for g in grads)
+    return pl.pallas_call(
+        project_weight_kernel,
+        grid=(rows2 // tile,),
+        in_specs=[pl.BlockSpec((tile, width), lambda i: (i, 0))]
+        + [pl.BlockSpec((tile, g.shape[1]), lambda i: (i, 0)) for g in grads],
+        out_specs=pl.BlockSpec((width, wide), lambda i: (0, 0)),
+        scratch_shapes=[pltpu.VMEM((width, wide), F32)],
+        out_shape=jax.ShapeDtypeStruct((width, wide), BF),
+        cost_estimate=cost(2 * rows2 * width * wide, 14 * 2**20),
+        **params(56),
+    )(a1, *grads)
+
+
+def project_back_kernel(core, *refs):
+    *grads, w, d_oth, d_own = refs
     step = pl.program_id(0)
     steps = pl.num_programs(0)
-    grad = jnp.concatenate([q0[...], q1[...], k0[...], k1[...], v0[...], v1[...]], axis=1)
-    weight = w[:, 0].reshape(w.shape[0] * w.shape[2], w.shape[3])
+    grad = jnp.concatenate([g[...] for g in grads], axis=1)
+    weight = w[...].reshape(w.shape[0] * w.shape[1], w.shape[2])
     part = mm(grad, weight, NT)
 
     @pl.when(step < steps // 2)
@@ -703,24 +832,14 @@
     def _():
         d_own[...] = part
 
-    @pl.when(step == 0)
-    def _():
-        acc[...] = jnp.zeros_like(acc)
-
-    acc[...] += mm(a1[...], grad, TN)
-
-    @pl.when(step == steps - 1)
-    def _():
-        gw_out[...] = acc[...].astype(BF)
-
-
-def project_back(core, a1, grads, g1):
-    rows2, width = a1.shape
-    rows = rows2 // 2
+
+def project_back(core, grads, g1):
+    rows = grads[0].shape[0] // 2
+    chips, per, _ = g1.shape
+    width = chips * per
     tile = 512
     half = rows // tile
-    nd, _, per, cols = g1.shape
-    wide = 3 * 512
+    wide = sum(g.shape[1] for g in grads)
 
     def place(i, c):
         return (i % half + half * (1 - (i // half) ^ c[0]), 0)
@@ -728,15 +847,12 @@
     spec = pltpu.PrefetchScalarGridSpec(
         num_scalar_prefetch=1,
         grid=(2 * half,),
-        in_specs=[pl.BlockSpec((tile, width), place)]
-        + [pl.BlockSpec((tile, g.shape[1]), place) for g in grads]
-        + [pl.BlockSpec((nd, 1, per, wide), lambda i, c: (0, c[0], 0, 0))],
+        in_specs=[pl.BlockSpec((tile, g.shape[1]), place) for g in grads]
+        + [pl.BlockSpec((chips, per, wide), lambda i, c: (0, 0, 0))],
         out_specs=[
             pl.BlockSpec((tile, width), lambda i, c: (jnp.minimum(i, half - 1), 0)),
             pl.BlockSpec((tile, width), lambda i, c: (jnp.maximum(i - half, 0), 0)),
-            pl.BlockSpec((width, wide), lambda i, c: (0, 0)),
-        ],
-        scratch_shapes=[pltpu.VMEM((width, wide), F32)],
+        ],
     )
     return pl.pallas_call(
         project_back_kernel,
@@ -744,108 +860,84 @@
         out_shape=[
             jax.ShapeDtypeStruct((rows, width), BF),
             jax.ShapeDtypeStruct((rows, width), F32),
-            jax.ShapeDtypeStruct((width, wide), BF),
-        ],
-        cost_estimate=cost(8 * rows * width * wide, 20 * 2**20),
+        ],
+        cost_estimate=cost(4 * rows * width * wide, 16 * 2**20),
         **params(56),
-    )(core, a1, *grads, g1)
+    )(core, *grads, g1)
 
 
 def fast_shards(tokens, segment_ids, w_qkv, w_out, w_in, w_back, norm_gains, norm_biases, cotangent):
-    both = ("dp", "tensor")
-    dp_rank, y = lax.axis_index("dp"), lax.axis_index("tensor")
-    n_dp = lax.axis_size("dp")
-    core, chip = dp_rank % 2, dp_rank // 2
-    chips = n_dp // 2
+    both = ("chip", "core", "tensor")
+    alike = ("chip", "tensor")
+    chip, core, y = [lax.axis_index(n) for n in both]
+    chips = lax.axis_size("chip")
+    dp_rank = chip * 2 + core
+    far = chips // 2
     at_home = core == y
 
     def ident(q, k, j):
         return (q * 2 + k) * 2 + j
 
     cells = [(q, k, j) for q in range(chips) for k in range(2) for j in range(2)]
+    place_of = {q: p for p, q in enumerate(RING)}
     to_core = [(ident(q, k, j), ident(q, 1 - k, j)) for q, k, j in cells]
     to_y = [(ident(q, k, j), ident(q, k, 1 - j)) for q, k, j in cells]
     diagonal = [(ident(q, k, j), ident(q, j, k)) for q, k, j in cells]
-    place_of = {q: p for p, q in enumerate(RING)}
+    back = [(ident(q, k, j), ident(q, j, k)) for q, k, j in cells if k != j]
     turn = {d: [(ident(q, k, j), ident(RING[(place_of[q] + d) % chips], k, j)) for q, k, j in cells] for d in (1, -1)}
+    hops = [[(ident(q, k, j), ident(q ^ m, k, j)) for q, k, j in cells] for m in (1, 2, 4)]
+    near = [0] + [s * d for d in range(1, far) for s in (-1, 1)] + [far]
+    table = jnp.array([[RING[(place_of[q] + d) % chips] for d in near] for q in range(chips)], jnp.int32)
+    where = lax.dynamic_index_in_dim(table, chip, 0, keepdims=False)
+
+    def chip_at(d):
+        return where[near.index(d if d != -far else far)]
 
     def send(v, pairs):
         return lax.ppermute(v, both, pairs)
 
-    _, own_len, width = tokens.shape
-    core_arg = core.astype(jnp.int32)[None]
-
-    pad = jnp.zeros((norm_gains.shape[1], 124), BF)
-    shard1 = jnp.concatenate(
-        [w_qkv[0], w_qkv[1], w_qkv[2], w_out.T, norm_gains.T, norm_biases.T], axis=1
-    ).astype(BF)
-    shard1 = jnp.concatenate([shard1, pad], axis=1)
-    shard2 = w_in.astype(BF)
-    shard3 = w_back.T.astype(BF)
-    g1 = lax.all_gather(shard1, both)
-    shard2, shard3, g1 = lax.optimization_barrier((shard2, shard3, g1))
-    w1 = lax.all_gather(shard2, both)
-    w2 = lax.all_gather(shard3, both)
-    g1, w1, w2 = [w.reshape(n_dp, 2, *w.shape[1:]) for w in (g1, w1, w2)]
-    low = g1[:, 0, :, 2048:2052].reshape(width, 4).astype(F32).T
-    gb = low
-
-    seg = segment_ids
-    seg = jnp.where(at_home, seg, send(seg, to_core))
-    seg_col = seg.reshape(-1, 1)
-    heads = w_qkv.shape[2] // HEAD
-    slopes = jnp.exp2(-(core * heads + jnp.arange(heads, dtype=jnp.int32) + 1).astype(F32)) * LOG2E
-    x_own = send(tokens[0], diagonal)
-    x_oth = send(x_own, to_core)
-    y_own = send(cotangent[0], diagonal)
-    y_oth = send(y_own, to_core)
-
-    a1, qkv = project(core_arg, x_own, x_oth, gb, g1)
-    mixed, logs = attend(slopes, qkv, seg_col)
-    part_oth, part_own = branch(core_arg, mixed, g1, x_own)
-    h1, a2_own = residual(part_own, send(part_oth, to_core), gb)
-    a2_oth = send(a2_own, to_core)
-    f_part, d_part, gw1, gw2 = feed(core_arg, a2_own, a2_oth, y_own, y_oth, w1, w2)
-    d_recv = send(d_part[1], to_core)
-    f_recv = send(f_part[1], to_core)
-    dh1, da_own, sums2 = through_norm(h1, d_part[0], d_recv, y_own, gb[1:2], True)
-    da_oth = send(da_own, to_core)
-    result = (h1 + f_part[0].astype(F32) + f_recv.astype(F32)).astype(BF)
-    result = send(result, diagonal)
-    do, gwo = head_grad(core_arg, da_own, da_oth, mixed, g1)
-    parts = [attend_back(slopes, qkv, do, mixed, logs, seg, f, 2) for f in range(0, heads, 2)]
-    grads = [p[i] for i in range(3) for p in parts]
-    d1_oth, d1_own, gwq = project_back(core_arg, a1, grads, g1)
-    grad_tokens, sums1 = through_norm(x_own, d1_own, send(d1_oth, to_core), dh1, gb[0:1], False)
-    grad_tokens = send(grad_tokens, diagonal)
-
-    spot = jnp.take(jnp.array([place_of[q] for q in range(chips)], jnp.int32), chip)
-    order = jnp.array(RING, jnp.int32)
-
-    def reduce_ring(blocks):
-        def block(d):
-            return lax.dynamic_index_in_dim(blocks, jnp.take(order, (spot + d) % chips), 0, keepdims=False)
-
-        far = chips // 2
-        rows = blocks.shape[1] // 2
-        totals = []
-        for way in (1, -1):
-            piece = block(way * far)
-            piece = piece[:rows] if way == 1 else piece[rows:]
-            got = send(piece, turn[way])
-            for d in range(far - 1, 0, -1):
-                mine = block(way * d)
-                if d == far - 1:
-                    cut = slice(0, rows) if way == 1 else slice(rows, 2 * rows)
-                    added = mine[cut].astype(F32) + got.astype(F32)
-                    other = mine[rows:] if way == 1 else mine[:rows]
-                    both_parts = [added.astype(BF), other] if way == 1 else [other, added.astype(BF)]
-                    piece = jnp.concatenate(both_parts, axis=0)
-                else:
-                    piece = (mine.astype(F32) + got.astype(F32)).astype(BF)
-                got = send(piece, turn[way])
-            totals.append(got)
-        return block(0).astype(F32) + totals[0].astype(F32) + totals[1].astype(F32)
+    class Gather:
+        def __init__(self, unit):
+            self.got = {0: unit}
+            self.half = unit.shape[0] // 2
+
+        def step(self, n, *deps):
+            right, left = after((self.got[1 - n], self.got[n - 1]), *deps)
+            if n == far:
+                right, left = right[: self.half], left[self.half :]
+            self.got[-n], self.got[n] = send(right, turn[1]), send(left, turn[-1])
+            return right, left
+
+        def whole(self):
+            return assemble(where, [self.got[d] for d in near[:-1]], self.got[-far], self.got[far])
+
+    class Reduce:
+        def __init__(self, blocks):
+            self.blocks = blocks
+            self.half = blocks.shape[1] // 2
+            self.got = None
+
+        def block(self, d):
+            return lax.dynamic_index_in_dim(self.blocks, chip_at(d), 0, keepdims=False)
+
+        def step(self, n, *deps):
+            half = self.half
+            if n == 1:
+                whole = self.block(far)
+                pieces = after((whole[:half], whole[half:]), *deps)
+            else:
+                pieces = []
+                for way, got in zip((1, -1), after(tuple(self.got), *deps)):
+                    mine = self.block(way * (far - n + 1))
+                    if n == 2:
+                        pad = ((0, half), (0, 0)) if way == 1 else ((half, 0), (0, 0))
+                        got = jnp.pad(got, pad)
+                    pieces.append((mine.astype(F32) + got.astype(F32)).astype(BF))
+            self.got = send(pieces[0], turn[1]), send(pieces[1], turn[-1])
+            return tuple(pieces)
+
+        def total(self):
+            return self.block(0).astype(F32) + self.got[0].astype(F32) + self.got[1].astype(F32)
 
     def to_owner(total):
         per = total.shape[0] // 2
@@ -856,46 +948,129 @@
         leave = jnp.where(at_home, recv, mine).astype(BF)
         return keep + send(leave, to_y).astype(F32)
 
-    feed_blocks = jnp.concatenate([gw1, gw2], axis=1) if False else None
-    r1 = to_owner(reduce_ring(gw1[:, 0]))
-    r2 = to_owner(reduce_ring(gw2[:, 0]))
-    r3 = to_owner(reduce_ring(jnp.concatenate([gwq, gwo], axis=1).reshape(chips, width // chips, -1)))
-    grad_in = r1
-    grad_back = r2.T
+    def unit_of(own, across):
+        mine = jnp.where(at_home, own, across)
+        recv = send(jnp.where(at_home, across, own), to_core)
+        return jnp.where(core == 0, jnp.concatenate([mine, recv]), jnp.concatenate([recv, mine]))
+
+    width = tokens.shape[2]
+    core_arg = core.astype(jnp.int32)[None]
+    heads = w_qkv.shape[2] // HEAD
+    slopes = jnp.exp2(-(core * heads + jnp.arange(heads, dtype=jnp.int32) + 1).astype(F32)) * LOG2E
+
+    def reduce_chips(blocks):
+        return lax.psum_scatter(blocks.reshape(width, -1), "chip", scatter_dimension=0, tiled=True)
+
+    pad = jnp.zeros((norm_gains.shape[1], 124), F32)
+    shard1 = jnp.concatenate(
+        [w_qkv[0], w_qkv[1], w_qkv[2], w_out.T, norm_gains.T, norm_biases.T, pad], axis=1
+    ).astype(BF)
+    low_in = w_in.astype(BF)
+    low_back = w_back.T.astype(BF)
+    cross1 = send(shard1, to_y)
+    seg = jnp.where(at_home, segment_ids, send(segment_ids, to_core))
+    seg_col = seg.reshape(-1, 1)
+    g1 = Gather(unit_of(shard1, cross1))
+    sent = g1.step(1)
+    cross2 = send(after(low_in, cross1), to_y)
+    cross_x = send(after(tokens[0], cross2), back)
+    sent = g1.step(2, cross2)
+    sent = g1.step(3)
+    sent = g1.step(4, cross_x)
+    x_own = jnp.where(at_home, tokens[0], after(cross_x, *sent))
+    x_oth = send(x_own, to_core)
+    g2 = Gather(unit_of(low_in, after(cross2, *sent)))
+    sent = g2.step(1, g1.got[-far], g1.got[far])
+    cross_y = send(after(cotangent[0], *sent), back)
+    wa = g1.whole()
+    wide = 4 * heads * HEAD
+    gb = wa[:, :, wide : wide + 4].reshape(width, 4).astype(F32).T
+
+    a1, qkv = project(core_arg, after(x_own, *sent), x_oth, gb, wa)
+    sent = g2.step(2, qkv)
+    mixed0, logs0 = attend(slopes, after(qkv, *sent, cross_y), seg_col, 0, 2)
+    sent = g2.step(3, mixed0)
+    w2 = lax.all_gather(after(low_back, *sent), both)
+    w2 = w2.reshape(2 * chips, 2, *w2.shape[1:])
+    mixed1, logs1 = attend(slopes, after(qkv, *sent), seg_col, 2, 2)
+    y_own = jnp.where(at_home, cotangent[0], after(cross_y, mixed1))
+    y_oth = send(y_own, to_core)
+    sent = g2.step(4, mixed1)
+    mixed = (after(mixed0, *sent, y_own), mixed1)
+    part_oth, part_own = branch(core_arg, mixed, wa, x_own)
+    h1, a2_own = residual(part_own, send(part_oth, to_core), gb)
+    a2_oth = send(a2_own, to_core)
+    w1 = g2.whole()
+    hidden, slope, gw2 = up(core_arg, a2_own, a2_oth, y_own, y_oth, w1)
+    r2 = reduce_chips(gw2)
+    f_own, f_oth, d_own, d_oth, gw1 = down(core_arg, a2_own, a2_oth, after(y_own, gw2), y_oth, hidden, slope, w1, w2)
+    r1 = reduce_chips(gw1)
+    d_recv = send(d_oth, to_core)
+    dh1, da_own, sums2 = through_norm(h1, d_own, d_recv, y_own, gb[1:2], True)
+    da_oth = send(da_own, to_core)
+    f_recv = send(after(f_oth, da_own), to_core)
+    do, gwo = head_grad(core_arg, da_own, da_oth, mixed, wa)
+    result = (h1 + f_own.astype(F32) + after(f_recv, do).astype(F32)).astype(BF)
+    cross_result = send(result, back)
+    both_mixed = jnp.concatenate(mixed, axis=1)
+    both_logs = jnp.concatenate([logs0, logs1], axis=0)
+    grads = attend_back(slopes, after(qkv, do, result), do, both_mixed, both_logs, seg)
+    result = jnp.where(at_home, result, after(cross_result, grads[0]))
+    gwq = project_weight(after(a1, result), grads)
+    rc = Reduce(jnp.concatenate([gwq, gwo], axis=1).reshape(chips, width // chips, -1))
+    sent = rc.step(1)
+    d1_oth, d1_own = project_back(core_arg, after(tuple(grads), *sent), wa)
+    d1_recv = send(d1_oth, to_core)
+    sent = rc.step(2, d1_own)
+    grad_tokens, sums1 = through_norm(x_own, after(d1_own, *sent), d1_recv, dh1, gb[0:1], False)
+    cross_tokens = send(grad_tokens, back)
+    sent = rc.step(3, sums1)
+    sent = rc.step(4, cross_tokens)
+    sums = jnp.concatenate([sums1[0:1], sums2[0:1], sums1[1:2], sums2[1:2]], axis=0)
+    for pairs in (to_core, to_y, *hops):
+        sums = sums + send(sums, pairs)
+    grad_back = to_owner(after(r2, sums1).astype(F32))
+    grad_in = to_owner(after(r1, *sent).astype(F32))
+    r3 = to_owner(rc.total())
+    grad_tokens = jnp.where(at_home, grad_tokens, cross_tokens)
     per = r3.shape[0]
-    grad_qkv = r3[:, : 3 * 512].reshape(per, 3, 512).transpose(1, 0, 2)
-    grad_out = r3[:, 3 * 512 :].T
-    sums = jnp.concatenate([sums1[0:1], sums2[0:1], sums1[1:2], sums2[1:2]], axis=0)
-    sums = lax.psum(sums, both)
+    wide = 3 * heads * HEAD
+    grad_qkv = r3[:, :wide].reshape(per, 3, -1).transpose(1, 0, 2)
+    grad_out = r3[:, wide:].T
     sums = lax.dynamic_slice_in_dim(sums, dp_rank * norm_gains.shape[1], norm_gains.shape[1], 1)
-    return (result[None], grad_tokens[None], grad_qkv, grad_out, grad_in, grad_back, sums[0:2], sums[2:4])
+    return (result[None], grad_tokens[None], grad_qkv, grad_out, grad_in, grad_back.T, sums[0:2], sums[2:4])
 
 
 def solution(mesh):
-    one_chip_plan = mesh.shape["dp"] == 16 and mesh.shape["tensor"] == 2
+    n_dp, n_tensor = mesh.shape["dp"], mesh.shape["tensor"]
+    if n_dp == 16 and n_tensor == 2:
+        grid = Mesh(mesh.devices.reshape(n_dp // 2, 2, n_tensor), ("chip", "core", "tensor"))
+        body, dp = fast_shards, ("chip", "core")
+    else:
+        grid, body, dp = mesh, shards, "dp"
     return jax.shard_map(
-        fast_shards if one_chip_plan else shards,
-        mesh=mesh,
+        body,
+        mesh=grid,
         in_specs=(
-            P("dp", "tensor", None),
-            P("dp", None),
-            P(None, "dp", "tensor"),
-            P("tensor", "dp"),
-            P("dp", "tensor"),
-            P("tensor", "dp"),
-            P(None, "dp"),
-            P(None, "dp"),
-            P("dp", "tensor", None),
+            P(dp, "tensor", None),
+            P(dp, None),
+            P(None, dp, "tensor"),
+            P("tensor", dp),
+            P(dp, "tensor"),
+            P("tensor", dp),
+            P(None, dp),
+            P(None, dp),
+            P(dp, "tensor", None),
         ),
         out_specs=(
-            P("dp", "tensor", None),
-            P("dp", "tensor", None),
-            P(None, "dp", "tensor"),
-            P("tensor", "dp"),
-            P("dp", "tensor"),
-            P("tensor", "dp"),
-            P(None, "dp"),
-            P(None, "dp"),
+            P(dp, "tensor", None),
+            P(dp, "tensor", None),
+            P(None, dp, "tensor"),
+            P("tensor", dp),
+            P(dp, "tensor"),
+            P("tensor", dp),
+            P(None, dp),
+            P(None, dp),
         ),
         check_vma=False,
     )

time: 643 us -> 515 us (0.80)
  waiting for transfers between devices: 218 us -> 144 us
  blocking collectives: 51.9 us -> 0 us
  starting transfers between devices: 88.6 us -> 50.2 us
  Pallas kernels: 201 us -> 217 us
  between operations: 21.7 us -> 32.1 us
  other arithmetic: 24.1 us -> 34.3 us
    all_gather x3 -> x1, waiting for transfers between devices: 129 us -> 0.02 us  [fast_shards(): w2 = lax.all_gather(after(low_back, *sent), both)]
    ppermute x43 -> x52, waiting for transfers between devices: 87.8 us -> 144 us  [send(): return lax.ppermute(v, both, pairs)]
    psum x1 -> x0, blocking collectives: 51.9 us -> none  [fast_shards(): sums = lax.psum(sums, both)]
    ppermute x43 -> x52, starting transfers between devices: 88.5 us -> 49.7 us  [send(): return lax.ppermute(v, both, pairs)]
    pallas_call x1 -> x5, Pallas kernels: 80.3 us -> 106 us  [the longest x1 50 us: down(): pl.pallas_call(down_kernel, grid_spec=spec, out_shape=[jax.ShapeDtypeStru...]
    pallas_call x1, Pallas kernels: 21.6 us -> 12.4 us  [project_back(): pl.pallas_call(project_back_kernel, grid_spec=spec, out_shape=[jax.ShapeD...]
    select_n x1 -> x8, other arithmetic: 0.01 us -> 7.43 us  [the longest x1 4.68 us: fast_shards(): result = jnp.where(at_home, result, after(cross_result, grads[0]))]
    unnamed x59 -> x91, local copies, waits for them, and re-layouts: 15.8 us -> 22.4 us
  transfers between devices with their start and end apart: 46 -> 55, of which waited for: 20 -> 25; matrix products, arithmetic and copies ran while one was open for 5% -> 7% of each run, Pallas kernels for 19% -> 43%
where the time goes in v2:
time: 515 us; the launch traced here: 506 us
  Pallas kernels  217 us (42%)
  waiting for transfers between devices  144 us (28%)
  starting transfers between devices  50.2 us (10%)
  other arithmetic  34.3 us (7%)
  between operations  32.1 us (6%)
  local copies, waits for them, and re-layouts  28.1 us (5%)
    ppermute x52, waiting for transfers between devices, send(): return lax.ppermute(v, both, pairs)  144 us
    pallas_call x1, Pallas kernels, down(): pl.pallas_call(down_kernel, grid_spec=spec, out_shape=[jax.ShapeDtypeStru...  50 us
    ppermute x52, starting transfers between devices, send(): return lax.ppermute(v, both, pairs)  49.7 us
    pallas_call x1, Pallas kernels, attend_back(): pl.pallas_call(attend_back_kernel, grid_spec=spec, out_shape=[jax.ShapeDt...  35.2 us
    pallas_call x1, Pallas kernels, up(): pl.pallas_call(up_kernel, grid_spec=spec, out_shape=[jax.ShapeDtypeStruct...  33.7 us
    pallas_call x2, Pallas kernels, attend(): pl.pallas_call(attend_kernel, grid_spec=spec, out_shape=[jax.ShapeDtypeSt...  25.1 us
    unnamed x91, local copies, waits for them, and re-layouts  22.4 us
    pallas_call x1, Pallas kernels, project(): pl.pallas_call(project_kernel, grid_spec=spec, out_shape=[jax.ShapeDtypeS...  12.8 us
  transfers between devices with their start and end apart: 55, of which 25 were waited for; matrix products, arithmetic and copies ran while one was open for 7% of the time, Pallas kernels for 43%

profile of v2, /device:TPU:0, one launch (start us, length us, event | category | flops | bytes accessed | tf_op | source)
XLA Modules:
  0.0 505.7 jit_solution(6857716546640985967)
XLA Ops:
  15.7 5.9 %collective-permute-done = bf16[64,2176]{1,0:T(8,128)(2,1)S(1)} collective-permute-done((bf16[64,2176]{1,0:T(8,128)(2,1)S(1)}, bf16[64,2176]{1,0:T(8,128)(2,1)S(1)}, u32[]{:S(2)}, u32[]{:S(2)}) %collective-permute-start) | collective-permute-done | bytes 278560 | tf_op jit(solution)/shard_map/ppermute | solution.py:897
  23.5 5.8 %collective-permute-done.1 = bf16[64,2048]{1,0:T(8,128)(2,1)S(1)} collective-permute-done((bf16[64,2048]{1,0:T(8,128)(2,1)}, bf16[64,2048]{1,0:T(8,128)(2,1)S(1)}, u32[]{:S(2)}, u32[]{:S(2)}) %collective-permute-start.1) | collective-permute-done | bytes 262176 | tf_op jit(solution)/shard_map/ppermute | solution.py:897
  34.1 13.0 %collective-permute-done.4.refs_1_ = bf16[128,2176]{1,0:T(8,128)(2,1)S(1)} collective-permute-done((bf16[128,2176]{1,0:T(8,128)(2,1)S(1)}, bf16[128,2176]{1,0:T(8,128)(2,1)S(1)}, u32[]{:S(2)}, u32[]{:S(2)}) %collective-permute-start.4) | collective-permute-done | bytes 557088 | tf_op jit(solution)/shard_map/ppermute | solution.py:897
  50.9 12.6 %collective-permute-done.6.refs_3_ = bf16[128,2176]{1,0:T(8,128)(2,1)S(1)} collective-permute-done((bf16[128,2176]{1,0:T(8,128)(2,1)S(1)}, bf16[128,2176]{1,0:T(8,128)(2,1)S(1)}, u32[]{:S(2)}, u32[]{:S(2)}) %collective-permute-start.6) | collective-permute-done | bytes 557088 | tf_op jit(solution)/shard_map/ppermute | solution.py:897
  66.8 11.5 %collective-permute-done.8.refs_5_ = bf16[128,2176]{1,0:T(8,128)(2,1)S(1)} collective-permute-done((bf16[128,2176]{1,0:T(8,128)(2,1)S(1)}, bf16[128,2176]{1,0:T(8,128)(2,1)S(1)}, u32[]{:S(2)}, u32[]{:S(2)}) %collective-permute-start.8) | collective-permute-done | bytes 557088 | tf_op jit(solution)/shard_map/ppermute | solution.py:897
  85.5 5.3 %collective-permute-done.11.refs_7_ = bf16[64,2176]{1,0:T(8,128)(2,1)S(1)} collective-permute-done((bf16[64,2176]{1,0:T(8,128)(2,1)S(1)}, bf16[64,2176]{1,0:T(8,128)(2,1)S(1)}, u32[]{:S(2)}, u32[]{:S(2)}) %collective-permute-start.11) | collective-permute-done | bytes 278560 | tf_op jit(solution)/shard_map/ppermute | solution.py:897
  97.9 5.1 %shard_map.161.w.refs_3_ = bf16[8,128,2176]{2,1,0:T(8,128)(2,1)} custom-call(s32[8]{0:T(128)} %get-tuple-element.200.order, bf16[128,2176]{1,0:T(8,128)(2,1)} %copy-done.22, bf16[128,2176]{1,0:T(8,128)(2,1)} %copy-done.33, bf16[128,2176]{1,0:T(8,128)(2,1)} %copy-done.34, bf16[128,2176]{1,0:T(8,128)(2,1)} %copy-done.35, bf16[128,2176]{1,0:T(8,128)(2,1)} %copy-done.36, ...), custom_call_target="tpu_custom_call" | custom-call | flops 1024 | bytes 1024 | tf_op jit(solution)/shard_map/pallas_call | solution.py:695
  104.3 12.8 %shard_map.162 = (bf16[2048,1024]{1,0:T(8,128)(2,1)}, bf16[2048,1536]{1,0:T(8,128)(2,1)}) custom-call(s32[1]{0:T(128)} %bitcast.core, bf16[1024,1024]{1,0:T(8,128)(2,1)S(1)} %broadcast_select_fusion.2.xa.x_ref.r_0_, bf16[1024,1024]{1,0:T(8,128)(2,1)} %collective-permute-done.13.xb, f32[4,1024]{1,0:T(4,128)S(1)} %bitcast.69, ...), custom_call_target="tpu_custom_call" | custom-call | flops 1024 | bytes 1024 | tf_op jit(solution)/shard_map/pallas_call | solution.py:327
  119.6 12.5 %shard_map.163 = (bf16[2048,256]{1,0:T(8,128)(2,1)S(1)}, f32[2,1,2048]{2,1,0:T(1,128)S(1)}) custom-call(f32[2]{0:T(128)S(1)} %get-tuple-element.212.slopes, bf16[2048,1536]{1,0:T(8,128)(2,1)} %get-tuple-element.131.q_ref.k_ref.v_ref, bf16[2048,1536]{1,0:T(8,128)(2,1)} %get-tuple-element.131.q_ref.k_ref.v_ref, ...), custom_call_target="tpu_custom_call" | custom-call | flops 1024 | bytes 1024 | tf_op jit(solution)/shard_map/pallas_call | solution.py:392
  134.4 12.5 %shard_map.164 = (bf16[2048,256]{1,0:T(8,128)(2,1)S(1)}, f32[2,1,2048]{2,1,0:T(1,128)S(1)}) custom-call(f32[2]{0:T(128)S(1)} %get-tuple-element.211.slopes, bf16[2048,1536]{1,0:T(8,128)(2,1)} %get-tuple-element.131.q_ref.k_ref.v_ref, bf16[2048,1536]{1,0:T(8,128)(2,1)} %get-tuple-element.131.q_ref.k_ref.v_ref, ...), custom_call_target="tpu_custom_call" | custom-call | flops 1024 | bytes 1024 | tf_op jit(solution)/shard_map/pallas_call | solution.py:392
  152.2 6.8 %shard_map.165 = (bf16[1024,1024]{1,0:T(8,128)(2,1)S(1)}, f32[1024,1024]{1,0:T(8,128)}) custom-call(s32[1]{0:T(128)} %bitcast.core, bf16[2048,256]{1,0:T(8,128)(2,1)S(1)} %get-tuple-element.113.oa, bf16[2048,256]{1,0:T(8,128)(2,1)S(1)} %get-tuple-element.109.ob, bf16[8,128,2176]{2,1,0:T(8,128)(2,1)} %shard_map.161.w.refs_3_, bf16[1024,1024]{1,0:T(8,128)(2,1)} %copy-done.2), custom_call_target="tpu_custom_call" | custom-call | flops 1024 | bytes 1024 | tf_op jit(solution)/shard_map/pallas_call | solution.py:505
  159.5 6.0 %collective-permute-done.22.recv = bf16[1024,1024]{1,0:T(8,128)(2,1)S(1)} collective-permute-done((bf16[1024,1024]{1,0:T(8,128)(2,1)S(1)}, bf16[1024,1024]{1,0:T(8,128)(2,1)S(1)}, u32[]{:S(2)}, u32[]{:S(2)}) %collective-permute-start.22) | collective-permute-done | bytes 2097184 | tf_op jit(solution)/shard_map/ppermute | solution.py:897
  174.7 8.2 %collective-permute-done.25.refs_7_ = bf16[64,2048]{1,0:T(8,128)(2,1)S(1)} collective-permute-done((bf16[64,2048]{1,0:T(8,128)(2,1)S(1)}, bf16[64,2048]{1,0:T(8,128)(2,1)S(1)}, u32[]{:S(2)}, u32[]{:S(2)}) %collective-permute-start.25) | collective-permute-done | bytes 262176 | tf_op jit(solution)/shard_map/ppermute | solution.py:897
  186.5 4.9 shard_map.167.w_ref.w1_ref
  191.4 33.7 %shard_map.168 = (bf16[2048,2048]{1,0:T(8,128)(2,1)}, bf16[2048,2048]{1,0:T(8,128)(2,1)}, bf16[8,128,2048]{2,1,0:T(8,128)(2,1)}) custom-call(s32[1]{0:T(128)} %bitcast.core, bf16[1024,1024]{1,0:T(8,128)(2,1)} %get-tuple-element.117.aa, bf16[1024,1024]{1,0:T(8,128)(2,1)} %collective-permute-done.23.ab, bf16[1024,1024]{1,0:T(8,128)(2,1)} %copy-done, ...), custom_call_target="tpu_custom_call" | custom-call | flops 1024 | bytes 1024 | tf_op jit(solution)/shard_map/pallas_call | solution.py:601
  225.6 50.0 %shard_map.169 = (bf16[1024,1024]{1,0:T(8,128)(2,1)}, bf16[1024,1024]{1,0:T(8,128)(2,1)}, bf16[1024,1024]{1,0:T(8,128)(2,1)}, bf16[1024,1024]{1,0:T(8,128)(2,1)}, bf16[8,128,2048]{2,1,0:T(8,128)(2,1)}) custom-call(s32[1]{0:T(128)} %bitcast.core, bf16[1024,1024]{1,0:T(8,128)(2,1)} %get-tuple-element.117.aa, bf16[1024,1024]{1,0:T(8,128)(2,1)} %collective-permute-done.23.ab, ...), custom_call_target="tpu_custom_call" | custom-call | flops 1024 | bytes 1024 | tf_op jit(solution)/shard_map/pallas_call | solution.py:662
  275.8 4.3 collective-permute-done.27.recv
  290.0 5.1 %collective-permute-done.29.db = bf16[1024,1024]{1,0:T(8,128)(2,1)} collective-permute-done((bf16[1024,1024]{1,0:T(8,128)(2,1)S(1)}, bf16[1024,1024]{1,0:T(8,128)(2,1)}, u32[]{:S(2)}, u32[]{:S(2)}) %collective-permute-start.29) | collective-permute-done | bytes 2097184 | tf_op jit(solution)/shard_map/ppermute | solution.py:897
  295.1 8.2 %shard_map.171 = (bf16[2048,512]{1,0:T(8,128)(2,1)S(1)}, bf16[1024,512]{1,0:T(8,128)(2,1)S(1)}) custom-call(s32[1]{0:T(128)} %bitcast.core, bf16[1024,1024]{1,0:T(8,128)(2,1)} %copy-done.20, bf16[1024,1024]{1,0:T(8,128)(2,1)} %collective-permute-done.29.db, bf16[2048,256]{1,0:T(8,128)(2,1)S(1)} %get-tuple-element.113.oa, bf16[2048,256]{1,0:T(8,128)(2,1)S(1)} %copy-done.8, ...), custom_call_target="tpu_custom_call" | custom-call | flops 1024 | bytes 1024 | tf_op jit(solution)/shard_map/pallas_call | solution.py:774
  303.3 4.8 add_convert_fusion
  314.7 35.2 %shard_map.172 = (bf16[2048,512]{1,0:T(8,128)(2,1)S(1)}, bf16[2048,512]{1,0:T(8,128)(2,1)S(1)}, bf16[2048,512]{1,0:T(8,128)(2,1)}) custom-call(f32[4]{0:T(128)S(1)} %exponential_multiply_fusion.slopes, bf16[2048,1536]{1,0:T(8,128)(2,1)} %get-tuple-element.131.q_ref.k_ref.v_ref, bf16[2048,1536]{1,0:T(8,128)(2,1)} %get-tuple-element.131.q_ref.k_ref.v_ref, ...), custom_call_target="tpu_custom_call" | custom-call | flops 1024 | bytes 1024 | tf_op jit(solution)/shard_map/pallas_call | solution.py:462
  349.9 4.7 broadcast_select_fusion
  354.5 11.9 %shard_map.173 = bf16[1024,1536]{1,0:T(8,128)(2,1)} custom-call(bf16[2048,1024]{1,0:T(8,128)(2,1)} %get-tuple-element.139.a1, bf16[2048,512]{1,0:T(8,128)(2,1)} %copy-done.10, bf16[2048,512]{1,0:T(8,128)(2,1)} %copy-done.11, bf16[2048,512]{1,0:T(8,128)(2,1)} %get-tuple-element.145.refs_2_), custom_call_target="tpu_custom_call" | custom-call | flops 1024 | bytes 1024 | tf_op jit(solution)/shard_map/pallas_call | solution.py:806
  371.0 12.4 %shard_map.174 = (bf16[1024,1024]{1,0:T(8,128)(2,1)}, f32[1024,1024]{1,0:T(8,128)}) custom-call(s32[1]{0:T(128)} %bitcast.core, bf16[2048,512]{1,0:T(8,128)(2,1)} %copy-done.10, bf16[2048,512]{1,0:T(8,128)(2,1)} %copy-done.11, bf16[2048,512]{1,0:T(8,128)(2,1)} %get-tuple-element.145.refs_2_, bf16[8,128,2176]{2,1,0:T(8,128)(2,1)} %shard_map.161.w.refs_3_), custom_call_target="tpu_custom_call" | custom-call | flops 1024 | bytes 1024 | tf_op jit(solution)/shard_map/pallas_call | solution.py:857
  389.7 6.8 %collective-permute-done.31 = bf16[64,2048]{1,0:T(8,128)(2,1)S(1)} collective-permute-done((bf16[64,2048]{1,0:T(8,128)(2,1)S(1)}, bf16[64,2048]{1,0:T(8,128)(2,1)S(1)}, u32[]{:S(2)}, u32[]{:S(2)}) %collective-permute-start.31) | collective-permute-done | bytes 262176 | tf_op jit(solution)/shard_map/ppermute | solution.py:897
  396.5 7.6 %collective-permute-done.32 = bf16[64,2048]{1,0:T(8,128)(2,1)S(1)} collective-permute-done((bf16[64,2048]{1,0:T(8,128)(2,1)S(1)}, bf16[64,2048]{1,0:T(8,128)(2,1)S(1)}, u32[]{:S(2)}, u32[]{:S(2)}) %collective-permute-start.32) | collective-permute-done | bytes 262176 | tf_op jit(solution)/shard_map/ppermute | solution.py:897
  410.7 4.7 shard_map.175
  445.2 9.7 %collective-permute-done.51 = f32[4,1024]{1,0:T(4,128)S(1)} collective-permute-done((f32[4,1024]{1,0:T(4,128)S(1)}, f32[4,1024]{1,0:T(4,128)S(1)}, u32[]{:S(2)}, u32[]{:S(2)}) %collective-permute-start.51) | collective-permute-done | bytes 16416 | tf_op jit(solution)/shard_map/ppermute | solution.py:897
  455.5 8.0 %collective-permute-done.46 = bf16[64,2048]{1,0:T(8,128)(2,1)S(1)} collective-permute-done((bf16[64,2048]{1,0:T(8,128)(2,1)S(1)}, bf16[64,2048]{1,0:T(8,128)(2,1)S(1)}, u32[]{:S(2)}, u32[]{:S(2)}) %collective-permute-start.46) | collective-permute-done | bytes 262176 | tf_op jit(solution)/shard_map/ppermute | solution.py:897
  471.9 8.2 %collective-permute-done.39 = bf16[128,2048]{1,0:T(8,128)(2,1)S(1)} collective-permute-done((bf16[128,2048]{1,0:T(8,128)(2,1)}, bf16[128,2048]{1,0:T(8,128)(2,1)S(1)}, u32[]{:S(2)}, u32[]{:S(2)}) %collective-permute-start.39) | collective-permute-done | bytes 524320 | tf_op jit(solution)/shard_map/ppermute | solution.py:897
  484.6 6.3 %collective-permute-done.44 = bf16[64,2048]{1,0:T(8,128)(2,1)S(1)} collective-permute-done((bf16[64,2048]{1,0:T(8,128)(2,1)S(1)}, bf16[64,2048]{1,0:T(8,128)(2,1)S(1)}, u32[]{:S(2)}, u32[]{:S(2)}) %collective-permute-start.44) | collective-permute-done | bytes 262176 | tf_op jit(solution)/shard_map/ppermute | solution.py:897
  491.8 4.3 collective-permute-done.42
  (252 shorter events, 124.7 us)
Async XLA Ops:
  8.0 217.6 %all-gather.3.cloned.1.call-start = ((), (), s32[]{:S(2)}) async-start(), calls=%async_computation.4 | async-start | bytes 8650752 | tf_op jit(solution)/shard_map/all_gather | solution.py:993
  30.0 49.6 %collective-permute-start.2 = (bf16[1024,1024]{1,0:T(8,128)(2,1)S(1)}, bf16[1024,1024]{1,0:T(8,128)(2,1)}, u32[]{:S(2)}, u32[]{:S(2)}) collective-permute-start(bf16[1024,1024]{1,0:T(8,128)(2,1)S(1)} %bitcast.81), channel_id=1, source_target_pairs={{1,2},{2,1},{5,6},{6,5},{9,10},{10,9},{13,14},{14,13},{17,18},{18,... | collective-permute-start | bytes 6291464 | tf_op jit(solution)/shard_map/ppermute | solution.py:897
  32.1 15.1 %collective-permute-start.4 = (bf16[128,2176]{1,0:T(8,128)(2,1)S(1)}, bf16[128,2176]{1,0:T(8,128)(2,1)S(1)}, u32[]{:S(2)}, u32[]{:S(2)}) collective-permute-start(bf16[128,2176]{1,0:T(8,128)(2,1)S(1)} %maximum_select_fusion.refs_0_), channel_id=1, source_target_pairs={{0,8},{1,9},{2,10},{3,11},{4,0},{5,1},{6,2},{7,3},{8,16},{9,17},{1... | collective-permute-start | bytes 1671176 | tf_op jit(solution)/shard_map/ppermute | solution.py:897
  33.6 15.2 %collective-permute-start.5 = (bf16[128,2176]{1,0:T(8,128)(2,1)S(1)}, bf16[128,2176]{1,0:T(8,128)(2,1)S(1)}, u32[]{:S(2)}, u32[]{:S(2)}) collective-permute-start(bf16[128,2176]{1,0:T(8,128)(2,1)S(1)} %maximum_select_fusion.refs_0_), channel_id=1, source_target_pairs={{0,4},{1,5},{2,6},{3,7},{4,12},{5,13},{6,14},{7,15},{8,0},{9,1},{1... | collective-permute-start | bytes 1671176 | tf_op jit(solution)/shard_map/ppermute | solution.py:897
  48.8 14.6 %collective-permute-start.6 = (bf16[128,2176]{1,0:T(8,128)(2,1)S(1)}, bf16[128,2176]{1,0:T(8,128)(2,1)S(1)}, u32[]{:S(2)}, u32[]{:S(2)}) collective-permute-start(bf16[128,2176]{1,0:T(8,128)(2,1)S(1)} %collective-permute-done.4.refs_1_), channel_id=1, source_target_pairs={{0,8},{1,9},{2,10},{3,11},{4,0},{5,1},{6,2},{7,3},{8,16},{9,17},{1... | collective-permute-start | bytes 1671176 | tf_op jit(solution)/shard_map/ppermute | solution.py:897
  50.4 14.4 %collective-permute-start.7 = (bf16[128,2176]{1,0:T(8,128)(2,1)S(1)}, bf16[128,2176]{1,0:T(8,128)(2,1)S(1)}, u32[]{:S(2)}, u32[]{:S(2)}) collective-permute-start(bf16[128,2176]{1,0:T(8,128)(2,1)S(1)} %collective-permute-done.5.refs_2_), channel_id=1, source_target_pairs={{0,4},{1,5},{2,6},{3,7},{4,12},{5,13},{6,14},{7,15},{8,0},{9,1},{1... | collective-permute-start | bytes 1671176 | tf_op jit(solution)/shard_map/ppermute | solution.py:897
  64.8 13.5 %collective-permute-start.8 = (bf16[128,2176]{1,0:T(8,128)(2,1)S(1)}, bf16[128,2176]{1,0:T(8,128)(2,1)S(1)}, u32[]{:S(2)}, u32[]{:S(2)}) collective-permute-start(bf16[128,2176]{1,0:T(8,128)(2,1)S(1)} %collective-permute-done.6.refs_3_), channel_id=1, source_target_pairs={{0,8},{1,9},{2,10},{3,11},{4,0},{5,1},{6,2},{7,3},{8,16},{9,17},{1... | collective-permute-start | bytes 1671176 | tf_op jit(solution)/shard_map/ppermute | solution.py:897
  80.7 23.5 %collective-permute-start.13 = (bf16[1024,1024]{1,0:T(8,128)(2,1)S(1)}, bf16[1024,1024]{1,0:T(8,128)(2,1)}, u32[]{:S(2)}, u32[]{:S(2)}) collective-permute-start(bf16[1024,1024]{1,0:T(8,128)(2,1)S(1)} %broadcast_select_fusion.2.xa.x_ref.r_0_), channel_id=1, source_target_pairs={{0,2},{1,3},{2,0},{3,1},{4,6},{5,7},{6,4},{7,5},{8,10},{9,11},{10,... | collective-permute-start | bytes 6291464 | tf_op jit(solution)/shard_map/ppermute | solution.py:897
  92.0 27.6 %collective-permute-start.16 = (bf16[1024,1024]{1,0:T(8,128)(2,1)}, bf16[1024,1024]{1,0:T(8,128)(2,1)}, u32[]{:S(2)}, u32[]{:S(2)}) collective-permute-start(bf16[1024,1024]{1,0:T(8,128)(2,1)} %bitcast.11), channel_id=1, source_target_pairs={{1,2},{2,1},{5,6},{6,5},{9,10},{10,9},{13,14},{14,13},{17,18},{18,... | collective-permute-start | bytes 6291464 | tf_op jit(solution)/shard_map/ppermute | solution.py:897
  93.9 25.2 %collective-permute-start.17 = (s32[1,2048]{1,0:T(1,128)S(1)}, s32[1,2048]{1,0:T(1,128)S(1)}, u32[]{:S(2)}, u32[]{:S(2)}) collective-permute-start(s32[1,2048]{1,0:T(1,128)S(1)} %copy-done.44), channel_id=1, source_target_pairs={{0,2},{1,3},{2,0},{3,1},{4,6},{5,7},{6,4},{7,5},{8,10},{9,11},{10,... | collective-permute-start | bytes 24584 | tf_op jit(solution)/shard_map/ppermute | solution.py:897
  93.9 23.1 %collective-permute-start.14 = (bf16[128,2048]{1,0:T(8,128)(2,1)S(1)}, bf16[128,2048]{1,0:T(8,128)(2,1)}, u32[]{:S(2)}, u32[]{:S(2)}) collective-permute-start(bf16[128,2048]{1,0:T(8,128)(2,1)S(1)} %maximum_select_fusion.1.refs_0_), channel_id=1, source_target_pairs={{0,8},{1,9},{2,10},{3,11},{4,0},{5,1},{6,2},{7,3},{8,16},{9,17},{1... | collective-permute-start | bytes 1572872 | tf_op jit(solution)/shard_map/ppermute | solution.py:897
  94.6 22.4 %collective-permute-start.15 = (bf16[128,2048]{1,0:T(8,128)(2,1)S(1)}, bf16[128,2048]{1,0:T(8,128)(2,1)}, u32[]{:S(2)}, u32[]{:S(2)}) collective-permute-start(bf16[128,2048]{1,0:T(8,128)(2,1)S(1)} %maximum_select_fusion.1.refs_0_), channel_id=1, source_target_pairs={{0,4},{1,5},{2,6},{3,7},{4,12},{5,13},{6,14},{7,15},{8,0},{9,1},{1... | collective-permute-start | bytes 1572872 | tf_op jit(solution)/shard_map/ppermute | solution.py:897
  117.0 15.1 %collective-permute-start.18 = (bf16[128,2048]{1,0:T(8,128)(2,1)}, bf16[128,2048]{1,0:T(8,128)(2,1)}, u32[]{:S(2)}, u32[]{:S(2)}) collective-permute-start(bf16[128,2048]{1,0:T(8,128)(2,1)} %collective-permute-done.14.refs_1_), channel_id=1, source_target_pairs={{0,8},{1,9},{2,10},{3,11},{4,0},{5,1},{6,2},{7,3},{8,16},{9,17},{1... | collective-permute-start | bytes 1572872 | tf_op jit(solution)/shard_map/ppermute | solution.py:897
  117.7 14.4 %collective-permute-start.19 = (bf16[128,2048]{1,0:T(8,128)(2,1)}, bf16[128,2048]{1,0:T(8,128)(2,1)}, u32[]{:S(2)}, u32[]{:S(2)}) collective-permute-start(bf16[128,2048]{1,0:T(8,128)(2,1)} %collective-permute-done.15.refs_2_), channel_id=1, source_target_pairs={{0,4},{1,5},{2,6},{3,7},{4,12},{5,13},{6,14},{7,15},{8,0},{9,1},{1... | collective-permute-start | bytes 1572872 | tf_op jit(solution)/shard_map/ppermute | solution.py:897
  132.2 297.3 %reduce-scatter.5.cloned.1.call-start = ((), (), s32[]{:S(2)}) async-start(), calls=%async_computation.3 | async-start | bytes 4718592 | tf_op jit(solution)/shard_map/reduce_scatter | solution.py:962
  132.2 17.0 %collective-permute-start.20 = (bf16[128,2048]{1,0:T(8,128)(2,1)}, bf16[128,2048]{1,0:T(8,128)(2,1)S(1)}, u32[]{:S(2)}, u32[]{:S(2)}) collective-permute-start(bf16[128,2048]{1,0:T(8,128)(2,1)} %collective-permute-done.18.refs_3_), channel_id=1, source_target_pairs={{0,8},{1,9},{2,10},{3,11},{4,0},{5,1},{6,2},{7,3},{8,16},{9,17},{1... | collective-permute-start | bytes 1572872 | tf_op jit(solution)/shard_map/ppermute | solution.py:897
  132.9 18.5 %collective-permute-start.21 = (bf16[128,2048]{1,0:T(8,128)(2,1)}, bf16[128,2048]{1,0:T(8,128)(2,1)S(1)}, u32[]{:S(2)}, u32[]{:S(2)}) collective-permute-start(bf16[128,2048]{1,0:T(8,128)(2,1)} %collective-permute-done.19.refs_4_), channel_id=1, source_target_pairs={{0,4},{1,5},{2,6},{3,7},{4,12},{5,13},{6,14},{7,15},{8,0},{9,1},{1... | collective-permute-start | bytes 1572872 | tf_op jit(solution)/shard_map/ppermute | solution.py:897
  159.0 32.3 %collective-permute-start.24 = (bf16[1024,1024]{1,0:T(8,128)(2,1)S(1)}, bf16[1024,1024]{1,0:T(8,128)(2,1)}, u32[]{:S(2)}, u32[]{:S(2)}) collective-permute-start(bf16[1024,1024]{1,0:T(8,128)(2,1)S(1)} %broadcast_select_fusion.1.ya.skip), channel_id=1, source_target_pairs={{0,2},{1,3},{2,0},{3,1},{4,6},{5,7},{6,4},{7,5},{8,10},{9,11},{10,... | collective-permute-start | bytes 6291464 | tf_op jit(solution)/shard_map/ppermute | solution.py:897
  172.5 18.9 %collective-permute-start.23 = (bf16[1024,1024]{1,0:T(8,128)(2,1)}, bf16[1024,1024]{1,0:T(8,128)(2,1)}, u32[]{:S(2)}, u32[]{:S(2)}) collective-permute-start(bf16[1024,1024]{1,0:T(8,128)(2,1)} %get-tuple-element.117.aa), channel_id=1, source_target_pairs={{0,2},{1,3},{2,0},{3,1},{4,6},{5,7},{6,4},{7,5},{8,10},{9,11},{10,... | collective-permute-start | bytes 6291464 | tf_op jit(solution)/shard_map/ppermute | solution.py:897
  225.1 243.9 %reduce-scatter.3.cloned.1.call-start = ((), (), s32[]{:S(2)}) async-start(), calls=%async_computation.2 | async-start | bytes 4718592 | tf_op jit(solution)/shard_map/reduce_scatter | solution.py:962
  289.6 13.7 %collective-permute-start.28 = (bf16[1024,1024]{1,0:T(8,128)(2,1)}, bf16[1024,1024]{1,0:T(8,128)(2,1)}, u32[]{:S(2)}, u32[]{:S(2)}) collective-permute-start(bf16[1024,1024]{1,0:T(8,128)(2,1)} %get-tuple-element.128), channel_id=1, source_target_pairs={{0,2},{1,3},{2,0},{3,1},{4,6},{5,7},{6,4},{7,5},{8,10},{9,11},{10,... | collective-permute-start | bytes 6291464 | tf_op jit(solution)/shard_map/ppermute | solution.py:897
  308.2 41.7 %collective-permute-start.30 = (bf16[1024,1024]{1,0:T(8,128)(2,1)}, bf16[1024,1024]{1,0:T(8,128)(2,1)}, u32[]{:S(2)}, u32[]{:S(2)}) collective-permute-start(bf16[1024,1024]{1,0:T(8,128)(2,1)} %add_convert_fusion), channel_id=1, source_target_pairs={{1,2},{2,1},{5,6},{6,5},{9,10},{10,9},{13,14},{14,13},{17,18},{18,... | collective-permute-start | bytes 6291464 | tf_op jit(solution)/shard_map/ppermute | solution.py:897
  383.4 22.8 %collective-permute-start.33 = (bf16[1024,1024]{1,0:T(8,128)(2,1)}, bf16[1024,1024]{1,0:T(8,128)(2,1)}, u32[]{:S(2)}, u32[]{:S(2)}) collective-permute-start(bf16[1024,1024]{1,0:T(8,128)(2,1)} %get-tuple-element.150), channel_id=1, source_target_pairs={{0,2},{1,3},{2,0},{3,1},{4,6},{5,7},{6,4},{7,5},{8,10},{9,11},{10,... | collective-permute-start | bytes 6291464 | tf_op jit(solution)/shard_map/ppermute | solution.py:897
  383.8 20.3 %collective-permute-start.32 = (bf16[64,2048]{1,0:T(8,128)(2,1)S(1)}, bf16[64,2048]{1,0:T(8,128)(2,1)S(1)}, u32[]{:S(2)}, u32[]{:S(2)}) collective-permute-start(bf16[64,2048]{1,0:T(8,128)(2,1)S(1)} %get-tuple-element.142), channel_id=1, source_target_pairs={{0,4},{1,5},{2,6},{3,7},{4,12},{5,13},{6,14},{7,15},{8,0},{9,1},{1... | collective-permute-start | bytes 786440 | tf_op jit(solution)/shard_map/ppermute | solution.py:897
  416.8 17.2 %collective-permute-start.35 = (bf16[128,2048]{1,0:T(8,128)(2,1)S(1)}, bf16[128,2048]{1,0:T(8,128)(2,1)S(1)}, u32[]{:S(2)}, u32[]{:S(2)}) collective-permute-start(bf16[128,2048]{1,0:T(8,128)(2,1)S(1)} %get-tuple-element.183), channel_id=1, source_target_pairs={{0,8},{1,9},{2,10},{3,11},{4,0},{5,1},{6,2},{7,3},{8,16},{9,17},{1... | collective-permute-start | bytes 1572872 | tf_op jit(solution)/shard_map/ppermute | solution.py:897
  416.9 17.2 %collective-permute-start.36 = (bf16[128,2048]{1,0:T(8,128)(2,1)S(1)}, bf16[128,2048]{1,0:T(8,128)(2,1)S(1)}, u32[]{:S(2)}, u32[]{:S(2)}) collective-permute-start(bf16[128,2048]{1,0:T(8,128)(2,1)S(1)} %get-tuple-element.182), channel_id=1, source_target_pairs={{0,4},{1,5},{2,6},{3,7},{4,12},{5,13},{6,14},{7,15},{8,0},{9,1},{1... | collective-permute-start | bytes 1572872 | tf_op jit(solution)/shard_map/ppermute | solution.py:897
  419.0 13.7 %collective-permute-start.48 = (f32[4,1024]{1,0:T(4,128)S(1)}, f32[4,1024]{1,0:T(4,128)S(1)}, u32[]{:S(2)}, u32[]{:S(2)}) collective-permute-start(f32[4,1024]{1,0:T(4,128)S(1)} %fusion.16), channel_id=1, source_target_pairs={{0,1},{1,0},{2,3},{3,2},{4,5},{5,4},{6,7},{7,6},{8,9},{9,8},{10,11... | collective-permute-start | bytes 49160 | tf_op jit(solution)/shard_map/ppermute | solution.py:897
  430.6 33.9 %collective-permute-start.34 = (bf16[1024,1024]{1,0:T(8,128)(2,1)}, bf16[1024,1024]{1,0:T(8,128)(2,1)}, u32[]{:S(2)}, u32[]{:S(2)}) collective-permute-start(bf16[1024,1024]{1,0:T(8,128)(2,1)} %copy-done.16), channel_id=1, source_target_pairs={{1,2},{2,1},{5,6},{6,5},{9,10},{10,9},{13,14},{14,13},{17,18},{18,... | collective-permute-start | bytes 6291464 | tf_op jit(solution)/shard_map/ppermute | solution.py:897
  438.5 26.0 %collective-permute-start.37 = (bf16[128,2048]{1,0:T(8,128)(2,1)S(1)}, bf16[128,2048]{1,0:T(8,128)(2,1)S(1)}, u32[]{:S(2)}, u32[]{:S(2)}) collective-permute-start(bf16[128,2048]{1,0:T(8,128)(2,1)S(1)} %get-tuple-element.181), channel_id=1, source_target_pairs={{0,8},{1,9},{2,10},{3,11},{4,0},{5,1},{6,2},{7,3},{8,16},{9,17},{1... | collective-permute-start | bytes 1572872 | tf_op jit(solution)/shard_map/ppermute | solution.py:897
  440.2 24.3 %collective-permute-start.38 = (bf16[128,2048]{1,0:T(8,128)(2,1)S(1)}, bf16[128,2048]{1,0:T(8,128)(2,1)S(1)}, u32[]{:S(2)}, u32[]{:S(2)}) collective-permute-start(bf16[128,2048]{1,0:T(8,128)(2,1)S(1)} %get-tuple-element.180), channel_id=1, source_target_pairs={{0,4},{1,5},{2,6},{3,7},{4,12},{5,13},{6,14},{7,15},{8,0},{9,1},{1... | collective-permute-start | bytes 1572872 | tf_op jit(solution)/shard_map/ppermute | solution.py:897
  440.6 14.3 %collective-permute-start.51 = (f32[4,1024]{1,0:T(4,128)S(1)}, f32[4,1024]{1,0:T(4,128)S(1)}, u32[]{:S(2)}, u32[]{:S(2)}) collective-permute-start(f32[4,1024]{1,0:T(4,128)S(1)} %add.146), channel_id=1, source_target_pairs={{0,16},{1,17},{2,18},{3,19},{4,20},{5,21},{6,22},{7,23},{8,24},{9,... | collective-permute-start | bytes 49160 | tf_op jit(solution)/shard_map/ppermute | solution.py:897
  443.8 19.8 %collective-permute-start.46 = (bf16[64,2048]{1,0:T(8,128)(2,1)S(1)}, bf16[64,2048]{1,0:T(8,128)(2,1)S(1)}, u32[]{:S(2)}, u32[]{:S(2)}) collective-permute-start(bf16[64,2048]{1,0:T(8,128)(2,1)S(1)} %fusion.13), channel_id=1, source_target_pairs={{0,1},{1,0},{2,3},{3,2},{4,5},{5,4},{6,7},{7,6},{8,9},{9,8},{10,11... | collective-permute-start | bytes 786440 | tf_op jit(solution)/shard_map/ppermute | solution.py:897
  (68 other events, 682.6 us)
Sparse Core Ops, SparseCore 0:
  132.3 75.4 all-gather.2
Sparse Core Ops, SparseCore 1:
  225.2 86.5 reduce-scatter.4
  315.8 93.0 reduce-scatter.2

commit v3 on v2

--- a/solution.py
+++ b/solution.py
@@ -468,50 +468,43 @@
     )(slopes, qkv, qkv, qkv, grad, mixed, logs, seg_row)
 
 
-def branch_kernel(core, oa, ob, w, x_ref, oth_out, own_out):
-    step = pl.program_id(0)
-    half = pl.num_programs(0) // 2
+def branch_oth_kernel(core, oa, ob, w, out):
     weight = w[...].reshape(w.shape[0] * w.shape[1], w.shape[2])
-    part = mm(jnp.concatenate([oa[...], ob[...]], axis=1), weight, NT)
-
-    @pl.when(step < half)
-    def _():
-        oth_out[...] = part.astype(BF)
-
-    @pl.when(step >= half)
-    def _():
-        own_out[...] = x_ref[...].astype(F32) + part
-
-
-def branch(core, mixed, g1, x_own):
-    rows, width = x_own.shape
+    out[...] = mm(jnp.concatenate([oa[...], ob[...]], axis=1), weight, NT).astype(BF)
+
+
+def branch_own_kernel(core, oa, ob, w, x_ref, out):
+    weight = w[...].reshape(w.shape[0] * w.shape[1], w.shape[2])
+    out[...] = x_ref[...].astype(F32) + mm(jnp.concatenate([oa[...], ob[...]], axis=1), weight, NT)
+
+
+def branch(core, mixed, weights, x_own=None):
+    rows = mixed[0].shape[0] // 2
+    chips, per, _ = weights.shape
+    width = chips * per
     tile = 512
     half = rows // tile
-    chips, per, _ = g1.shape
+    own = x_own is not None
+    own_rows = pl.BlockSpec((tile, width), lambda i, c: (i, 0))
+
+    def place(i, c):
+        return (i + half * (c[0] if own else 1 - c[0]), 0)
+
     spec = pltpu.PrefetchScalarGridSpec(
         num_scalar_prefetch=1,
-        grid=(2 * half,),
-        in_specs=[
-            pl.BlockSpec((tile, 256), lambda i, c: (i % half + half * (1 - (i // half) ^ c[0]), 0)),
-            pl.BlockSpec((tile, 256), lambda i, c: (i % half + half * (1 - (i // half) ^ c[0]), 0)),
-            pl.BlockSpec((chips, per, 512), lambda i, c: (0, 0, 3)),
-            pl.BlockSpec((tile, width), lambda i, c: (jnp.maximum(i - half, 0), 0)),
-        ],
-        out_specs=[
-            pl.BlockSpec((tile, width), lambda i, c: (jnp.minimum(i, half - 1), 0)),
-            pl.BlockSpec((tile, width), lambda i, c: (jnp.maximum(i - half, 0), 0)),
-        ],
-    )
-    return pl.pallas_call(
-        branch_kernel,
+        grid=(half,),
+        in_specs=[pl.BlockSpec((tile, 256), place)] * 2
+        + [pl.BlockSpec((chips, per, 512), lambda i, c: (0, 0, 3))]
+        + ([own_rows] if own else []),
+        out_specs=own_rows,
+    )
+    return pl.pallas_call(
+        branch_own_kernel if own else branch_oth_kernel,
         grid_spec=spec,
-        out_shape=[
-            jax.ShapeDtypeStruct((rows, width), BF),
-            jax.ShapeDtypeStruct((rows, width), F32),
-        ],
-        cost_estimate=cost(4 * rows * width * 512, 12 * 2**20),
+        out_shape=jax.ShapeDtypeStruct((rows, width), F32 if own else BF),
+        cost_estimate=cost(2 * rows * width * 512, 6 * 2**20),
         **params(48),
-    )(core, *mixed, g1, x_own)
+    )(core, *mixed, weights, *([x_own] if own else []))
 
 
 def residual_kernel(part, recv, gb, h_out, a2_out):
@@ -551,16 +544,24 @@
     def _():
         acc[...] = jnp.zeros_like(acc)
 
+    def product(c):
+        return mm(a2, w_ref[:, :, c : c + chunk].reshape(chips * per, chunk), NN)
+
+    u, held = product(0), []
     for c in range(0, hidden, chunk):
         cols = slice(c, c + chunk)
-        u = mm(a2, w_ref[:, :, cols].reshape(chips * per, chunk), NN)
+        later = product(c + chunk) if c + chunk < hidden else None
         sq = u * u
         th = jnp.tanh(u * (c0 + c0 * c1 * sq))
         hp = 0.5 + 0.5 * th
         g = (u * hp).astype(BF)
         g_out[:, cols] = g
         s_out[:, cols] = (hp + (0.5 * u) * (1.0 - th * th) * (c0 + 3.0 * c0 * c1 * sq)).astype(BF)
-        acc[:, cols] += mm(dyt, g, NN)
+        held.append((cols, g))
+        if c > 0:
+            acc[:, held[-2][0]] += mm(dyt, held[-2][1], NN)
+        u = later
+    acc[:, held[-1][0]] += mm(dyt, held[-1][1], NN)
 
     @pl.when(step == steps - 1)
     def _():
@@ -608,28 +609,23 @@
     )(core, a_own, a_oth, y_own, y_oth, w1)
 
 
-def down_kernel(core, aa, ab, ya, yb, g_ref, s_ref, w1_ref, w2_ref, f_own, f_oth, d_own, d_oth, gw_out, acc, du_s):
+def down_kernel(core, aa, ab, ya, yb, g_ref, s_ref, w1_ref, w2_ref, f_own, f_oth, d_own, d_oth, gw_out, a2t_s, du_s):
     step = pl.program_id(0)
     steps = pl.num_programs(0)
     half = steps // 2
     chips, per, hidden = w1_ref.shape
     width = chips * per
-    a2t = jnp.where(step < half, aa[...], ab[...]).T
+    tile = aa.shape[0]
+    rows = pl.ds(pl.multiple_of(step * tile, tile), tile)
+    a2t_s[:, rows] = jnp.where(step < half, aa[...], ab[...]).T
     dy = jnp.where(step < half, ya[...], yb[...])
     chunk = 512
-
-    @pl.when(step == 0)
-    def _():
-        acc[...] = jnp.zeros_like(acc)
-
     for c in range(0, hidden, chunk):
         cols = slice(c, c + chunk)
         dg = mm(dy, w2_ref[:, 0, :, cols].reshape(width, chunk), NN)
-        du = (dg * s_ref[:, cols].astype(F32)).astype(BF)
-        du_s[:, cols] = du
-        acc[:, cols] += mm(a2t, du, NN)
+        du_s[rows, cols] = (dg * s_ref[:, cols].astype(F32)).astype(BF)
     f = mm(g_ref[...], w2_ref[:, 0].reshape(width, hidden), NT).astype(BF)
-    d = mm(du_s[...], w1_ref[...].reshape(width, hidden), NT).astype(BF)
+    d = mm(du_s[rows, :], w1_ref[...].reshape(width, hidden), NT).astype(BF)
 
     @pl.when(step < half)
     def _():
@@ -643,7 +639,9 @@
 
     @pl.when(step == steps - 1)
     def _():
-        gw_out[...] = acc[...].astype(BF).reshape(gw_out.shape)
+        for c in range(0, hidden, chunk):
+            cols = slice(c, c + chunk)
+            gw_out[:, :, cols] = mm(a2t_s[...], du_s[:, cols], NN).astype(BF).reshape(chips, per, chunk)
 
 
 def down(core, a_own, a_oth, y_own, y_oth, hidden_units, slope, w1, w2):
@@ -657,7 +655,7 @@
         in_specs=halves(tile, width, rows // tile) * 2 + [units, units, ringed(w1), gathered(w2)],
         out_specs=halves(tile, width, rows // tile) * 2
         + [pl.BlockSpec((chips, per, hidden), lambda i, c: (0, 0, 0), pipeline_mode=pl.Buffered(1))],
-        scratch_shapes=[pltpu.VMEM((width, hidden), F32), pltpu.VMEM((tile, hidden), BF)],
+        scratch_shapes=[pltpu.VMEM((width, 2 * rows), BF), pltpu.VMEM((2 * rows, hidden), BF)],
     )
     return pl.pallas_call(
         down_kernel,
@@ -783,37 +781,40 @@
     )(core, d_own, d_oth, *mixed, g1)
 
 
-def project_weight_kernel(a1, *refs):
+def project_weight_kernel(a1, gwo, *refs):
     *grads, gw_out, acc = refs
     step = pl.program_id(0)
     grad = jnp.concatenate([g[...] for g in grads], axis=1)
+    wide = grad.shape[1]
 
     @pl.when(step == 0)
     def _():
         acc[...] = jnp.zeros_like(acc)
+        gw_out[:, wide:] = gwo[...]
 
     acc[...] += mm(a1[...], grad, TN)
 
     @pl.when(step == pl.num_programs(0) - 1)
     def _():
-        gw_out[...] = acc[...].astype(BF)
-
-
-def project_weight(a1, grads):
+        gw_out[:, :wide] = acc[...].astype(BF)
+
+
+def project_weight(a1, gwo, grads):
     rows2, width = a1.shape
     tile = 512
     wide = sum(g.shape[1] for g in grads)
+    total = wide + gwo.shape[1]
     return pl.pallas_call(
         project_weight_kernel,
         grid=(rows2 // tile,),
-        in_specs=[pl.BlockSpec((tile, width), lambda i: (i, 0))]
+        in_specs=[pl.BlockSpec((tile, width), lambda i: (i, 0)), pl.BlockSpec(gwo.shape, lambda i: (0, 0))]
         + [pl.BlockSpec((tile, g.shape[1]), lambda i: (i, 0)) for g in grads],
-        out_specs=pl.BlockSpec((width, wide), lambda i: (0, 0)),
+        out_specs=pl.BlockSpec((width, total), lambda i: (0, 0)),
         scratch_shapes=[pltpu.VMEM((width, wide), F32)],
-        out_shape=jax.ShapeDtypeStruct((width, wide), BF),
+        out_shape=jax.ShapeDtypeStruct((width, total), BF),
         cost_estimate=cost(2 * rows2 * width * wide, 14 * 2**20),
         **params(56),
-    )(a1, *grads)
+    )(a1, gwo, *grads)
 
 
 def project_back_kernel(core, *refs):
@@ -887,8 +888,8 @@
     turn = {d: [(ident(q, k, j), ident(RING[(place_of[q] + d) % chips], k, j)) for q, k, j in cells] for d in (1, -1)}
     hops = [[(ident(q, k, j), ident(q ^ m, k, j)) for q, k, j in cells] for m in (1, 2, 4)]
     near = [0] + [s * d for d in range(1, far) for s in (-1, 1)] + [far]
-    table = jnp.array([[RING[(place_of[q] + d) % chips] for d in near] for q in range(chips)], jnp.int32)
-    where = lax.dynamic_index_in_dim(table, chip, 0, keepdims=False)
+    table = jnp.array([[RING[(place_of[q] + d) % chips] for d in near] for q in range(chips)], jnp.uint32)
+    where = lax.dynamic_index_in_dim(table, chip.astype(jnp.uint32), 0, keepdims=False)
 
     def chip_at(d):
         return where[near.index(d if d != -far else far)]
@@ -909,7 +910,7 @@
             return right, left
 
         def whole(self):
-            return assemble(where, [self.got[d] for d in near[:-1]], self.got[-far], self.got[far])
+            return assemble(where.astype(jnp.int32), [self.got[d] for d in near[:-1]], self.got[-far], self.got[far])
 
     class Reduce:
         def __init__(self, blocks):
@@ -941,8 +942,8 @@
 
     def to_owner(total):
         per = total.shape[0] // 2
-        mine = lax.dynamic_slice_in_dim(total, core * per, per, 0)
-        theirs = lax.dynamic_slice_in_dim(total, (1 - core) * per, per, 0).astype(BF)
+        mine = jnp.where(core == 0, total[:per], total[per:])
+        theirs = jnp.where(core == 0, total[per:], total[:per]).astype(BF)
         recv = send(theirs, to_core).astype(F32)
         keep = jnp.where(at_home, mine, recv)
         leave = jnp.where(at_home, recv, mine).astype(BF)
@@ -972,9 +973,9 @@
     seg_col = seg.reshape(-1, 1)
     g1 = Gather(unit_of(shard1, cross1))
     sent = g1.step(1)
-    cross2 = send(after(low_in, cross1), to_y)
-    cross_x = send(after(tokens[0], cross2), back)
-    sent = g1.step(2, cross2)
+    cross_x = send(after(tokens[0], cross1), back)
+    sent = g1.step(2)
+    cross2 = send(after(low_in, *sent), to_y)
     sent = g1.step(3)
     sent = g1.step(4, cross_x)
     x_own = jnp.where(at_home, tokens[0], after(cross_x, *sent))
@@ -997,10 +998,11 @@
     y_oth = send(y_own, to_core)
     sent = g2.step(4, mixed1)
     mixed = (after(mixed0, *sent, y_own), mixed1)
-    part_oth, part_own = branch(core_arg, mixed, wa, x_own)
-    h1, a2_own = residual(part_own, send(part_oth, to_core), gb)
+    part_recv = send(branch(core_arg, mixed, wa), to_core)
+    part_own = branch(core_arg, (after(mixed[0], g2.got[far], g2.got[-far]), mixed[1]), wa, x_own)
+    w1 = g2.whole()
+    h1, a2_own = residual(after(part_own, w1), part_recv, gb)
     a2_oth = send(a2_own, to_core)
-    w1 = g2.whole()
     hidden, slope, gw2 = up(core_arg, a2_own, a2_oth, y_own, y_oth, w1)
     r2 = reduce_chips(gw2)
     f_own, f_oth, d_own, d_oth, gw1 = down(core_arg, a2_own, a2_oth, after(y_own, gw2), y_oth, hidden, slope, w1, w2)
@@ -1015,29 +1017,29 @@
     both_mixed = jnp.concatenate(mixed, axis=1)
     both_logs = jnp.concatenate([logs0, logs1], axis=0)
     grads = attend_back(slopes, after(qkv, do, result), do, both_mixed, both_logs, seg)
-    result = jnp.where(at_home, result, after(cross_result, grads[0]))
-    gwq = project_weight(after(a1, result), grads)
-    rc = Reduce(jnp.concatenate([gwq, gwo], axis=1).reshape(chips, width // chips, -1))
+    d1_oth, d1_own = project_back(core_arg, after(tuple(grads), r2), wa)
+    d1_recv = send(d1_oth, to_core)
+    grad_back = to_owner(after(r2, d1_own).astype(F32))
+    gwq = project_weight(after(a1, d1_own), gwo, grads)
+    result = jnp.where(at_home, result, after(cross_result, gwq))
+    rc = Reduce(gwq.reshape(chips, width // chips, -1))
     sent = rc.step(1)
-    d1_oth, d1_own = project_back(core_arg, after(tuple(grads), *sent), wa)
-    d1_recv = send(d1_oth, to_core)
-    sent = rc.step(2, d1_own)
-    grad_tokens, sums1 = through_norm(x_own, after(d1_own, *sent), d1_recv, dh1, gb[0:1], False)
+    grad_tokens, sums1 = through_norm(x_own, after(d1_own, *sent, grad_back), d1_recv, dh1, gb[0:1], False)
     cross_tokens = send(grad_tokens, back)
-    sent = rc.step(3, sums1)
+    sent = rc.step(2, sums1)
+    sent = rc.step(3, result)
     sent = rc.step(4, cross_tokens)
+    grad_in = to_owner(after(r1, *sent).astype(F32))
     sums = jnp.concatenate([sums1[0:1], sums2[0:1], sums1[1:2], sums2[1:2]], axis=0)
     for pairs in (to_core, to_y, *hops):
         sums = sums + send(sums, pairs)
-    grad_back = to_owner(after(r2, sums1).astype(F32))
-    grad_in = to_owner(after(r1, *sent).astype(F32))
     r3 = to_owner(rc.total())
     grad_tokens = jnp.where(at_home, grad_tokens, cross_tokens)
     per = r3.shape[0]
     wide = 3 * heads * HEAD
     grad_qkv = r3[:, :wide].reshape(per, 3, -1).transpose(1, 0, 2)
     grad_out = r3[:, wide:].T
-    sums = lax.dynamic_slice_in_dim(sums, dp_rank * norm_gains.shape[1], norm_gains.shape[1], 1)
+    sums = lax.dynamic_slice_in_dim(sums, dp_rank.astype(jnp.uint32) * norm_gains.shape[1], norm_gains.shape[1], 1)
     return (result[None], grad_tokens[None], grad_qkv, grad_out, grad_in, grad_back.T, sums[0:2], sums[2:4])
 
 

time: 515 us -> 487 us (0.946)
  between operations: 32.1 us -> 16.5 us
  starting transfers between devices: 50.2 us -> 45 us
    ppermute x52, starting transfers between devices: 49.7 us -> 44.5 us  [send(): return lax.ppermute(v, both, pairs)]
    unnamed x91 -> x93, local copies, waits for them, and re-layouts: 22.4 us -> 21.8 us
  transfers between devices with their start and end apart: 55 -> 55, of which waited for: 25 -> 28; matrix products, arithmetic and copies ran while one was open for 7% -> 7% of each run, Pallas kernels for 43% -> 44%
where the time goes in v3:
time: 487 us; the launch traced here: 478 us
  Pallas kernels  212 us (44%)
  waiting for transfers between devices  143 us (29%)
  starting transfers between devices  45 us (9%)
  other arithmetic  33.4 us (7%)
  local copies, waits for them, and re-layouts  28 us (6%)
  between operations  16.5 us (3%)
    ppermute x52, waiting for transfers between devices, send(): return lax.ppermute(v, both, pairs)  143 us
    pallas_call x1, Pallas kernels, down(): pl.pallas_call(down_kernel, grid_spec=spec, out_shape=[jax.ShapeDtypeStru...  46.2 us
    ppermute x52, starting transfers between devices, send(): return lax.ppermute(v, both, pairs)  44.5 us
    pallas_call x1, Pallas kernels, attend_back(): pl.pallas_call(attend_back_kernel, grid_spec=spec, out_shape=[jax.ShapeDt...  35.2 us
    pallas_call x1, Pallas kernels, up(): pl.pallas_call(up_kernel, grid_spec=spec, out_shape=[jax.ShapeDtypeStruct...  29.2 us
    pallas_call x2, Pallas kernels, attend(): pl.pallas_call(attend_kernel, grid_spec=spec, out_shape=[jax.ShapeDtypeSt...  25.1 us
    unnamed x93, local copies, waits for them, and re-layouts  21.8 us
    pallas_call x1, Pallas kernels, project_weight(): pl.pallas_call(project_weight_kernel, grid=(rows2 // tile,), in_specs=[pl...  13.3 us
  transfers between devices with their start and end apart: 55, of which 28 were waited for; matrix products, arithmetic and copies ran while one was open for 7% of the time, Pallas kernels for 44%

profile of v3, /device:TPU:0, one launch (start us, length us, event | category | flops | bytes accessed | tf_op | source)
XLA Modules:
  0.0 478.0 jit_solution(11841038818437944709)
XLA Ops:
  14.9 6.7 %collective-permute-done = bf16[64,2176]{1,0:T(8,128)(2,1)S(1)} collective-permute-done((bf16[64,2176]{1,0:T(8,128)(2,1)S(1)}, bf16[64,2176]{1,0:T(8,128)(2,1)S(1)}, u32[]{:S(2)}, u32[]{:S(2)}) %collective-permute-start) | collective-permute-done | bytes 278560 | tf_op jit(solution)/shard_map/ppermute | solution.py:898
  28.3 12.7 %collective-permute-done.3.refs_1_ = bf16[128,2176]{1,0:T(8,128)(2,1)S(1)} collective-permute-done((bf16[128,2176]{1,0:T(8,128)(2,1)S(1)}, bf16[128,2176]{1,0:T(8,128)(2,1)S(1)}, u32[]{:S(2)}, u32[]{:S(2)}) %collective-permute-start.3) | collective-permute-done | bytes 557088 | tf_op jit(solution)/shard_map/ppermute | solution.py:898
  45.3 12.7 %collective-permute-done.5.refs_3_ = bf16[128,2176]{1,0:T(8,128)(2,1)S(1)} collective-permute-done((bf16[128,2176]{1,0:T(8,128)(2,1)S(1)}, bf16[128,2176]{1,0:T(8,128)(2,1)S(1)}, u32[]{:S(2)}, u32[]{:S(2)}) %collective-permute-start.5) | collective-permute-done | bytes 557088 | tf_op jit(solution)/shard_map/ppermute | solution.py:898
  61.4 11.4 %collective-permute-done.7.refs_5_ = bf16[128,2176]{1,0:T(8,128)(2,1)S(1)} collective-permute-done((bf16[128,2176]{1,0:T(8,128)(2,1)S(1)}, bf16[128,2176]{1,0:T(8,128)(2,1)S(1)}, u32[]{:S(2)}, u32[]{:S(2)}) %collective-permute-start.7) | collective-permute-done | bytes 557088 | tf_op jit(solution)/shard_map/ppermute | solution.py:898
  79.5 5.0 %collective-permute-done.11.refs_7_ = bf16[64,2176]{1,0:T(8,128)(2,1)S(1)} collective-permute-done((bf16[64,2176]{1,0:T(8,128)(2,1)S(1)}, bf16[64,2176]{1,0:T(8,128)(2,1)S(1)}, u32[]{:S(2)}, u32[]{:S(2)}) %collective-permute-start.11) | collective-permute-done | bytes 278560 | tf_op jit(solution)/shard_map/ppermute | solution.py:898
  91.9 5.1 %shard_map.161.w.refs_3_ = bf16[8,128,2176]{2,1,0:T(8,128)(2,1)} custom-call(s32[8]{0:T(128)} %get-tuple-element.200.order, bf16[128,2176]{1,0:T(8,128)(2,1)} %copy-done.25, bf16[128,2176]{1,0:T(8,128)(2,1)} %copy-done.35, bf16[128,2176]{1,0:T(8,128)(2,1)} %copy-done.36, bf16[128,2176]{1,0:T(8,128)(2,1)} %copy-done.37, bf16[128,2176]{1,0:T(8,128)(2,1)} %copy-done.38, ...), custom_call_target="tpu_custom_call" | custom-call | flops 1024 | bytes 1024 | tf_op jit(solution)/shard_map/pallas_call | solution.py:693
  98.2 12.7 %shard_map.162 = (bf16[2048,1024]{1,0:T(8,128)(2,1)}, bf16[2048,1536]{1,0:T(8,128)(2,1)}) custom-call(s32[1]{0:T(128)} %bitcast.core, bf16[1024,1024]{1,0:T(8,128)(2,1)S(1)} %broadcast_select_fusion.2.xa.x_ref.r_0_, bf16[1024,1024]{1,0:T(8,128)(2,1)} %collective-permute-done.13.xb, f32[4,1024]{1,0:T(4,128)S(1)} %bitcast.68, ...), custom_call_target="tpu_custom_call" | custom-call | flops 1024 | bytes 1024 | tf_op jit(solution)/shard_map/pallas_call | solution.py:327
  113.5 12.5 %shard_map.163 = (bf16[2048,256]{1,0:T(8,128)(2,1)S(1)}, f32[2,1,2048]{2,1,0:T(1,128)S(1)}) custom-call(f32[2]{0:T(128)S(1)} %get-tuple-element.212.slopes, bf16[2048,1536]{1,0:T(8,128)(2,1)} %get-tuple-element.132.q_ref.k_ref.v_ref, bf16[2048,1536]{1,0:T(8,128)(2,1)} %get-tuple-element.132.q_ref.k_ref.v_ref, ...), custom_call_target="tpu_custom_call" | custom-call | flops 1024 | bytes 1024 | tf_op jit(solution)/shard_map/pallas_call | solution.py:392
  128.4 12.5 %shard_map.164 = (bf16[2048,256]{1,0:T(8,128)(2,1)S(1)}, f32[2,1,2048]{2,1,0:T(1,128)S(1)}) custom-call(f32[2]{0:T(128)S(1)} %get-tuple-element.211.slopes, bf16[2048,1536]{1,0:T(8,128)(2,1)} %get-tuple-element.132.q_ref.k_ref.v_ref, bf16[2048,1536]{1,0:T(8,128)(2,1)} %get-tuple-element.132.q_ref.k_ref.v_ref, ...), custom_call_target="tpu_custom_call" | custom-call | flops 1024 | bytes 1024 | tf_op jit(solution)/shard_map/pallas_call | solution.py:392
  145.7 3.9 shard_map.167
  151.6 15.7 %collective-permute-done.22.refs_8_ = bf16[64,2048]{1,0:T(8,128)(2,1)S(1)} collective-permute-done((bf16[64,2048]{1,0:T(8,128)(2,1)S(1)}, bf16[64,2048]{1,0:T(8,128)(2,1)S(1)}, u32[]{:S(2)}, u32[]{:S(2)}) %collective-permute-start.22) | collective-permute-done | bytes 262176 | tf_op jit(solution)/shard_map/ppermute | solution.py:898
  167.3 4.1 shard_map.165.part
  171.5 5.0 %shard_map.166.w_ref.w1_ref = bf16[8,128,2048]{2,1,0:T(8,128)(2,1)} custom-call(s32[8]{0:T(128)} %get-tuple-element.200.order, bf16[128,2048]{1,0:T(8,128)(2,1)} %copy-done.30, bf16[128,2048]{1,0:T(8,128)(2,1)} %collective-permute-done.14.refs_1_, bf16[128,2048]{1,0:T(8,128)(2,1)} %collective-permute-done.15.refs_2_, ...), custom_call_target="tpu_custom_call" | custom-call | flops 1024 | bytes 1024 | tf_op jit(solution)/shard_map/pallas_call | solution.py:693
  188.5 29.2 %shard_map.169 = (bf16[2048,2048]{1,0:T(8,128)(2,1)}, bf16[2048,2048]{1,0:T(8,128)(2,1)}, bf16[8,128,2048]{2,1,0:T(8,128)(2,1)}) custom-call(s32[1]{0:T(128)} %bitcast.core, bf16[1024,1024]{1,0:T(8,128)(2,1)} %copy-done.11, bf16[1024,1024]{1,0:T(8,128)(2,1)} %collective-permute-done.25.ab, bf16[1024,1024]{1,0:T(8,128)(2,1)} %copy-done, ...), custom_call_target="tpu_custom_call" | custom-call | flops 1024 | bytes 1024 | tf_op jit(solution)/shard_map/pallas_call | solution.py:602
  218.2 46.2 %shard_map.170 = (bf16[1024,1024]{1,0:T(8,128)(2,1)}, bf16[1024,1024]{1,0:T(8,128)(2,1)}, bf16[1024,1024]{1,0:T(8,128)(2,1)}, bf16[1024,1024]{1,0:T(8,128)(2,1)}, bf16[8,128,2048]{2,1,0:T(8,128)(2,1)}) custom-call(s32[1]{0:T(128)} %bitcast.core, bf16[1024,1024]{1,0:T(8,128)(2,1)} %copy-done.11, bf16[1024,1024]{1,0:T(8,128)(2,1)} %collective-permute-done.25.ab, ...), custom_call_target="tpu_custom_call" | custom-call | flops 1024 | bytes 1024 | tf_op jit(solution)/shard_map/pallas_call | solution.py:660
  264.5 4.4 collective-permute-done.27.recv
  272.8 4.9 %shard_map.171 = (f32[1024,1024]{1,0:T(8,128)S(1)}, bf16[1024,1024]{1,0:T(8,128)(2,1)S(1)}, f32[2,1024]{1,0:T(2,128)S(1)}) custom-call(f32[1024,1024]{1,0:T(8,128)S(1)} %copy-done.6, bf16[1024,1024]{1,0:T(8,128)(2,1)S(1)} %copy-done.17, bf16[1024,1024]{1,0:T(8,128)(2,1)} %collective-permute-done.27.recv, bf16[1024,1024]{1,0:T(8,128)(2,1)S(1)} %copy-done.1, ...), custom_call_target="tpu_custom_call" | custom-call | flops 1024 | bytes 1024 | tf_op jit(solution)/shard_map/pallas_call | solution.py:722
  280.3 3.9 collective-permute-done.29.db
  284.2 8.3 %shard_map.172 = (bf16[2048,512]{1,0:T(8,128)(2,1)S(1)}, bf16[1024,512]{1,0:T(8,128)(2,1)S(1)}) custom-call(s32[1]{0:T(128)} %bitcast.core, bf16[1024,1024]{1,0:T(8,128)(2,1)} %copy-done.21, bf16[1024,1024]{1,0:T(8,128)(2,1)} %collective-permute-done.29.db, bf16[2048,256]{1,0:T(8,128)(2,1)S(1)} %get-tuple-element.114.oa, bf16[2048,256]{1,0:T(8,128)(2,1)S(1)} %copy-done.10, ...), custom_call_target="tpu_custom_call" | custom-call | flops 1024 | bytes 1024 | tf_op jit(solution)/shard_map/pallas_call | solution.py:772
  297.5 35.2 %shard_map.173 = (bf16[2048,512]{1,0:T(8,128)(2,1)S(1)}, bf16[2048,512]{1,0:T(8,128)(2,1)S(1)}, bf16[2048,512]{1,0:T(8,128)(2,1)}) custom-call(f32[4]{0:T(128)S(1)} %exponential_multiply_fusion.slopes, bf16[2048,1536]{1,0:T(8,128)(2,1)} %get-tuple-element.132.q_ref.k_ref.v_ref, bf16[2048,1536]{1,0:T(8,128)(2,1)} %get-tuple-element.132.q_ref.k_ref.v_ref, ...), custom_call_target="tpu_custom_call" | custom-call | flops 1024 | bytes 1024 | tf_op jit(solution)/shard_map/pallas_call | solution.py:462
  335.3 12.5 %shard_map.174 = (bf16[1024,1024]{1,0:T(8,128)(2,1)}, f32[1024,1024]{1,0:T(8,128)}) custom-call(s32[1]{0:T(128)} %bitcast.core, bf16[2048,512]{1,0:T(8,128)(2,1)} %copy-done.12, bf16[2048,512]{1,0:T(8,128)(2,1)} %copy-done.13, bf16[2048,512]{1,0:T(8,128)(2,1)} %get-tuple-element.140.refs_2_, bf16[8,128,2176]{2,1,0:T(8,128)(2,1)} %shard_map.161.w.refs_3_), custom_call_target="tpu_custom_call" | custom-call | flops 1024 | bytes 1024 | tf_op jit(solution)/shard_map/pallas_call | solution.py:858
  354.5 13.3 %shard_map.175 = bf16[1024,2048]{1,0:T(8,128)(2,1)} custom-call(bf16[2048,1024]{1,0:T(8,128)(2,1)} %get-tuple-element.142.a1, bf16[1024,512]{1,0:T(8,128)(2,1)} %copy-done.22, bf16[2048,512]{1,0:T(8,128)(2,1)} %copy-done.12, bf16[2048,512]{1,0:T(8,128)(2,1)} %copy-done.13, bf16[2048,512]{1,0:T(8,128)(2,1)} %get-tuple-element.140.refs_2_), custom_call_target="tpu_custom_call" | custom-call | flops 1024 | bytes 1024 | tf_op jit(solution)/shard_map/pallas_call | solution.py:807
  371.8 11.0 %collective-permute-done.32 = bf16[64,2048]{1,0:T(8,128)(2,1)} collective-permute-done((bf16[64,2048]{1,0:T(8,128)(2,1)}, bf16[64,2048]{1,0:T(8,128)(2,1)}, u32[]{:S(2)}, u32[]{:S(2)}) %collective-permute-start.32) | collective-permute-done | bytes 262176 | tf_op jit(solution)/shard_map/ppermute | solution.py:898
  389.8 3.5 shard_map.176
  402.0 9.3 %collective-permute-done.37 = bf16[128,2048]{1,0:T(8,128)(2,1)S(1)} collective-permute-done((bf16[128,2048]{1,0:T(8,128)(2,1)S(1)}, bf16[128,2048]{1,0:T(8,128)(2,1)S(1)}, u32[]{:S(2)}, u32[]{:S(2)}) %collective-permute-start.37) | collective-permute-done | bytes 524320 | tf_op jit(solution)/shard_map/ppermute | solution.py:898
  420.7 7.2 %collective-permute-done.49 = f32[4,1024]{1,0:T(4,128)S(1)} collective-permute-done((f32[4,1024]{1,0:T(4,128)S(1)}, f32[4,1024]{1,0:T(4,128)S(1)}, u32[]{:S(2)}, u32[]{:S(2)}) %collective-permute-start.49) | collective-permute-done | bytes 16416 | tf_op jit(solution)/shard_map/ppermute | solution.py:898
  427.9 3.7 collective-permute-done.50
  432.9 3.4 collective-permute-done.51
  437.0 3.8 fusion.5
  445.6 5.8 %collective-permute-done.41 = bf16[128,2048]{1,0:T(8,128)(2,1)S(1)} collective-permute-done((bf16[128,2048]{1,0:T(8,128)(2,1)}, bf16[128,2048]{1,0:T(8,128)(2,1)S(1)}, u32[]{:S(2)}, u32[]{:S(2)}) %collective-permute-start.41) | collective-permute-done | bytes 524320 | tf_op jit(solution)/shard_map/ppermute | solution.py:898
  456.3 6.9 %collective-permute-done.46 = bf16[64,2048]{1,0:T(8,128)(2,1)S(1)} collective-permute-done((bf16[64,2048]{1,0:T(8,128)(2,1)S(1)}, bf16[64,2048]{1,0:T(8,128)(2,1)S(1)}, u32[]{:S(2)}, u32[]{:S(2)}) %collective-permute-start.46) | collective-permute-done | bytes 262176 | tf_op jit(solution)/shard_map/ppermute | solution.py:898
  464.1 4.3 collective-permute-done.44
  (254 shorter events, 124.8 us)
Async XLA Ops:
  8.0 210.1 %all-gather.3.cloned.1.call-start = ((), (), s32[]{:S(2)}) async-start(), calls=%async_computation.4 | async-start | bytes 8650752 | tf_op jit(solution)/shard_map/all_gather | solution.py:994
  22.4 51.7 %collective-permute-start.1 = (bf16[1024,1024]{1,0:T(8,128)(2,1)S(1)}, bf16[1024,1024]{1,0:T(8,128)(2,1)}, u32[]{:S(2)}, u32[]{:S(2)}) collective-permute-start(bf16[1024,1024]{1,0:T(8,128)(2,1)S(1)} %bitcast.80), channel_id=1, source_target_pairs={{1,2},{2,1},{5,6},{6,5},{9,10},{10,9},{13,14},{14,13},{17,18},{18,... | collective-permute-start | bytes 6291464 | tf_op jit(solution)/shard_map/ppermute | solution.py:898
  26.2 14.8 %collective-permute-start.3 = (bf16[128,2176]{1,0:T(8,128)(2,1)S(1)}, bf16[128,2176]{1,0:T(8,128)(2,1)S(1)}, u32[]{:S(2)}, u32[]{:S(2)}) collective-permute-start(bf16[128,2176]{1,0:T(8,128)(2,1)S(1)} %maximum_select_fusion.refs_0_), channel_id=1, source_target_pairs={{0,8},{1,9},{2,10},{3,11},{4,0},{5,1},{6,2},{7,3},{8,16},{9,17},{1... | collective-permute-start | bytes 1671176 | tf_op jit(solution)/shard_map/ppermute | solution.py:898
  28.1 15.2 %collective-permute-start.4 = (bf16[128,2176]{1,0:T(8,128)(2,1)S(1)}, bf16[128,2176]{1,0:T(8,128)(2,1)S(1)}, u32[]{:S(2)}, u32[]{:S(2)}) collective-permute-start(bf16[128,2176]{1,0:T(8,128)(2,1)S(1)} %maximum_select_fusion.refs_0_), channel_id=1, source_target_pairs={{0,4},{1,5},{2,6},{3,7},{4,12},{5,13},{6,14},{7,15},{8,0},{9,1},{1... | collective-permute-start | bytes 1671176 | tf_op jit(solution)/shard_map/ppermute | solution.py:898
  43.2 14.7 %collective-permute-start.5 = (bf16[128,2176]{1,0:T(8,128)(2,1)S(1)}, bf16[128,2176]{1,0:T(8,128)(2,1)S(1)}, u32[]{:S(2)}, u32[]{:S(2)}) collective-permute-start(bf16[128,2176]{1,0:T(8,128)(2,1)S(1)} %collective-permute-done.3.refs_1_), channel_id=1, source_target_pairs={{0,8},{1,9},{2,10},{3,11},{4,0},{5,1},{6,2},{7,3},{8,16},{9,17},{1... | collective-permute-start | bytes 1671176 | tf_op jit(solution)/shard_map/ppermute | solution.py:898
  44.8 14.4 %collective-permute-start.6 = (bf16[128,2176]{1,0:T(8,128)(2,1)S(1)}, bf16[128,2176]{1,0:T(8,128)(2,1)S(1)}, u32[]{:S(2)}, u32[]{:S(2)}) collective-permute-start(bf16[128,2176]{1,0:T(8,128)(2,1)S(1)} %collective-permute-done.4.refs_2_), channel_id=1, source_target_pairs={{0,4},{1,5},{2,6},{3,7},{4,12},{5,13},{6,14},{7,15},{8,0},{9,1},{1... | collective-permute-start | bytes 1671176 | tf_op jit(solution)/shard_map/ppermute | solution.py:898
  75.2 23.0 %collective-permute-start.13 = (bf16[1024,1024]{1,0:T(8,128)(2,1)S(1)}, bf16[1024,1024]{1,0:T(8,128)(2,1)}, u32[]{:S(2)}, u32[]{:S(2)}) collective-permute-start(bf16[1024,1024]{1,0:T(8,128)(2,1)S(1)} %broadcast_select_fusion.2.xa.x_ref.r_0_), channel_id=1, source_target_pairs={{0,2},{1,3},{2,0},{3,1},{4,6},{5,7},{6,4},{7,5},{8,10},{9,11},{10,... | collective-permute-start | bytes 6291464 | tf_op jit(solution)/shard_map/ppermute | solution.py:898
  85.7 27.8 %collective-permute-start.16 = (bf16[1024,1024]{1,0:T(8,128)(2,1)}, bf16[1024,1024]{1,0:T(8,128)(2,1)}, u32[]{:S(2)}, u32[]{:S(2)}) collective-permute-start(bf16[1024,1024]{1,0:T(8,128)(2,1)} %bitcast.11), channel_id=1, source_target_pairs={{1,2},{2,1},{5,6},{6,5},{9,10},{10,9},{13,14},{14,13},{17,18},{18,... | collective-permute-start | bytes 6291464 | tf_op jit(solution)/shard_map/ppermute | solution.py:898
  87.7 25.5 %collective-permute-start.17 = (s32[1,2048]{1,0:T(1,128)S(1)}, s32[1,2048]{1,0:T(1,128)S(1)}, u32[]{:S(2)}, u32[]{:S(2)}) collective-permute-start(s32[1,2048]{1,0:T(1,128)S(1)} %copy-done.45), channel_id=1, source_target_pairs={{0,2},{1,3},{2,0},{3,1},{4,6},{5,7},{6,4},{7,5},{8,10},{9,11},{10,... | collective-permute-start | bytes 24584 | tf_op jit(solution)/shard_map/ppermute | solution.py:898
  87.9 23.1 %collective-permute-start.14 = (bf16[128,2048]{1,0:T(8,128)(2,1)S(1)}, bf16[128,2048]{1,0:T(8,128)(2,1)}, u32[]{:S(2)}, u32[]{:S(2)}) collective-permute-start(bf16[128,2048]{1,0:T(8,128)(2,1)S(1)} %maximum_select_fusion.1.refs_0_), channel_id=1, source_target_pairs={{0,8},{1,9},{2,10},{3,11},{4,0},{5,1},{6,2},{7,3},{8,16},{9,17},{1... | collective-permute-start | bytes 1572872 | tf_op jit(solution)/shard_map/ppermute | solution.py:898
  88.7 22.2 %collective-permute-start.15 = (bf16[128,2048]{1,0:T(8,128)(2,1)S(1)}, bf16[128,2048]{1,0:T(8,128)(2,1)}, u32[]{:S(2)}, u32[]{:S(2)}) collective-permute-start(bf16[128,2048]{1,0:T(8,128)(2,1)S(1)} %maximum_select_fusion.1.refs_0_), channel_id=1, source_target_pairs={{0,4},{1,5},{2,6},{3,7},{4,12},{5,13},{6,14},{7,15},{8,0},{9,1},{1... | collective-permute-start | bytes 1572872 | tf_op jit(solution)/shard_map/ppermute | solution.py:898
  111.0 15.1 %collective-permute-start.18 = (bf16[128,2048]{1,0:T(8,128)(2,1)}, bf16[128,2048]{1,0:T(8,128)(2,1)}, u32[]{:S(2)}, u32[]{:S(2)}) collective-permute-start(bf16[128,2048]{1,0:T(8,128)(2,1)} %collective-permute-done.14.refs_1_), channel_id=1, source_target_pairs={{0,8},{1,9},{2,10},{3,11},{4,0},{5,1},{6,2},{7,3},{8,16},{9,17},{1... | collective-permute-start | bytes 1572872 | tf_op jit(solution)/shard_map/ppermute | solution.py:898
  126.1 209.2 %reduce-scatter.3.cloned.1.call-start = ((), (), s32[]{:S(2)}) async-start(), calls=%async_computation.2 | async-start | bytes 4718592 | tf_op jit(solution)/shard_map/reduce_scatter | solution.py:963
  126.2 17.0 %collective-permute-start.20 = (bf16[128,2048]{1,0:T(8,128)(2,1)}, bf16[128,2048]{1,0:T(8,128)(2,1)S(1)}, u32[]{:S(2)}, u32[]{:S(2)}) collective-permute-start(bf16[128,2048]{1,0:T(8,128)(2,1)} %collective-permute-done.18.refs_3_), channel_id=1, source_target_pairs={{0,8},{1,9},{2,10},{3,11},{4,0},{5,1},{6,2},{7,3},{8,16},{9,17},{1... | collective-permute-start | bytes 1572872 | tf_op jit(solution)/shard_map/ppermute | solution.py:898
  127.0 18.6 %collective-permute-start.21 = (bf16[128,2048]{1,0:T(8,128)(2,1)}, bf16[128,2048]{1,0:T(8,128)(2,1)S(1)}, u32[]{:S(2)}, u32[]{:S(2)}) collective-permute-start(bf16[128,2048]{1,0:T(8,128)(2,1)} %collective-permute-done.19.refs_4_), channel_id=1, source_target_pairs={{0,4},{1,5},{2,6},{3,7},{4,12},{5,13},{6,14},{7,15},{8,0},{9,1},{1... | collective-permute-start | bytes 1572872 | tf_op jit(solution)/shard_map/ppermute | solution.py:898
  149.6 26.9 %collective-permute-start.24 = (bf16[1024,1024]{1,0:T(8,128)(2,1)}, bf16[1024,1024]{1,0:T(8,128)(2,1)}, u32[]{:S(2)}, u32[]{:S(2)}) collective-permute-start(bf16[1024,1024]{1,0:T(8,128)(2,1)} %shard_map.167), channel_id=1, source_target_pairs={{0,2},{1,3},{2,0},{3,1},{4,6},{5,7},{6,4},{7,5},{8,10},{9,11},{10,... | collective-permute-start | bytes 6291464 | tf_op jit(solution)/shard_map/ppermute | solution.py:898
  149.6 17.7 %collective-permute-start.22 = (bf16[64,2048]{1,0:T(8,128)(2,1)S(1)}, bf16[64,2048]{1,0:T(8,128)(2,1)S(1)}, u32[]{:S(2)}, u32[]{:S(2)}) collective-permute-start(bf16[64,2048]{1,0:T(8,128)(2,1)S(1)} %slice.140), channel_id=1, source_target_pairs={{0,4},{1,5},{2,6},{3,7},{4,12},{5,13},{6,14},{7,15},{8,0},{9,1},{1... | collective-permute-start | bytes 786440 | tf_op jit(solution)/shard_map/ppermute | solution.py:898
  149.6 17.7 %collective-permute-start.23 = (bf16[64,2048]{1,0:T(8,128)(2,1)S(1)}, bf16[64,2048]{1,0:T(8,128)(2,1)}, u32[]{:S(2)}, u32[]{:S(2)}) collective-permute-start(bf16[64,2048]{1,0:T(8,128)(2,1)S(1)} %slice.139), channel_id=1, source_target_pairs={{0,8},{1,9},{2,10},{3,11},{4,0},{5,1},{6,2},{7,3},{8,16},{9,17},{1... | collective-permute-start | bytes 786440 | tf_op jit(solution)/shard_map/ppermute | solution.py:898
  151.6 32.7 %collective-permute-start.26 = (bf16[1024,1024]{1,0:T(8,128)(2,1)S(1)}, bf16[1024,1024]{1,0:T(8,128)(2,1)}, u32[]{:S(2)}, u32[]{:S(2)}) collective-permute-start(bf16[1024,1024]{1,0:T(8,128)(2,1)S(1)} %broadcast_select_fusion.1.ya.skip), channel_id=1, source_target_pairs={{0,2},{1,3},{2,0},{3,1},{4,6},{5,7},{6,4},{7,5},{8,10},{9,11},{10,... | collective-permute-start | bytes 6291464 | tf_op jit(solution)/shard_map/ppermute | solution.py:898
  217.7 225.1 %reduce-scatter.5.cloned.1.call-start = ((), (), s32[]{:S(2)}) async-start(), calls=%async_computation.3 | async-start | bytes 4718592 | tf_op jit(solution)/shard_map/reduce_scatter | solution.py:963
  277.8 17.2 %collective-permute-start.28 = (bf16[1024,1024]{1,0:T(8,128)(2,1)}, bf16[1024,1024]{1,0:T(8,128)(2,1)S(1)}, u32[]{:S(2)}, u32[]{:S(2)}) collective-permute-start(bf16[1024,1024]{1,0:T(8,128)(2,1)} %get-tuple-element.128), channel_id=1, source_target_pairs={{0,2},{1,3},{2,0},{3,1},{4,6},{5,7},{6,4},{7,5},{8,10},{9,11},{10,... | collective-permute-start | bytes 6291464 | tf_op jit(solution)/shard_map/ppermute | solution.py:898
  347.9 36.7 %collective-permute-start.33 = (bf16[1024,1024]{1,0:T(8,128)(2,1)}, bf16[1024,1024]{1,0:T(8,128)(2,1)S(1)}, u32[]{:S(2)}, u32[]{:S(2)}) collective-permute-start(bf16[1024,1024]{1,0:T(8,128)(2,1)} %get-tuple-element.149), channel_id=1, source_target_pairs={{0,2},{1,3},{2,0},{3,1},{4,6},{5,7},{6,4},{7,5},{8,10},{9,11},{10,... | collective-permute-start | bytes 6291464 | tf_op jit(solution)/shard_map/ppermute | solution.py:898
  349.2 49.8 %collective-permute-start.30 = (bf16[1024,1024]{1,0:T(8,128)(2,1)}, bf16[1024,1024]{1,0:T(8,128)(2,1)}, u32[]{:S(2)}, u32[]{:S(2)}) collective-permute-start(bf16[1024,1024]{1,0:T(8,128)(2,1)} %add_convert_fusion), channel_id=1, source_target_pairs={{1,2},{2,1},{5,6},{6,5},{9,10},{10,9},{13,14},{14,13},{17,18},{18,... | collective-permute-start | bytes 6291464 | tf_op jit(solution)/shard_map/ppermute | solution.py:898
  353.5 29.2 %collective-permute-start.32 = (bf16[64,2048]{1,0:T(8,128)(2,1)}, bf16[64,2048]{1,0:T(8,128)(2,1)}, u32[]{:S(2)}, u32[]{:S(2)}) collective-permute-start(bf16[64,2048]{1,0:T(8,128)(2,1)} %fusion.8), channel_id=1, source_target_pairs={{0,1},{1,0},{2,3},{3,2},{4,5},{5,4},{6,7},{7,6},{8,9},{9,8},{10,11... | collective-permute-start | bytes 786440 | tf_op jit(solution)/shard_map/ppermute | solution.py:898
  369.7 25.9 %collective-permute-start.35 = (bf16[64,2048]{1,0:T(8,128)(2,1)S(1)}, bf16[64,2048]{1,0:T(8,128)(2,1)S(1)}, u32[]{:S(2)}, u32[]{:S(2)}) collective-permute-start(bf16[64,2048]{1,0:T(8,128)(2,1)S(1)} %get-tuple-element.145), channel_id=1, source_target_pairs={{0,8},{1,9},{2,10},{3,11},{4,0},{5,1},{6,2},{7,3},{8,16},{9,17},{1... | collective-permute-start | bytes 786440 | tf_op jit(solution)/shard_map/ppermute | solution.py:898
  369.7 25.8 %collective-permute-start.36 = (bf16[64,2048]{1,0:T(8,128)(2,1)S(1)}, bf16[64,2048]{1,0:T(8,128)(2,1)S(1)}, u32[]{:S(2)}, u32[]{:S(2)}) collective-permute-start(bf16[64,2048]{1,0:T(8,128)(2,1)S(1)} %get-tuple-element.146), channel_id=1, source_target_pairs={{0,4},{1,5},{2,6},{3,7},{4,12},{5,13},{6,14},{7,15},{8,0},{9,1},{1... | collective-permute-start | bytes 786440 | tf_op jit(solution)/shard_map/ppermute | solution.py:898
  393.3 43.6 %collective-permute-start.34 = (bf16[1024,1024]{1,0:T(8,128)(2,1)S(1)}, bf16[1024,1024]{1,0:T(8,128)(2,1)}, u32[]{:S(2)}, u32[]{:S(2)}) collective-permute-start(bf16[1024,1024]{1,0:T(8,128)(2,1)S(1)} %get-tuple-element.151), channel_id=1, source_target_pairs={{1,2},{2,1},{5,6},{6,5},{9,10},{10,9},{13,14},{14,13},{17,18},{18,... | collective-permute-start | bytes 6291464 | tf_op jit(solution)/shard_map/ppermute | solution.py:898
  396.9 14.4 %collective-permute-start.37 = (bf16[128,2048]{1,0:T(8,128)(2,1)S(1)}, bf16[128,2048]{1,0:T(8,128)(2,1)S(1)}, u32[]{:S(2)}, u32[]{:S(2)}) collective-permute-start(bf16[128,2048]{1,0:T(8,128)(2,1)S(1)} %get-tuple-element.183), channel_id=1, source_target_pairs={{0,8},{1,9},{2,10},{3,11},{4,0},{5,1},{6,2},{7,3},{8,16},{9,17},{1... | collective-permute-start | bytes 1572872 | tf_op jit(solution)/shard_map/ppermute | solution.py:898
  397.0 14.4 %collective-permute-start.38 = (bf16[128,2048]{1,0:T(8,128)(2,1)S(1)}, bf16[128,2048]{1,0:T(8,128)(2,1)S(1)}, u32[]{:S(2)}, u32[]{:S(2)}) collective-permute-start(bf16[128,2048]{1,0:T(8,128)(2,1)S(1)} %get-tuple-element.182), channel_id=1, source_target_pairs={{0,4},{1,5},{2,6},{3,7},{4,12},{5,13},{6,14},{7,15},{8,0},{9,1},{1... | collective-permute-start | bytes 1572872 | tf_op jit(solution)/shard_map/ppermute | solution.py:898
  400.6 18.6 %collective-permute-start.48 = (f32[4,1024]{1,0:T(4,128)S(1)}, f32[4,1024]{1,0:T(4,128)S(1)}, u32[]{:S(2)}, u32[]{:S(2)}) collective-permute-start(f32[4,1024]{1,0:T(4,128)S(1)} %fusion.14), channel_id=1, source_target_pairs={{0,1},{1,0},{2,3},{3,2},{4,5},{5,4},{6,7},{7,6},{8,9},{9,8},{10,11... | collective-permute-start | bytes 49160 | tf_op jit(solution)/shard_map/ppermute | solution.py:898
  413.8 23.1 %collective-permute-start.39 = (bf16[128,2048]{1,0:T(8,128)(2,1)}, bf16[128,2048]{1,0:T(8,128)(2,1)S(1)}, u32[]{:S(2)}, u32[]{:S(2)}) collective-permute-start(bf16[128,2048]{1,0:T(8,128)(2,1)} %get-tuple-element.181), channel_id=1, source_target_pairs={{0,8},{1,9},{2,10},{3,11},{4,0},{5,1},{6,2},{7,3},{8,16},{9,17},{1... | collective-permute-start | bytes 1572872 | tf_op jit(solution)/shard_map/ppermute | solution.py:898
  415.6 21.4 %collective-permute-start.40 = (bf16[128,2048]{1,0:T(8,128)(2,1)S(1)}, bf16[128,2048]{1,0:T(8,128)(2,1)}, u32[]{:S(2)}, u32[]{:S(2)}) collective-permute-start(bf16[128,2048]{1,0:T(8,128)(2,1)S(1)} %get-tuple-element.180), channel_id=1, source_target_pairs={{0,4},{1,5},{2,6},{3,7},{4,12},{5,13},{6,14},{7,15},{8,0},{9,1},{1... | collective-permute-start | bytes 1572872 | tf_op jit(solution)/shard_map/ppermute | solution.py:898
  (69 other events, 707.2 us)
Sparse Core Ops, SparseCore 0:
  126.2 78.2 all-gather.2
Sparse Core Ops, SparseCore 1:
  217.8 86.4 reduce-scatter.2
  308.1 87.4 reduce-scatter.4

commit v4 on v3

--- a/solution.py
+++ b/solution.py
@@ -1013,7 +1013,6 @@
     f_recv = send(after(f_oth, da_own), to_core)
     do, gwo = head_grad(core_arg, da_own, da_oth, mixed, wa)
     result = (h1 + f_own.astype(F32) + after(f_recv, do).astype(F32)).astype(BF)
-    cross_result = send(result, back)
     both_mixed = jnp.concatenate(mixed, axis=1)
     both_logs = jnp.concatenate([logs0, logs1], axis=0)
     grads = attend_back(slopes, after(qkv, do, result), do, both_mixed, both_logs, seg)
@@ -1021,6 +1020,7 @@
     d1_recv = send(d1_oth, to_core)
     grad_back = to_owner(after(r2, d1_own).astype(F32))
     gwq = project_weight(after(a1, d1_own), gwo, grads)
+    cross_result = send(after(result, grad_back), back)
     result = jnp.where(at_home, result, after(cross_result, gwq))
     rc = Reduce(gwq.reshape(chips, width // chips, -1))
     sent = rc.step(1)
@@ -1030,7 +1030,7 @@
     sent = rc.step(3, result)
     sent = rc.step(4, cross_tokens)
     grad_in = to_owner(after(r1, *sent).astype(F32))
-    sums = jnp.concatenate([sums1[0:1], sums2[0:1], sums1[1:2], sums2[1:2]], axis=0)
+    sums = after(jnp.concatenate([sums1[0:1], sums2[0:1], sums1[1:2], sums2[1:2]], axis=0), *sent)
     for pairs in (to_core, to_y, *hops):
         sums = sums + send(sums, pairs)
     r3 = to_owner(rc.total())

time: 487 us -> 491 us (level)
  transfers between devices with their start and end apart: 55 -> 55, of which waited for: 28 -> 29; matrix products, arithmetic and copies ran while one was open for 7% -> 7% of each run, Pallas kernels for 44% -> 44%
where the time goes in v4:
time: 491 us; the launch traced here: 482 us
  Pallas kernels  214 us (44%)
  waiting for transfers between devices  146 us (30%)
  starting transfers between devices  47.8 us (10%)
  other arithmetic  31.8 us (6%)
  local copies, waits for them, and re-layouts  26.7 us (5%)
  between operations  16.5 us (3%)
    ppermute x52, waiting for transfers between devices, send(): return lax.ppermute(v, both, pairs)  146 us
    ppermute x52, starting transfers between devices, send(): return lax.ppermute(v, both, pairs)  47.3 us
    pallas_call x1, Pallas kernels, down(): pl.pallas_call(down_kernel, grid_spec=spec, out_shape=[jax.ShapeDtypeStru...  46.1 us
    pallas_call x1, Pallas kernels, attend_back(): pl.pallas_call(attend_back_kernel, grid_spec=spec, out_shape=[jax.ShapeDt...  35.2 us
    pallas_call x1, Pallas kernels, up(): pl.pallas_call(up_kernel, grid_spec=spec, out_shape=[jax.ShapeDtypeStruct...  29.2 us
    pallas_call x2, Pallas kernels, attend(): pl.pallas_call(attend_kernel, grid_spec=spec, out_shape=[jax.ShapeDtypeSt...  25.1 us
    unnamed x93, local copies, waits for them, and re-layouts  20.7 us
    pallas_call x1, Pallas kernels, project_weight(): pl.pallas_call(project_weight_kernel, grid=(rows2 // tile,), in_specs=[pl...  13.3 us
  transfers between devices with their start and end apart: 55, of which 29 were waited for; matrix products, arithmetic and copies ran while one was open for 7% of the time, Pallas kernels for 44%

profile of v4, /device:TPU:0, one launch (start us, length us, event | category | flops | bytes accessed | tf_op | source)
XLA Modules:
  0.0 482.0 jit_solution(5530315330070481195)
XLA Ops:
  14.9 6.7 %collective-permute-done = bf16[64,2176]{1,0:T(8,128)(2,1)S(1)} collective-permute-done((bf16[64,2176]{1,0:T(8,128)(2,1)S(1)}, bf16[64,2176]{1,0:T(8,128)(2,1)S(1)}, u32[]{:S(2)}, u32[]{:S(2)}) %collective-permute-start) | collective-permute-done | bytes 278560 | tf_op jit(solution)/shard_map/ppermute | solution.py:898
  26.5 12.6 %collective-permute-done.3.refs_1_ = bf16[128,2176]{1,0:T(8,128)(2,1)S(1)} collective-permute-done((bf16[128,2176]{1,0:T(8,128)(2,1)S(1)}, bf16[128,2176]{1,0:T(8,128)(2,1)S(1)}, u32[]{:S(2)}, u32[]{:S(2)}) %collective-permute-start.3) | collective-permute-done | bytes 557088 | tf_op jit(solution)/shard_map/ppermute | solution.py:898
  43.5 12.6 %collective-permute-done.5.refs_3_ = bf16[128,2176]{1,0:T(8,128)(2,1)S(1)} collective-permute-done((bf16[128,2176]{1,0:T(8,128)(2,1)S(1)}, bf16[128,2176]{1,0:T(8,128)(2,1)S(1)}, u32[]{:S(2)}, u32[]{:S(2)}) %collective-permute-start.5) | collective-permute-done | bytes 557088 | tf_op jit(solution)/shard_map/ppermute | solution.py:898
  59.6 11.3 %collective-permute-done.7.refs_5_ = bf16[128,2176]{1,0:T(8,128)(2,1)S(1)} collective-permute-done((bf16[128,2176]{1,0:T(8,128)(2,1)S(1)}, bf16[128,2176]{1,0:T(8,128)(2,1)S(1)}, u32[]{:S(2)}, u32[]{:S(2)}) %collective-permute-start.7) | collective-permute-done | bytes 557088 | tf_op jit(solution)/shard_map/ppermute | solution.py:898
  78.1 5.2 %collective-permute-done.11.refs_7_ = bf16[64,2176]{1,0:T(8,128)(2,1)S(1)} collective-permute-done((bf16[64,2176]{1,0:T(8,128)(2,1)S(1)}, bf16[64,2176]{1,0:T(8,128)(2,1)S(1)}, u32[]{:S(2)}, u32[]{:S(2)}) %collective-permute-start.11) | collective-permute-done | bytes 278560 | tf_op jit(solution)/shard_map/ppermute | solution.py:898
  90.5 5.1 %shard_map.161.w.refs_3_ = bf16[8,128,2176]{2,1,0:T(8,128)(2,1)} custom-call(s32[8]{0:T(128)} %get-tuple-element.204.order, bf16[128,2176]{1,0:T(8,128)(2,1)} %copy-done.23, bf16[128,2176]{1,0:T(8,128)(2,1)} %copy-done.36, bf16[128,2176]{1,0:T(8,128)(2,1)} %copy-done.37, bf16[128,2176]{1,0:T(8,128)(2,1)} %copy-done.38, bf16[128,2176]{1,0:T(8,128)(2,1)} %copy-done.39, ...), custom_call_target="tpu_custom_call" | custom-call | flops 1024 | bytes 1024 | tf_op jit(solution)/shard_map/pallas_call | solution.py:693
  96.8 12.9 %shard_map.162 = (bf16[2048,1024]{1,0:T(8,128)(2,1)}, bf16[2048,1536]{1,0:T(8,128)(2,1)}) custom-call(s32[1]{0:T(128)} %bitcast.core, bf16[1024,1024]{1,0:T(8,128)(2,1)S(1)} %broadcast_select_fusion.2.xa.x_ref.r_0_, bf16[1024,1024]{1,0:T(8,128)(2,1)} %collective-permute-done.13.xb, f32[4,1024]{1,0:T(4,128)S(1)} %bitcast.68, ...), custom_call_target="tpu_custom_call" | custom-call | flops 1024 | bytes 1024 | tf_op jit(solution)/shard_map/pallas_call | solution.py:327
  112.2 12.6 %shard_map.163 = (bf16[2048,256]{1,0:T(8,128)(2,1)S(1)}, f32[2,1,2048]{2,1,0:T(1,128)S(1)}) custom-call(f32[2]{0:T(128)S(1)} %get-tuple-element.216.slopes, bf16[2048,1536]{1,0:T(8,128)(2,1)} %get-tuple-element.133.q_ref.k_ref.v_ref, bf16[2048,1536]{1,0:T(8,128)(2,1)} %get-tuple-element.133.q_ref.k_ref.v_ref, ...), custom_call_target="tpu_custom_call" | custom-call | flops 1024 | bytes 1024 | tf_op jit(solution)/shard_map/pallas_call | solution.py:392
  127.1 12.6 %shard_map.164 = (bf16[2048,256]{1,0:T(8,128)(2,1)S(1)}, f32[2,1,2048]{2,1,0:T(1,128)S(1)}) custom-call(f32[2]{0:T(128)S(1)} %get-tuple-element.215.slopes, bf16[2048,1536]{1,0:T(8,128)(2,1)} %get-tuple-element.133.q_ref.k_ref.v_ref, bf16[2048,1536]{1,0:T(8,128)(2,1)} %get-tuple-element.133.q_ref.k_ref.v_ref, ...), custom_call_target="tpu_custom_call" | custom-call | flops 1024 | bytes 1024 | tf_op jit(solution)/shard_map/pallas_call | solution.py:392
  145.0 3.9 shard_map.167
  150.9 15.5 %collective-permute-done.22.refs_8_ = bf16[64,2048]{1,0:T(8,128)(2,1)S(1)} collective-permute-done((bf16[64,2048]{1,0:T(8,128)(2,1)S(1)}, bf16[64,2048]{1,0:T(8,128)(2,1)S(1)}, u32[]{:S(2)}, u32[]{:S(2)}) %collective-permute-start.22) | collective-permute-done | bytes 262176 | tf_op jit(solution)/shard_map/ppermute | solution.py:898
  166.4 4.1 shard_map.165.part
  170.5 5.2 %shard_map.166.w_ref.w1_ref = bf16[8,128,2048]{2,1,0:T(8,128)(2,1)} custom-call(s32[8]{0:T(128)} %get-tuple-element.204.order, bf16[128,2048]{1,0:T(8,128)(2,1)} %copy-done.31, bf16[128,2048]{1,0:T(8,128)(2,1)} %collective-permute-done.14.refs_1_, bf16[128,2048]{1,0:T(8,128)(2,1)} %collective-permute-done.15.refs_2_, ...), custom_call_target="tpu_custom_call" | custom-call | flops 1024 | bytes 1024 | tf_op jit(solution)/shard_map/pallas_call | solution.py:693
  178.0 3.3 shard_map.168
  187.7 29.2 %shard_map.169 = (bf16[2048,2048]{1,0:T(8,128)(2,1)}, bf16[2048,2048]{1,0:T(8,128)(2,1)}, bf16[8,128,2048]{2,1,0:T(8,128)(2,1)}) custom-call(s32[1]{0:T(128)} %bitcast.core, bf16[1024,1024]{1,0:T(8,128)(2,1)} %copy-done.11, bf16[1024,1024]{1,0:T(8,128)(2,1)} %collective-permute-done.25.ab, bf16[1024,1024]{1,0:T(8,128)(2,1)} %copy-done, ...), custom_call_target="tpu_custom_call" | custom-call | flops 1024 | bytes 1024 | tf_op jit(solution)/shard_map/pallas_call | solution.py:602
  217.4 46.1 %shard_map.170 = (bf16[1024,1024]{1,0:T(8,128)(2,1)}, bf16[1024,1024]{1,0:T(8,128)(2,1)}, bf16[1024,1024]{1,0:T(8,128)(2,1)}, bf16[1024,1024]{1,0:T(8,128)(2,1)}, bf16[8,128,2048]{2,1,0:T(8,128)(2,1)}) custom-call(s32[1]{0:T(128)} %bitcast.core, bf16[1024,1024]{1,0:T(8,128)(2,1)} %copy-done.11, bf16[1024,1024]{1,0:T(8,128)(2,1)} %collective-permute-done.25.ab, ...), custom_call_target="tpu_custom_call" | custom-call | flops 1024 | bytes 1024 | tf_op jit(solution)/shard_map/pallas_call | solution.py:660
  263.6 4.3 collective-permute-done.27.recv
  271.8 4.4 shard_map.171
  282.7 8.6 %shard_map.172 = (bf16[2048,512]{1,0:T(8,128)(2,1)S(1)}, bf16[1024,512]{1,0:T(8,128)(2,1)S(1)}) custom-call(s32[1]{0:T(128)} %bitcast.core, bf16[1024,1024]{1,0:T(8,128)(2,1)} %get-tuple-element.129.da, bf16[1024,1024]{1,0:T(8,128)(2,1)} %collective-permute-done.29.db, bf16[2048,256]{1,0:T(8,128)(2,1)S(1)} %get-tuple-element.116.oa, ...), custom_call_target="tpu_custom_call" | custom-call | flops 1024 | bytes 1024 | tf_op jit(solution)/shard_map/pallas_call | solution.py:772
  291.4 5.2 %add_convert_fusion = bf16[1024,1024]{1,0:T(8,128)(2,1)} fusion(bf16[1024,1024]{1,0:T(8,128)(2,1)} %collective-permute-done.28, f32[1024,1024]{1,0:T(8,128)S(1)} %copy-done.7, bf16[1024,1024]{1,0:T(8,128)(2,1)S(1)} %copy-done.28), kind=kLoop, calls=%fused_computation | loop fusion | flops 5242880 | bytes 10485760 | tf_op jit(solution)/shard_map/convert_element_type | solution.py:1015
  296.5 35.2 %shard_map.173 = (bf16[2048,512]{1,0:T(8,128)(2,1)S(1)}, bf16[2048,512]{1,0:T(8,128)(2,1)S(1)}, bf16[2048,512]{1,0:T(8,128)(2,1)}) custom-call(f32[4]{0:T(128)S(1)} %exponential_multiply_fusion.slopes, bf16[2048,1536]{1,0:T(8,128)(2,1)} %get-tuple-element.133.q_ref.k_ref.v_ref, bf16[2048,1536]{1,0:T(8,128)(2,1)} %get-tuple-element.133.q_ref.k_ref.v_ref, ...), custom_call_target="tpu_custom_call" | custom-call | flops 1024 | bytes 1024 | tf_op jit(solution)/shard_map/pallas_call | solution.py:462
  334.4 12.5 %shard_map.174 = (bf16[1024,1024]{1,0:T(8,128)(2,1)}, f32[1024,1024]{1,0:T(8,128)}) custom-call(s32[1]{0:T(128)} %bitcast.core, bf16[2048,512]{1,0:T(8,128)(2,1)} %copy-done.12, bf16[2048,512]{1,0:T(8,128)(2,1)} %copy-done.13, bf16[2048,512]{1,0:T(8,128)(2,1)} %get-tuple-element.141.refs_2_, bf16[8,128,2176]{2,1,0:T(8,128)(2,1)} %shard_map.161.w.refs_3_), custom_call_target="tpu_custom_call" | custom-call | flops 1024 | bytes 1024 | tf_op jit(solution)/shard_map/pallas_call | solution.py:858
  350.1 7.0 %collective-permute-done.31 = bf16[64,2048]{1,0:T(8,128)(2,1)S(1)} collective-permute-done((bf16[64,2048]{1,0:T(8,128)(2,1)S(1)}, bf16[64,2048]{1,0:T(8,128)(2,1)S(1)}, u32[]{:S(2)}, u32[]{:S(2)}) %collective-permute-start.31) | collective-permute-done | bytes 262176 | tf_op jit(solution)/shard_map/ppermute | solution.py:898
  360.9 13.3 %shard_map.175 = bf16[1024,2048]{1,0:T(8,128)(2,1)} custom-call(bf16[2048,1024]{1,0:T(8,128)(2,1)} %get-tuple-element.146.a1, bf16[1024,512]{1,0:T(8,128)(2,1)} %copy-done.21, bf16[2048,512]{1,0:T(8,128)(2,1)} %copy-done.12, bf16[2048,512]{1,0:T(8,128)(2,1)} %copy-done.13, bf16[2048,512]{1,0:T(8,128)(2,1)} %get-tuple-element.141.refs_2_), custom_call_target="tpu_custom_call" | custom-call | flops 1024 | bytes 1024 | tf_op jit(solution)/shard_map/pallas_call | solution.py:807
  380.4 4.9 %shard_map.176 = (bf16[1024,1024]{1,0:T(8,128)(2,1)S(1)}, f32[2,1024]{1,0:T(2,128)S(1)}) custom-call(bf16[1024,1024]{1,0:T(8,128)(2,1)S(1)} %copy-done.4, f32[1024,1024]{1,0:T(8,128)S(1)} %copy-done.16, bf16[1024,1024]{1,0:T(8,128)(2,1)} %collective-permute-done.33.r_2_, f32[1024,1024]{1,0:T(8,128)S(1)} %copy-done.15, f32[1,1024]{1,0:T(1,128)S(1)} %get-tuple-element.197.r_4_), custom_call_target="tpu_custom_call" | custom-call | flops 1024 | bytes 1024 | tf_op jit(solution)/shard_map/pallas_call | solution.py:722
  389.0 8.0 %collective-permute-done.36 = bf16[64,2048]{1,0:T(8,128)(2,1)S(1)} collective-permute-done((bf16[64,2048]{1,0:T(8,128)(2,1)S(1)}, bf16[64,2048]{1,0:T(8,128)(2,1)S(1)}, u32[]{:S(2)}, u32[]{:S(2)}) %collective-permute-start.36) | collective-permute-done | bytes 262176 | tf_op jit(solution)/shard_map/ppermute | solution.py:898
  400.6 3.1 broadcast_select_fusion
  403.7 8.3 %collective-permute-done.37 = bf16[128,2048]{1,0:T(8,128)(2,1)S(1)} collective-permute-done((bf16[128,2048]{1,0:T(8,128)(2,1)S(1)}, bf16[128,2048]{1,0:T(8,128)(2,1)S(1)}, u32[]{:S(2)}, u32[]{:S(2)}) %collective-permute-start.37) | collective-permute-done | bytes 524320 | tf_op jit(solution)/shard_map/ppermute | solution.py:898
  415.9 10.8 %collective-permute-done.39 = bf16[128,2048]{1,0:T(8,128)(2,1)S(1)} collective-permute-done((bf16[128,2048]{1,0:T(8,128)(2,1)S(1)}, bf16[128,2048]{1,0:T(8,128)(2,1)S(1)}, u32[]{:S(2)}, u32[]{:S(2)}) %collective-permute-start.39) | collective-permute-done | bytes 524320 | tf_op jit(solution)/shard_map/ppermute | solution.py:898
  441.1 9.1 %collective-permute-done.50 = f32[4,1024]{1,0:T(4,128)S(1)} collective-permute-done((f32[4,1024]{1,0:T(4,128)S(1)}, f32[4,1024]{1,0:T(4,128)S(1)}, u32[]{:S(2)}, u32[]{:S(2)}) %collective-permute-start.50) | collective-permute-done | bytes 16416 | tf_op jit(solution)/shard_map/ppermute | solution.py:898
  460.6 6.6 %collective-permute-done.46 = bf16[64,2048]{1,0:T(8,128)(2,1)S(1)} collective-permute-done((bf16[64,2048]{1,0:T(8,128)(2,1)S(1)}, bf16[64,2048]{1,0:T(8,128)(2,1)S(1)}, u32[]{:S(2)}, u32[]{:S(2)}) %collective-permute-start.46) | collective-permute-done | bytes 262176 | tf_op jit(solution)/shard_map/ppermute | solution.py:898
  468.0 4.3 collective-permute-done.44
  (254 shorter events, 121.1 us)
Async XLA Ops:
  8.0 209.3 %all-gather.3.cloned.1.call-start = ((), (), s32[]{:S(2)}) async-start(), calls=%async_computation.4 | async-start | bytes 8650752 | tf_op jit(solution)/shard_map/all_gather | solution.py:994
  22.4 49.9 %collective-permute-start.1 = (bf16[1024,1024]{1,0:T(8,128)(2,1)S(1)}, bf16[1024,1024]{1,0:T(8,128)(2,1)}, u32[]{:S(2)}, u32[]{:S(2)}) collective-permute-start(bf16[1024,1024]{1,0:T(8,128)(2,1)S(1)} %bitcast.80), channel_id=1, source_target_pairs={{1,2},{2,1},{5,6},{6,5},{9,10},{10,9},{13,14},{14,13},{17,18},{18,... | collective-permute-start | bytes 6291464 | tf_op jit(solution)/shard_map/ppermute | solution.py:898
  24.4 14.7 %collective-permute-start.3 = (bf16[128,2176]{1,0:T(8,128)(2,1)S(1)}, bf16[128,2176]{1,0:T(8,128)(2,1)S(1)}, u32[]{:S(2)}, u32[]{:S(2)}) collective-permute-start(bf16[128,2176]{1,0:T(8,128)(2,1)S(1)} %maximum_select_fusion.refs_0_), channel_id=1, source_target_pairs={{0,8},{1,9},{2,10},{3,11},{4,0},{5,1},{6,2},{7,3},{8,16},{9,17},{1... | collective-permute-start | bytes 1671176 | tf_op jit(solution)/shard_map/ppermute | solution.py:898
  26.3 15.2 %collective-permute-start.4 = (bf16[128,2176]{1,0:T(8,128)(2,1)S(1)}, bf16[128,2176]{1,0:T(8,128)(2,1)S(1)}, u32[]{:S(2)}, u32[]{:S(2)}) collective-permute-start(bf16[128,2176]{1,0:T(8,128)(2,1)S(1)} %maximum_select_fusion.refs_0_), channel_id=1, source_target_pairs={{0,4},{1,5},{2,6},{3,7},{4,12},{5,13},{6,14},{7,15},{8,0},{9,1},{1... | collective-permute-start | bytes 1671176 | tf_op jit(solution)/shard_map/ppermute | solution.py:898
  41.5 14.6 %collective-permute-start.5 = (bf16[128,2176]{1,0:T(8,128)(2,1)S(1)}, bf16[128,2176]{1,0:T(8,128)(2,1)S(1)}, u32[]{:S(2)}, u32[]{:S(2)}) collective-permute-start(bf16[128,2176]{1,0:T(8,128)(2,1)S(1)} %collective-permute-done.3.refs_1_), channel_id=1, source_target_pairs={{0,8},{1,9},{2,10},{3,11},{4,0},{5,1},{6,2},{7,3},{8,16},{9,17},{1... | collective-permute-start | bytes 1671176 | tf_op jit(solution)/shard_map/ppermute | solution.py:898
  43.1 14.4 %collective-permute-start.6 = (bf16[128,2176]{1,0:T(8,128)(2,1)S(1)}, bf16[128,2176]{1,0:T(8,128)(2,1)S(1)}, u32[]{:S(2)}, u32[]{:S(2)}) collective-permute-start(bf16[128,2176]{1,0:T(8,128)(2,1)S(1)} %collective-permute-done.4.refs_2_), channel_id=1, source_target_pairs={{0,4},{1,5},{2,6},{3,7},{4,12},{5,13},{6,14},{7,15},{8,0},{9,1},{1... | collective-permute-start | bytes 1671176 | tf_op jit(solution)/shard_map/ppermute | solution.py:898
  57.5 13.5 %collective-permute-start.7 = (bf16[128,2176]{1,0:T(8,128)(2,1)S(1)}, bf16[128,2176]{1,0:T(8,128)(2,1)S(1)}, u32[]{:S(2)}, u32[]{:S(2)}) collective-permute-start(bf16[128,2176]{1,0:T(8,128)(2,1)S(1)} %collective-permute-done.5.refs_3_), channel_id=1, source_target_pairs={{0,8},{1,9},{2,10},{3,11},{4,0},{5,1},{6,2},{7,3},{8,16},{9,17},{1... | collective-permute-start | bytes 1671176 | tf_op jit(solution)/shard_map/ppermute | solution.py:898
  59.5 13.5 %collective-permute-start.9 = (bf16[64,2048]{1,0:T(8,128)(2,1)S(1)}, bf16[64,2048]{1,0:T(8,128)(2,1)S(1)}, u32[]{:S(2)}, u32[]{:S(2)}) collective-permute-start(bf16[64,2048]{1,0:T(8,128)(2,1)S(1)} %convert_element_type.169), channel_id=1, source_target_pairs={{0,1},{1,0},{2,3},{3,2},{4,5},{5,4},{6,7},{7,6},{8,9},{9,8},{10,11... | collective-permute-start | bytes 786440 | tf_op jit(solution)/shard_map/ppermute | solution.py:898
  73.3 23.5 %collective-permute-start.13 = (bf16[1024,1024]{1,0:T(8,128)(2,1)S(1)}, bf16[1024,1024]{1,0:T(8,128)(2,1)}, u32[]{:S(2)}, u32[]{:S(2)}) collective-permute-start(bf16[1024,1024]{1,0:T(8,128)(2,1)S(1)} %broadcast_select_fusion.2.xa.x_ref.r_0_), channel_id=1, source_target_pairs={{0,2},{1,3},{2,0},{3,1},{4,6},{5,7},{6,4},{7,5},{8,10},{9,11},{10,... | collective-permute-start | bytes 6291464 | tf_op jit(solution)/shard_map/ppermute | solution.py:898
  84.5 27.7 %collective-permute-start.16 = (bf16[1024,1024]{1,0:T(8,128)(2,1)}, bf16[1024,1024]{1,0:T(8,128)(2,1)}, u32[]{:S(2)}, u32[]{:S(2)}) collective-permute-start(bf16[1024,1024]{1,0:T(8,128)(2,1)} %bitcast.11), channel_id=1, source_target_pairs={{1,2},{2,1},{5,6},{6,5},{9,10},{10,9},{13,14},{14,13},{17,18},{18,... | collective-permute-start | bytes 6291464 | tf_op jit(solution)/shard_map/ppermute | solution.py:898
  86.5 25.4 %collective-permute-start.17 = (s32[1,2048]{1,0:T(1,128)S(1)}, s32[1,2048]{1,0:T(1,128)S(1)}, u32[]{:S(2)}, u32[]{:S(2)}) collective-permute-start(s32[1,2048]{1,0:T(1,128)S(1)} %copy-done.45), channel_id=1, source_target_pairs={{0,2},{1,3},{2,0},{3,1},{4,6},{5,7},{6,4},{7,5},{8,10},{9,11},{10,... | collective-permute-start | bytes 24584 | tf_op jit(solution)/shard_map/ppermute | solution.py:898
  86.5 23.2 %collective-permute-start.14 = (bf16[128,2048]{1,0:T(8,128)(2,1)S(1)}, bf16[128,2048]{1,0:T(8,128)(2,1)}, u32[]{:S(2)}, u32[]{:S(2)}) collective-permute-start(bf16[128,2048]{1,0:T(8,128)(2,1)S(1)} %maximum_select_fusion.1.refs_0_), channel_id=1, source_target_pairs={{0,8},{1,9},{2,10},{3,11},{4,0},{5,1},{6,2},{7,3},{8,16},{9,17},{1... | collective-permute-start | bytes 1572872 | tf_op jit(solution)/shard_map/ppermute | solution.py:898
  87.2 22.5 %collective-permute-start.15 = (bf16[128,2048]{1,0:T(8,128)(2,1)S(1)}, bf16[128,2048]{1,0:T(8,128)(2,1)}, u32[]{:S(2)}, u32[]{:S(2)}) collective-permute-start(bf16[128,2048]{1,0:T(8,128)(2,1)S(1)} %maximum_select_fusion.1.refs_0_), channel_id=1, source_target_pairs={{0,4},{1,5},{2,6},{3,7},{4,12},{5,13},{6,14},{7,15},{8,0},{9,1},{1... | collective-permute-start | bytes 1572872 | tf_op jit(solution)/shard_map/ppermute | solution.py:898
  109.7 15.1 %collective-permute-start.18 = (bf16[128,2048]{1,0:T(8,128)(2,1)}, bf16[128,2048]{1,0:T(8,128)(2,1)}, u32[]{:S(2)}, u32[]{:S(2)}) collective-permute-start(bf16[128,2048]{1,0:T(8,128)(2,1)} %collective-permute-done.14.refs_1_), channel_id=1, source_target_pairs={{0,8},{1,9},{2,10},{3,11},{4,0},{5,1},{6,2},{7,3},{8,16},{9,17},{1... | collective-permute-start | bytes 1572872 | tf_op jit(solution)/shard_map/ppermute | solution.py:898
  110.4 14.4 %collective-permute-start.19 = (bf16[128,2048]{1,0:T(8,128)(2,1)}, bf16[128,2048]{1,0:T(8,128)(2,1)}, u32[]{:S(2)}, u32[]{:S(2)}) collective-permute-start(bf16[128,2048]{1,0:T(8,128)(2,1)} %collective-permute-done.15.refs_2_), channel_id=1, source_target_pairs={{0,4},{1,5},{2,6},{3,7},{4,12},{5,13},{6,14},{7,15},{8,0},{9,1},{1... | collective-permute-start | bytes 1572872 | tf_op jit(solution)/shard_map/ppermute | solution.py:898
  124.8 209.6 %reduce-scatter.3.cloned.1.call-start = ((), (), s32[]{:S(2)}) async-start(), calls=%async_computation.2 | async-start | bytes 4718592 | tf_op jit(solution)/shard_map/reduce_scatter | solution.py:963
  124.9 17.0 %collective-permute-start.20 = (bf16[128,2048]{1,0:T(8,128)(2,1)}, bf16[128,2048]{1,0:T(8,128)(2,1)S(1)}, u32[]{:S(2)}, u32[]{:S(2)}) collective-permute-start(bf16[128,2048]{1,0:T(8,128)(2,1)} %collective-permute-done.18.refs_3_), channel_id=1, source_target_pairs={{0,8},{1,9},{2,10},{3,11},{4,0},{5,1},{6,2},{7,3},{8,16},{9,17},{1... | collective-permute-start | bytes 1572872 | tf_op jit(solution)/shard_map/ppermute | solution.py:898
  125.6 18.6 %collective-permute-start.21 = (bf16[128,2048]{1,0:T(8,128)(2,1)}, bf16[128,2048]{1,0:T(8,128)(2,1)S(1)}, u32[]{:S(2)}, u32[]{:S(2)}) collective-permute-start(bf16[128,2048]{1,0:T(8,128)(2,1)} %collective-permute-done.19.refs_4_), channel_id=1, source_target_pairs={{0,4},{1,5},{2,6},{3,7},{4,12},{5,13},{6,14},{7,15},{8,0},{9,1},{1... | collective-permute-start | bytes 1572872 | tf_op jit(solution)/shard_map/ppermute | solution.py:898
  148.9 26.8 %collective-permute-start.24 = (bf16[1024,1024]{1,0:T(8,128)(2,1)}, bf16[1024,1024]{1,0:T(8,128)(2,1)}, u32[]{:S(2)}, u32[]{:S(2)}) collective-permute-start(bf16[1024,1024]{1,0:T(8,128)(2,1)} %shard_map.167), channel_id=1, source_target_pairs={{0,2},{1,3},{2,0},{3,1},{4,6},{5,7},{6,4},{7,5},{8,10},{9,11},{10,... | collective-permute-start | bytes 6291464 | tf_op jit(solution)/shard_map/ppermute | solution.py:898
  148.9 17.5 %collective-permute-start.22 = (bf16[64,2048]{1,0:T(8,128)(2,1)S(1)}, bf16[64,2048]{1,0:T(8,128)(2,1)S(1)}, u32[]{:S(2)}, u32[]{:S(2)}) collective-permute-start(bf16[64,2048]{1,0:T(8,128)(2,1)S(1)} %slice.140), channel_id=1, source_target_pairs={{0,4},{1,5},{2,6},{3,7},{4,12},{5,13},{6,14},{7,15},{8,0},{9,1},{1... | collective-permute-start | bytes 786440 | tf_op jit(solution)/shard_map/ppermute | solution.py:898
  148.9 17.5 %collective-permute-start.23 = (bf16[64,2048]{1,0:T(8,128)(2,1)S(1)}, bf16[64,2048]{1,0:T(8,128)(2,1)}, u32[]{:S(2)}, u32[]{:S(2)}) collective-permute-start(bf16[64,2048]{1,0:T(8,128)(2,1)S(1)} %slice.139), channel_id=1, source_target_pairs={{0,8},{1,9},{2,10},{3,11},{4,0},{5,1},{6,2},{7,3},{8,16},{9,17},{1... | collective-permute-start | bytes 786440 | tf_op jit(solution)/shard_map/ppermute | solution.py:898
  150.9 32.5 %collective-permute-start.26 = (bf16[1024,1024]{1,0:T(8,128)(2,1)S(1)}, bf16[1024,1024]{1,0:T(8,128)(2,1)}, u32[]{:S(2)}, u32[]{:S(2)}) collective-permute-start(bf16[1024,1024]{1,0:T(8,128)(2,1)S(1)} %broadcast_select_fusion.1.ya.skip), channel_id=1, source_target_pairs={{0,2},{1,3},{2,0},{3,1},{4,6},{5,7},{6,4},{7,5},{8,10},{9,11},{10,... | collective-permute-start | bytes 6291464 | tf_op jit(solution)/shard_map/ppermute | solution.py:898
  216.9 221.0 %reduce-scatter.5.cloned.1.call-start = ((), (), s32[]{:S(2)}) async-start(), calls=%async_computation.3 | async-start | bytes 4718592 | tf_op jit(solution)/shard_map/reduce_scatter | solution.py:963
  350.1 28.1 %collective-permute-start.33 = (bf16[1024,1024]{1,0:T(8,128)(2,1)}, bf16[1024,1024]{1,0:T(8,128)(2,1)}, u32[]{:S(2)}, u32[]{:S(2)}) collective-permute-start(bf16[1024,1024]{1,0:T(8,128)(2,1)} %get-tuple-element.152), channel_id=1, source_target_pairs={{0,2},{1,3},{2,0},{3,1},{4,6},{5,7},{6,4},{7,5},{8,10},{9,11},{10,... | collective-permute-start | bytes 6291464 | tf_op jit(solution)/shard_map/ppermute | solution.py:898
  358.1 42.5 %collective-permute-start.32 = (bf16[1024,1024]{1,0:T(8,128)(2,1)}, bf16[1024,1024]{1,0:T(8,128)(2,1)}, u32[]{:S(2)}, u32[]{:S(2)}) collective-permute-start(bf16[1024,1024]{1,0:T(8,128)(2,1)} %add_convert_fusion), channel_id=1, source_target_pairs={{1,2},{2,1},{5,6},{6,5},{9,10},{10,9},{13,14},{14,13},{17,18},{18,... | collective-permute-start | bytes 6291464 | tf_op jit(solution)/shard_map/ppermute | solution.py:898
  376.8 20.2 %collective-permute-start.36 = (bf16[64,2048]{1,0:T(8,128)(2,1)S(1)}, bf16[64,2048]{1,0:T(8,128)(2,1)S(1)}, u32[]{:S(2)}, u32[]{:S(2)}) collective-permute-start(bf16[64,2048]{1,0:T(8,128)(2,1)S(1)} %get-tuple-element.150), channel_id=1, source_target_pairs={{0,4},{1,5},{2,6},{3,7},{4,12},{5,13},{6,14},{7,15},{8,0},{9,1},{1... | collective-permute-start | bytes 786440 | tf_op jit(solution)/shard_map/ppermute | solution.py:898
  385.3 41.5 %collective-permute-start.34 = (bf16[1024,1024]{1,0:T(8,128)(2,1)S(1)}, bf16[1024,1024]{1,0:T(8,128)(2,1)S(1)}, u32[]{:S(2)}, u32[]{:S(2)}) collective-permute-start(bf16[1024,1024]{1,0:T(8,128)(2,1)S(1)} %get-tuple-element.154), channel_id=1, source_target_pairs={{1,2},{2,1},{5,6},{6,5},{9,10},{10,9},{13,14},{14,13},{17,18},{18,... | collective-permute-start | bytes 6291464 | tf_op jit(solution)/shard_map/ppermute | solution.py:898
  398.5 13.5 %collective-permute-start.37 = (bf16[128,2048]{1,0:T(8,128)(2,1)S(1)}, bf16[128,2048]{1,0:T(8,128)(2,1)S(1)}, u32[]{:S(2)}, u32[]{:S(2)}) collective-permute-start(bf16[128,2048]{1,0:T(8,128)(2,1)S(1)} %get-tuple-element.187), channel_id=1, source_target_pairs={{0,8},{1,9},{2,10},{3,11},{4,0},{5,1},{6,2},{7,3},{8,16},{9,17},{1... | collective-permute-start | bytes 1572872 | tf_op jit(solution)/shard_map/ppermute | solution.py:898
  398.8 13.3 %collective-permute-start.38 = (bf16[128,2048]{1,0:T(8,128)(2,1)S(1)}, bf16[128,2048]{1,0:T(8,128)(2,1)S(1)}, u32[]{:S(2)}, u32[]{:S(2)}) collective-permute-start(bf16[128,2048]{1,0:T(8,128)(2,1)S(1)} %get-tuple-element.186), channel_id=1, source_target_pairs={{0,4},{1,5},{2,6},{3,7},{4,12},{5,13},{6,14},{7,15},{8,0},{9,1},{1... | collective-permute-start | bytes 1572872 | tf_op jit(solution)/shard_map/ppermute | solution.py:898
  435.9 19.6 %collective-permute-start.41 = (bf16[128,2048]{1,0:T(8,128)(2,1)S(1)}, bf16[128,2048]{1,0:T(8,128)(2,1)}, u32[]{:S(2)}, u32[]{:S(2)}) collective-permute-start(bf16[128,2048]{1,0:T(8,128)(2,1)S(1)} %get-tuple-element.182), channel_id=1, source_target_pairs={{0,8},{1,9},{2,10},{3,11},{4,0},{5,1},{6,2},{7,3},{8,16},{9,17},{1... | collective-permute-start | bytes 1572872 | tf_op jit(solution)/shard_map/ppermute | solution.py:898
  437.6 17.9 %collective-permute-start.42 = (bf16[128,2048]{1,0:T(8,128)(2,1)S(1)}, bf16[128,2048]{1,0:T(8,128)(2,1)}, u32[]{:S(2)}, u32[]{:S(2)}) collective-permute-start(bf16[128,2048]{1,0:T(8,128)(2,1)S(1)} %get-tuple-element.183), channel_id=1, source_target_pairs={{0,4},{1,5},{2,6},{3,7},{4,12},{5,13},{6,14},{7,15},{8,0},{9,1},{1... | collective-permute-start | bytes 1572872 | tf_op jit(solution)/shard_map/ppermute | solution.py:898
  441.0 16.8 %collective-permute-start.45 = (bf16[64,2048]{1,0:T(8,128)(2,1)S(1)}, bf16[64,2048]{1,0:T(8,128)(2,1)S(1)}, u32[]{:S(2)}, u32[]{:S(2)}) collective-permute-start(bf16[64,2048]{1,0:T(8,128)(2,1)S(1)} %select_convert_fusion), channel_id=1, source_target_pairs={{0,2},{1,3},{2,0},{3,1},{4,6},{5,7},{6,4},{7,5},{8,10},{9,11},{10,... | collective-permute-start | bytes 786440 | tf_op jit(solution)/shard_map/ppermute | solution.py:898
  (69 other events, 773.3 us)
Sparse Core Ops, SparseCore 0:
  125.0 79.4 all-gather.2
Sparse Core Ops, SparseCore 1:
  217.0 86.8 reduce-scatter.2
  307.8 93.1 reduce-scatter.4
